TPU v7x, 32 devices: a whole 2x2x4 slice. The times are simulated.
32 devices in a mesh: dp: 8 (over y, x, core), mp: 4 (over z).
Axes of the slice: x: 2, y: 2, z: 4, core: 2. Of those that a mesh axis runs over, the one named last changes fastest.
Arguments:
- tokens: bfloat16 [18944, 1024], P(('dp', 'mp')), may hold values from -6 to 6
- cotangent: bfloat16 [18944, 1024], P(('dp', 'mp')), may hold values from -6 to 6
- timesteps: int32 [8], P('dp'), may hold values from 0 to 999
- item_lengths: int32 [8, 18], P('dp'), may hold values from 0 to 512, as said below
- w_qkv: bfloat16 [1024, 3, 1024], P(None, None, 'mp'), may hold values from -0.1875 to 0.1875
- bias_qv: bfloat16 [2, 1024], P(None, 'mp'), may hold values from -1.796875 to 1.796875
- w_out: bfloat16 [1024, 1024], P('mp'), may hold values from -1 to 1
- w_up: bfloat16 [1024, 4096], P(None, 'mp'), may hold values from -0.1875 to 0.1875
- bias_up: bfloat16 [4096], P('mp'), may hold values from -1.796875 to 1.796875
- w_down: bfloat16 [4096, 1024], P('mp'), may hold values from -0.09375 to 0.09375
- vectors: float32 [8, 1024], replicated
Outputs:
- output: bfloat16 [18944, 1024], P(('dp', 'mp'))
- input_grad: bfloat16 [18944, 1024], P(('dp', 'mp'))
- grad_qkv: float32 [1024, 3, 1024], P('dp', None, 'mp')
- grad_bias_qv: float32 [2, 1024], P(None, 'mp')
- grad_out: float32 [1024, 1024], P('mp', 'dp')
- grad_up: float32 [1024, 4096], P('dp', 'mp')
- grad_bias_up: float32 [4096], P('mp')
- grad_down: float32 [4096, 1024], P('mp', 'dp')
- grad_vectors: float32 [8, 1024], replicated
Inputs may be any that keep to these rules, and one draw needn't show every extreme that they name: `item_lengths`: each row lists items of 128 or 512 tokens, then zeros; the items of a row fill 18 * 128 tokens and at least one has 512.
All inputs are finite; a program needn't handle non-finite values.
Results may differ from a plain program's by a relative error of at most 0.02.
The roundings to bfloat16 on the way count: a program that leaves them out, or rounds other values in their place, can miss the bound.
Values may be sent and summed in bfloat16 or wider, within the bound.
A program may use at most 256 MiB of HBM per device.

v0:
```python
import jax
import jax.numpy as jnp
from jax import lax
from jax.sharding import PartitionSpec as P

D = 1024
HD = 64
FF = 4096
LEN = 2368


def norm_forward(value, gain, shift):
    average = jnp.mean(value, axis=-1, keepdims=True)
    centred = value - average
    inverse = lax.rsqrt(jnp.mean(centred * centred, axis=-1, keepdims=True) + 1e-05)
    normed = centred * inverse
    return (normed * gain + shift, normed, inverse)


def norm_backward(grad, normed, inverse, gain):
    scaled = grad * gain
    result = inverse * (
        scaled
        - jnp.mean(scaled, axis=-1, keepdims=True)
        - normed * jnp.mean(scaled * normed, axis=-1, keepdims=True)
    )
    return (result, jnp.sum(grad * normed, axis=0), jnp.sum(grad, axis=0))


def gelu_exact(value):
    return jax.nn.gelu(value, approximate=False)


def attend_forward(queries, keys, values, segments):
    scale = HD ** (-0.5)
    block_rows = LEN // 4

    def one_block(inputs):
        query_block, segment_block = inputs
        scores = (
            jnp.einsum("bhe,khe->hbk", query_block, keys, preferred_element_type=jnp.float32)
            * scale
        )
        allowed = segment_block[:, None] == segments[None, :]
        scores = jnp.where(allowed[None], scores, -1e30)
        highest = jnp.max(scores, axis=-1, keepdims=True)
        weights = jnp.exp(scores - highest)
        totals = jnp.sum(weights, axis=-1, keepdims=True)
        chances_low = (weights / totals).astype(jnp.bfloat16)
        result = jnp.einsum("hbk,khe->bhe", chances_low, values, preferred_element_type=jnp.float32)
        return (result.astype(jnp.bfloat16), (highest + jnp.log(totals))[..., 0])

    blocks = queries.reshape(4, block_rows, queries.shape[1], queries.shape[2])
    results, logsums = lax.map(one_block, (blocks, segments.reshape(4, block_rows)))
    return (results.reshape(queries.shape), logsums)


def attend_backward(queries, keys, values, out_grads, logsums, segments):
    scale = HD ** (-0.5)
    block_rows = LEN // 4

    def one_block(carry, inputs):
        key_grads, value_grads = carry
        query_block, grad_block, logsum_block, segment_block = inputs
        scores = (
            jnp.einsum("bhe,khe->hbk", query_block, keys, preferred_element_type=jnp.float32)
            * scale
        )
        allowed = segment_block[:, None] == segments[None, :]
        scores = jnp.where(allowed[None], scores, -1e30)
        chances = jnp.exp(scores - logsum_block[..., None])
        chances_low = chances.astype(jnp.bfloat16)
        value_grads = value_grads + jnp.einsum(
            "hbk,bhe->khe", chances_low, grad_block, preferred_element_type=jnp.float32
        )
        flow = jnp.einsum("bhe,khe->hbk", grad_block, values, preferred_element_type=jnp.float32)
        inner = jnp.sum(chances * flow, axis=-1, keepdims=True)
        score_grads = (chances * (flow - inner)).astype(jnp.bfloat16)
        query_grads = (
            jnp.einsum("hbk,khe->bhe", score_grads, keys, preferred_element_type=jnp.float32)
            * scale
        )
        key_grads = (
            key_grads
            + jnp.einsum(
                "hbk,bhe->khe", score_grads, query_block, preferred_element_type=jnp.float32
            )
            * scale
        )
        return ((key_grads, value_grads), query_grads)

    shape_blocks = (4, block_rows, queries.shape[1], queries.shape[2])
    zeros = jnp.zeros(keys.shape, jnp.float32)
    (key_grads, value_grads), query_grads = lax.scan(
        one_block,
        (zeros, zeros),
        (
            queries.reshape(shape_blocks),
            out_grads.reshape(shape_blocks),
            logsums,
            segments.reshape(4, block_rows),
        ),
    )
    return (query_grads.reshape(queries.shape), key_grads, value_grads)


def body(
    tokens,
    cotangent,
    timesteps,
    item_lengths,
    w_qkv,
    bias_qv,
    w_out,
    w_up,
    bias_up,
    w_down,
    vectors,
):
    rows = tokens.shape[0]
    total = rows * lax.axis_size("mp")
    seq_count = timesteps.shape[0]
    local_width = w_qkv.shape[2]
    local_hidden = w_up.shape[1]
    local_heads = local_width // HD
    my_index = lax.axis_index("mp")
    row_ids = my_index * rows + lax.iota(jnp.int32, rows)
    row_owner = row_ids // LEN
    step_times = timesteps.astype(jnp.float32) * 0.001
    time_rows = jnp.sum(
        jnp.where(
            row_owner[:, None] == lax.iota(jnp.int32, seq_count)[None, :], step_times[None, :], 0.0
        ),
        axis=1,
    )
    ends = jnp.cumsum(item_lengths, axis=1)
    segments = jnp.sum(
        (lax.iota(jnp.int32, LEN)[None, :, None] >= ends[:, None, :]).astype(jnp.int32), axis=2
    )
    lifted = tokens.astype(jnp.float32) + time_rows[:, None] * vectors[0] + vectors[1]
    gathered = lax.all_gather(lifted.astype(jnp.bfloat16), "mp", axis=0, tiled=True)
    projected = jnp.einsum("td,dce->cte", gathered, w_qkv, preferred_element_type=jnp.float32)
    shaped = (seq_count, LEN, local_heads, HD)
    head_query = (projected[0] + bias_qv[0]).astype(jnp.bfloat16).reshape(shaped)
    head_key = projected[1].astype(jnp.bfloat16).reshape(shaped)
    head_value = (projected[2] + bias_qv[1]).astype(jnp.bfloat16).reshape(shaped)
    attended, logsums = lax.map(
        lambda items: attend_forward(*items), (head_query, head_key, head_value, segments)
    )
    attended = attended.reshape(total, local_width)
    piece = attended
    mixed = (
        lax.psum_scatter(
            jnp.dot(piece, w_out, preferred_element_type=jnp.float32),
            "mp",
            scatter_dimension=0,
            tiled=True,
        )
        + vectors[2]
    )
    first, normed_one, inverse_one = norm_forward(lifted + mixed, vectors[4], vectors[5])
    hidden_all = lax.all_gather(first.astype(jnp.bfloat16), "mp", axis=0, tiled=True)
    upper = jnp.dot(hidden_all, w_up, preferred_element_type=jnp.float32) + bias_up
    activated, gelu_pull = jax.vjp(gelu_exact, upper)
    activated = activated.astype(jnp.bfloat16)
    piece = activated
    down = (
        lax.psum_scatter(
            jnp.dot(piece, w_down, preferred_element_type=jnp.float32).astype(jnp.bfloat16),
            "mp",
            scatter_dimension=0,
            tiled=True,
        ).astype(jnp.float32)
        + vectors[3]
    )
    output, normed_two, inverse_two = norm_forward(first + down, vectors[6], vectors[7])
    out_grads = cotangent.astype(jnp.float32)
    second_grads, gain_two, shift_two = norm_backward(
        out_grads, normed_two, inverse_two, vectors[6]
    )
    down_all = lax.all_gather(second_grads.astype(jnp.bfloat16), "mp", axis=0, tiled=True)
    grad_down = jnp.einsum("tf,td->fd", activated, down_all, preferred_element_type=jnp.float32)
    act_grads = jnp.einsum("td,fd->tf", down_all, w_down, preferred_element_type=jnp.float32)
    (upper_grads,) = gelu_pull(act_grads)
    upper_low = upper_grads.astype(jnp.bfloat16)
    grad_bias_up = jnp.sum(upper_low, axis=0, dtype=jnp.float32)
    grad_up = jnp.einsum("td,tf->df", hidden_all, upper_low, preferred_element_type=jnp.float32)
    piece = upper_low
    first_part = lax.psum_scatter(
        jnp.einsum("tf,df->td", piece, w_up, preferred_element_type=jnp.float32).astype(
            jnp.bfloat16
        ),
        "mp",
        scatter_dimension=0,
        tiled=True,
    ).astype(jnp.float32)
    first_grads = second_grads + first_part
    mixed_grads, gain_one, shift_one = norm_backward(
        first_grads, normed_one, inverse_one, vectors[4]
    )
    mixed_all = lax.all_gather(mixed_grads.astype(jnp.bfloat16), "mp", axis=0, tiled=True)
    grad_out = jnp.einsum("te,td->ed", attended, mixed_all, preferred_element_type=jnp.float32)
    attended_grads = jnp.einsum(
        "td,ed->te", mixed_all, w_out, preferred_element_type=jnp.float32
    ).astype(jnp.bfloat16)
    query_grads, key_grads, value_grads = lax.map(
        lambda items: attend_backward(*items),
        (head_query, head_key, head_value, attended_grads.reshape(shaped), logsums, segments),
    )
    qkv_low = jnp.stack(
        [
            query_grads.reshape(total, local_width),
            key_grads.reshape(total, local_width),
            value_grads.reshape(total, local_width),
        ],
        axis=1,
    ).astype(jnp.bfloat16)
    grad_bias_qv = jnp.sum(qkv_low[:, 0::2], axis=0, dtype=jnp.float32)
    grad_qkv = jnp.einsum("td,tcf->dcf", gathered, qkv_low, preferred_element_type=jnp.float32)
    piece = qkv_low
    input_part = lax.psum_scatter(
        jnp.einsum("tcf,dcf->td", piece, w_qkv, preferred_element_type=jnp.float32).astype(
            jnp.bfloat16
        ),
        "mp",
        scatter_dimension=0,
        tiled=True,
    ).astype(jnp.float32)
    input_sum = mixed_grads + input_part
    vector_terms = jnp.stack(
        [
            jnp.sum(time_rows[:, None] * input_sum, axis=0),
            jnp.sum(input_sum, axis=0),
            jnp.sum(mixed_grads, axis=0),
            jnp.sum(second_grads, axis=0),
            gain_one,
            shift_one,
            gain_two,
            shift_two,
        ],
        axis=0,
    )
    zero_index = jnp.zeros((), jnp.int32)
    qv_start = my_index * local_width
    up_start = my_index * local_hidden
    qv_placed = lax.dynamic_update_slice(
        jnp.zeros((2, D), jnp.float32), grad_bias_qv, (zero_index, qv_start)
    )
    up_placed = lax.dynamic_update_slice(jnp.zeros((FF,), jnp.float32), grad_bias_up, (up_start,))
    grad_qkv, grad_out, grad_up, grad_down = (
        lax.psum_scatter(
            grad_qkv.astype(jnp.bfloat16), "dp", scatter_dimension=0, tiled=True
        ).astype(jnp.float32),
        lax.psum_scatter(
            grad_out.astype(jnp.bfloat16), "dp", scatter_dimension=1, tiled=True
        ).astype(jnp.float32),
        lax.psum_scatter(
            grad_up.astype(jnp.bfloat16), "dp", scatter_dimension=0, tiled=True
        ).astype(jnp.float32),
        lax.psum_scatter(
            grad_down.astype(jnp.bfloat16), "dp", scatter_dimension=1, tiled=True
        ).astype(jnp.float32),
    )
    grad_vectors, qv_summed, up_summed = lax.psum(
        (vector_terms, qv_placed, up_placed), ("dp", "mp")
    )
    grad_bias_qv = lax.dynamic_slice_in_dim(qv_summed, qv_start, local_width, 1)
    grad_bias_up = lax.dynamic_slice_in_dim(up_summed, up_start, local_hidden, 0)
    return (
        output.astype(jnp.bfloat16),
        input_sum.astype(jnp.bfloat16),
        grad_qkv,
        grad_bias_qv,
        grad_out,
        grad_up,
        grad_bias_up,
        grad_down,
        grad_vectors,
    )


def solution(mesh):
    in_specs = (
        P(("dp", "mp"), None),
        P(("dp", "mp"), None),
        P("dp"),
        P("dp", None),
        P(None, None, "mp"),
        P(None, "mp"),
        P("mp", None),
        P(None, "mp"),
        P("mp"),
        P("mp", None),
        P(),
    )
    out_specs = (
        P(("dp", "mp"), None),
        P(("dp", "mp"), None),
        P("dp", None, "mp"),
        P(None, "mp"),
        P("mp", "dp"),
        P("dp", "mp"),
        P("mp"),
        P("mp", "dp"),
        P(),
    )
    return jax.shard_map(body, mesh=mesh, in_specs=in_specs, out_specs=out_specs, check_vma=False)
```

profile of v0, /device:TPU:0, one launch (start us, length us, event | category | flops | bytes accessed | tf_op | source)
XLA Modules:
  0.0 1561.9 jit_solution(12083884697471805062)
XLA Ops:
  13.9 93.6 %all-gather.5.cloned.1.call-done = bf16[2368,1024]{1,0:T(8,128)(2,1)} async-done(((bf16[592,1024]{1,0:T(8,128)(2,1)}), bf16[2368,1024]{1,0:T(8,128)(2,1)}) %all-gather.5.cloned.1.call-update) | async-done | bytes 4849680 | tf_op jit(solution)/shard_map/all_gather | solution.py:141
  134.8 146.9 %while.47 = (s32[]{:T(128)}, bf16[4,592,4,64]{1,3,2,0:T(8,128)(2,1)}, f32[4,4,592]{2,1,0:T(4,128)}, s32[4,592]{1,0:T(4,128)S(1)}, s32[2368]{0:T(1024)S(1)}, /*in...) while((s32[]{:T(128)}, ...), condition=%wide.region_5.6_spmd, body=%wide.region_2.5_spmd.sunk | while | flops 1504340736 | bytes 81525840 | solution.py:54
  135.9 11.4 fusion.126
  147.3 11.5 fusion.127
  158.8 12.3 fusion.128
  172.6 11.4 fusion.126
  184.0 11.5 fusion.127
  195.5 12.3 fusion.128
  209.3 11.4 fusion.126
  220.6 11.5 fusion.127
  232.2 12.3 fusion.128
  245.9 11.4 fusion.126
  257.3 11.5 fusion.127
  268.8 12.3 fusion.128
  296.3 163.6 %reduce-scatter.13.cloned.1.call-done = f32[592,1024]{1,0:T(8,128)} async-done(((f32[2368,1024]{1,0:T(8,128)}), f32[592,1024]{1,0:T(8,128)}) %reduce-scatter.13.cloned.1.call-update) | async-done | bytes 2424848 | tf_op jit(solution)/shard_map/reduce_scatter | solution.py:153
  465.4 92.6 %all-gather.7.cloned.1.call-done = bf16[2368,1024]{1,0:T(8,128)(2,1)} async-done(((bf16[592,1024]{1,0:T(8,128)(2,1)}), bf16[2368,1024]{1,0:T(8,128)(2,1)}) %all-gather.7.cloned.1.call-update) | async-done | bytes 4849680 | tf_op jit(solution)/shard_map/all_gather | solution.py:162
  558.0 29.3 %multiply_convert_fusion.1 = (bf16[2368,1024]{1,0:T(8,128)(2,1)S(1)}, f32[2368,1024]{1,0:T(8,128)}, f32[2368,1024]{1,0:T(8,128)}) fusion(f32[1024]{0:T(1024)S(1)} %convert_element_type.139, bf16[2368,1024]{1,0:T(8,128)(2,1)} %all-gather.7.cloned.1.call-done, bf16[1024,1024]{1,0:T(8,128)(2,1)S(1)} %copy-done), kind=kOutput, calls=%fused_computation.56 | convolution fusion | flops 5126094848 | bytes 31199232 | tf_op jit(solution)/shard_map/dot_general | solution.py:163
  596.3 85.9 %reduce-scatter.15.cloned.1.call-done = bf16[592,1024]{1,0:T(8,128)(2,1)} async-done(((bf16[2368,1024]{1,0:T(8,128)(2,1)}), bf16[592,1024]{1,0:T(8,128)(2,1)}) %reduce-scatter.15.cloned.1.call-update) | async-done | bytes 1212432 | tf_op jit(solution)/shard_map/reduce_scatter | solution.py:168
  691.2 92.0 %all-gather.9.cloned.1.call-done = bf16[2368,1024]{1,0:T(8,128)(2,1)} async-done(((bf16[592,1024]{1,0:T(8,128)(2,1)}), bf16[2368,1024]{1,0:T(8,128)(2,1)}) %all-gather.9.cloned.1.call-update) | async-done | bytes 4849680 | tf_op jit(solution)/shard_map/all_gather | solution.py:181
  783.2 15.8 %convert_reduce_fusion = (f32[1024]{0:T(1024)}, bf16[2368,1024]{1,0:T(8,128)(2,1)S(1)}) fusion(f32[2368,1024]{1,0:T(8,128)} %get-tuple-element.343, f32[2368,1024]{1,0:T(8,128)} %get-tuple-element.362, f32[1024]{0:T(1024)S(1)} %convert_element_type.139, bf16[2368,1024]{1,0:T(8,128)(2,1)} %all-gather.9.cloned.1.call-done, bf16[1024,1024]{1,0:T(8,128)(2,1)} %param.24), kind=kOutput, calls=%fused_computation.54 | convolution fusion | flops 5007277056 | bytes 31203328 | tf_op jit(solution)/shard_map/td,fd->tf/dot_general | solution.py:183
  808.5 85.9 %reduce-scatter.17.cloned.1.call-done = bf16[592,1024]{1,0:T(8,128)(2,1)} async-done(((bf16[2368,1024]{1,0:T(8,128)(2,1)}), bf16[592,1024]{1,0:T(8,128)(2,1)}) %reduce-scatter.17.cloned.1.call-update) | async-done | bytes 1212432 | tf_op jit(solution)/shard_map/reduce_scatter | solution.py:189
  901.9 9.0 convolution_convert_fusion.3
  913.6 10.0 convolution_convert_fusion.4
  923.7 70.4 %all-gather.11.cloned.1.call-done = bf16[2368,1024]{1,0:T(8,128)(2,1)} async-done(((bf16[592,1024]{1,0:T(8,128)(2,1)}), bf16[2368,1024]{1,0:T(8,128)(2,1)}) %all-gather.11.cloned.1.call-update) | async-done | bytes 4849680 | tf_op jit(solution)/shard_map/all_gather | solution.py:201
  1004.4 319.9 %while.48 = (s32[]{:T(128)}, f32[2368,4,64]{0,2,1:T(8,128)}, f32[2368,4,64]{0,2,1:T(8,128)}, bf16[4,592,4,64]{1,3,2,0:T(8,128)(2,1)}, bf16[4,592,4,64]{1,3,2,0:T...) while((s32[]{:T(128)}, f32[2368,4,64]{0,2,1:T(8,128)}, ...), condition=%wide.region_19.20_spmd.clone, body=%wide.region_17.19_spmd.clone.sunk | while | flops 3677444864 | bytes 219960528 | solution.py:94
  1007.1 10.8 fusion.138
  1017.9 12.4 fusion.140
  1030.3 17.4 %multiply_reduce_fusion.8 = (f32[4,592]{1,0:T(4,128)S(1)}, f32[4,592,2368]{2,1,0:T(8,128)}) fusion(f32[4,592,2368]{2,1,0:T(8,128)} %fusion.138, f32[4,592]{1,0:T(4,128)S(1)} %dynamic-slice_bitcast_fusion.2, pred[592,2368]{1,0:T(8,128)(4,1)S(1)} %broadcast_compare_fusion.5, bf16[2368,4,64]{0,2,1:T(8,128)(2,1)} %get-tuple-element.552, ...), kind=kOutput, calls=%fused_computation.19.clone.1 | convolution fusion | flops 745785024 | bytes 48459268 | tf_op jit(solution)/shard_map/while/body/eval_jaxpr/while/body/eval_jaxpr/bhe,khe->hbk/dot_general | solution.py:76
  1047.7 21.7 %multiply_convert_fusion.3 = bf16[4,592,2368]{2,1,0:T(8,128)(2,1)} fusion(f32[4,592,2368]{2,1,0:T(8,128)} %get-tuple-element.487, f32[4,592,2368]{2,1,0:T(8,128)} %fusion.138, f32[4,592]{1,0:T(4,128)S(1)} %get-tuple-element.488, f32[4,592]{1,0:T(4,128)S(1)} %dynamic-slice_bitcast_fusion.2, pred[592,2368]{1,0:T(8,128)(4,1)S(1)} %broadcast_compare_fusion.5), kind=kLoop, calls=%fused_computation.18.clone.1 | loop fusion | flops 33644544 | bytes 57495040 | tf_op jit(solution)/shard_map/while/body/eval_jaxpr/while/body/eval_jaxpr/convert_element_type | solution.py:78
  1069.4 7.9 fusion.141
  1088.3 10.4 fusion.138
  1098.7 12.7 fusion.140
  1111.4 17.2 %multiply_reduce_fusion.8 = (f32[4,592]{1,0:T(4,128)S(1)}, f32[4,592,2368]{2,1,0:T(8,128)}) fusion(f32[4,592,2368]{2,1,0:T(8,128)} %fusion.138, f32[4,592]{1,0:T(4,128)S(1)} %dynamic-slice_bitcast_fusion.2, pred[592,2368]{1,0:T(8,128)(4,1)S(1)} %broadcast_compare_fusion.5, bf16[2368,4,64]{0,2,1:T(8,128)(2,1)} %get-tuple-element.552, ...), kind=kOutput, calls=%fused_computation.19.clone.1 | convolution fusion | flops 745785024 | bytes 48459268 | tf_op jit(solution)/shard_map/while/body/eval_jaxpr/while/body/eval_jaxpr/bhe,khe->hbk/dot_general | solution.py:76
  1128.7 20.2 %multiply_convert_fusion.3 = bf16[4,592,2368]{2,1,0:T(8,128)(2,1)} fusion(f32[4,592,2368]{2,1,0:T(8,128)} %get-tuple-element.487, f32[4,592,2368]{2,1,0:T(8,128)} %fusion.138, f32[4,592]{1,0:T(4,128)S(1)} %get-tuple-element.488, f32[4,592]{1,0:T(4,128)S(1)} %dynamic-slice_bitcast_fusion.2, pred[592,2368]{1,0:T(8,128)(4,1)S(1)} %broadcast_compare_fusion.5), kind=kLoop, calls=%fused_computation.18.clone.1 | loop fusion | flops 33644544 | bytes 57495040 | tf_op jit(solution)/shard_map/while/body/eval_jaxpr/while/body/eval_jaxpr/convert_element_type | solution.py:78
  1167.7 10.4 fusion.138
  1178.1 12.7 fusion.140
  1190.8 17.2 %multiply_reduce_fusion.8 = (f32[4,592]{1,0:T(4,128)S(1)}, f32[4,592,2368]{2,1,0:T(8,128)}) fusion(f32[4,592,2368]{2,1,0:T(8,128)} %fusion.138, f32[4,592]{1,0:T(4,128)S(1)} %dynamic-slice_bitcast_fusion.2, pred[592,2368]{1,0:T(8,128)(4,1)S(1)} %broadcast_compare_fusion.5, bf16[2368,4,64]{0,2,1:T(8,128)(2,1)} %get-tuple-element.552, ...), kind=kOutput, calls=%fused_computation.19.clone.1 | convolution fusion | flops 745785024 | bytes 48459268 | tf_op jit(solution)/shard_map/while/body/eval_jaxpr/while/body/eval_jaxpr/bhe,khe->hbk/dot_general | solution.py:76
  1208.0 20.2 %multiply_convert_fusion.3 = bf16[4,592,2368]{2,1,0:T(8,128)(2,1)} fusion(f32[4,592,2368]{2,1,0:T(8,128)} %get-tuple-element.487, f32[4,592,2368]{2,1,0:T(8,128)} %fusion.138, f32[4,592]{1,0:T(4,128)S(1)} %get-tuple-element.488, f32[4,592]{1,0:T(4,128)S(1)} %dynamic-slice_bitcast_fusion.2, pred[592,2368]{1,0:T(8,128)(4,1)S(1)} %broadcast_compare_fusion.5), kind=kLoop, calls=%fused_computation.18.clone.1 | loop fusion | flops 33644544 | bytes 57495040 | tf_op jit(solution)/shard_map/while/body/eval_jaxpr/while/body/eval_jaxpr/convert_element_type | solution.py:78
  1247.1 10.4 fusion.138
  1257.5 12.7 fusion.140
  1270.2 17.2 %multiply_reduce_fusion.8 = (f32[4,592]{1,0:T(4,128)S(1)}, f32[4,592,2368]{2,1,0:T(8,128)}) fusion(f32[4,592,2368]{2,1,0:T(8,128)} %fusion.138, f32[4,592]{1,0:T(4,128)S(1)} %dynamic-slice_bitcast_fusion.2, pred[592,2368]{1,0:T(8,128)(4,1)S(1)} %broadcast_compare_fusion.5, bf16[2368,4,64]{0,2,1:T(8,128)(2,1)} %get-tuple-element.552, ...), kind=kOutput, calls=%fused_computation.19.clone.1 | convolution fusion | flops 745785024 | bytes 48459268 | tf_op jit(solution)/shard_map/while/body/eval_jaxpr/while/body/eval_jaxpr/bhe,khe->hbk/dot_general | solution.py:76
  1287.4 20.2 %multiply_convert_fusion.3 = bf16[4,592,2368]{2,1,0:T(8,128)(2,1)} fusion(f32[4,592,2368]{2,1,0:T(8,128)} %get-tuple-element.487, f32[4,592,2368]{2,1,0:T(8,128)} %fusion.138, f32[4,592]{1,0:T(4,128)S(1)} %get-tuple-element.488, f32[4,592]{1,0:T(4,128)S(1)} %dynamic-slice_bitcast_fusion.2, pred[592,2368]{1,0:T(8,128)(4,1)S(1)} %broadcast_compare_fusion.5), kind=kLoop, calls=%fused_computation.18.clone.1 | loop fusion | flops 33644544 | bytes 57495040 | tf_op jit(solution)/shard_map/while/body/eval_jaxpr/while/body/eval_jaxpr/convert_element_type | solution.py:78
  1342.9 8.7 fusion.60
  1351.6 8.0 bitcast_convert_fusion
  1366.4 9.5 reduce-scatter.25.cloned.1.call-done
  1377.5 40.5 %reduce-scatter.21.cloned.1.call-done = bf16[128,3,256]{2,0,1:T(8,128)(2,1)} async-done(((bf16[1024,3,256]{2,0,1:T(8,128)(2,1)}), bf16[128,3,256]{2,0,1:T(8,128)(2,1)}) %reduce-scatter.21.cloned.1.call-update) | async-done | bytes 196624 | tf_op jit(solution)/shard_map/reduce_scatter | solution.py:251
  1419.8 88.0 %reduce-scatter.19.cloned.1.call-done = bf16[592,1024]{1,0:T(8,128)(2,1)} async-done(((bf16[2368,1024]{1,0:T(8,128)(2,1)}), bf16[592,1024]{1,0:T(8,128)(2,1)}) %reduce-scatter.19.cloned.1.call-update) | async-done | bytes 1212432 | tf_op jit(solution)/shard_map/reduce_scatter | solution.py:221
  1511.5 42.1 %all-reduce = (f32[2,1024]{1,0:T(2,128)S(1)}, f32[4096]{0:T(1024)S(1)}, f32[8,1024]{1,0:T(8,128)}) all-reduce(f32[2,1024]{1,0:T(2,128)S(1)} %constant_dynamic-update-slice_fusion, f32[4096]{0:T(1024)S(1)} %dynamic_update_slice.32, f32[8,1024]{1,0:T(8,128)S(1)} %stack.40), channel_id=1, replica_groups=mesh['dp'=8,'mp'=4] {'dp','mp'}, use_global_device_ids=true, to_apply=%region_23.24 | all-reduce | flops 14336 | bytes 114688 | tf_op jit(solution)/shard_map/psum | solution.py:264
  (255 shorter events, 207.8 us)
Async XLA Ops:
  7.2 550.8 %copy-start = (bf16[1024,1024]{1,0:T(8,128)(2,1)S(1)}, bf16[1024,1024]{1,0:T(8,128)(2,1)}, u32[]{:S(2)}) copy-start(bf16[1024,1024]{1,0:T(8,128)(2,1)} %param.22) | copy-start | bytes 6291460
  7.2 100.3 %all-gather.5.cloned.1.call-start = ((), (), s32[]{:S(2)}) async-start(), calls=%async_computation.8 | async-start | bytes 6062080 | tf_op jit(solution)/shard_map/all_gather | solution.py:141
  9.7 104.1 %copy-start.28 = (f32[1,1024]{1,0:T(1,128)}, f32[1,1024]{1,0:T(1,128)S(1)}, u32[]{:S(2)}) copy-start(f32[1,1024]{1,0:T(1,128)S(1)} %get-tuple-element.359) | copy-start | bytes 12292
  9.7 104.1 %copy-start.30 = (f32[1,1024]{1,0:T(1,128)}, f32[1,1024]{1,0:T(1,128)S(1)}, u32[]{:S(2)}) copy-start(f32[1,1024]{1,0:T(1,128)S(1)} %get-tuple-element.360) | copy-start | bytes 12292
  13.1 446.8 %reduce-scatter.13.cloned.1.call-start = ((), (), s32[]{:S(2)}) async-start(), calls=%async_computation.9 | async-start | bytes 12124160 | tf_op jit(solution)/shard_map/reduce_scatter | solution.py:153
  147.3 11.5 copy-start.4
  184.0 11.5 copy-start.4
  220.6 11.5 copy-start.4
  257.3 11.5 copy-start.4
  281.7 7.4 copy-start.2
  281.8 7.4 copy-start.15
  281.8 7.4 copy-start.21
  295.8 164.1 %copy-start.12 = (bf16[592,1024]{1,0:T(8,128)(2,1)S(1)}, bf16[592,1024]{1,0:T(8,128)(2,1)}, u32[]{:S(2)}) copy-start(bf16[592,1024]{1,0:T(8,128)(2,1)} %param.15) | copy-start | bytes 3637252
  295.8 164.1 %copy-start.24 = (f32[592]{0:T(1024)S(1)}, f32[592]{0:T(1024)}, u32[]{:S(2)}) copy-start(f32[592]{0:T(1024)} %copy-done.23) | copy-start | bytes 7108
  295.8 164.1 %copy-start.29 = (f32[1,1024]{1,0:T(1,128)S(1)}, f32[1,1024]{1,0:T(1,128)}, u32[]{:S(2)}) copy-start(f32[1,1024]{1,0:T(1,128)} %copy-done.28) | copy-start | bytes 12292
  295.8 164.1 %copy-start.31 = (f32[1,1024]{1,0:T(1,128)S(1)}, f32[1,1024]{1,0:T(1,128)}, u32[]{:S(2)}) copy-start(f32[1,1024]{1,0:T(1,128)} %copy-done.30) | copy-start | bytes 12292
  295.8 164.1 %copy-start.39 = (f32[1,1024]{1,0:T(1,128)S(1)}, f32[1,1024]{1,0:T(1,128)}, u32[]{:S(2)}) copy-start(f32[1,1024]{1,0:T(1,128)} %get-tuple-element.358) | copy-start | bytes 12292
  295.8 262.1 %all-gather.7.cloned.1.call-start = ((), (), s32[]{:S(2)}) async-start(), calls=%async_computation.10 | async-start | bytes 6062080 | tf_op jit(solution)/shard_map/all_gather | solution.py:162
  465.3 216.9 %reduce-scatter.15.cloned.1.call-start = ((), (), s32[]{:S(2)}) async-start(), calls=%async_computation.11 | async-start | bytes 6062080 | tf_op jit(solution)/shard_map/reduce_scatter | solution.py:168
  558.0 31.5 %copy-start.43 = (bf16[1024,1024]{1,0:T(8,128)(2,1)S(1)}, bf16[1024,1024]{1,0:T(8,128)(2,1)}, u32[]{:S(2)}) copy-start(bf16[1024,1024]{1,0:T(8,128)(2,1)} %param.24) | copy-start | bytes 6291460
  596.2 86.0 %copy-start.36 = (f32[1,1024]{1,0:T(1,128)S(1)}, f32[1,1024]{1,0:T(1,128)}, u32[]{:S(2)}) copy-start(f32[1,1024]{1,0:T(1,128)} %get-tuple-element.355) | copy-start | bytes 12292
  596.2 187.0 %all-gather.9.cloned.1.call-start = ((), (), s32[]{:S(2)}) async-start(), calls=%async_computation.12 | async-start | bytes 6062080 | tf_op jit(solution)/shard_map/all_gather | solution.py:181
  691.0 203.4 %reduce-scatter.17.cloned.1.call-start = ((), (), s32[]{:S(2)}) async-start(), calls=%async_computation.13 | async-start | bytes 6062080 | tf_op jit(solution)/shard_map/reduce_scatter | solution.py:189
  808.4 185.7 %all-gather.11.cloned.1.call-start = ((), (), s32[]{:S(2)}) async-start(), calls=%async_computation.14 | async-start | bytes 6062080 | tf_op jit(solution)/shard_map/all_gather | solution.py:201
  901.9 458.9 %reduce-scatter.27.cloned.1.call-start = ((), (), s32[]{:S(2)}) async-start(), calls=%async_computation.19 | async-start | bytes 2359296
  913.5 449.2 %reduce-scatter.23.cloned.1.call-start = ((), (), s32[]{:S(2)}) async-start(), calls=%async_computation.17 | async-start | bytes 2359296 | tf_op jit(solution)/shard_map/reduce_scatter | solution.py:257
  913.6 80.5 %copy-start.20 = (bf16[256,1024]{1,0:T(8,128)(2,1)S(1)}, bf16[256,1024]{1,0:T(8,128)(2,1)}, u32[]{:S(2)}) copy-start(bf16[256,1024]{1,0:T(8,128)(2,1)} %param.21) | copy-start | bytes 1572868
  923.7 452.2 %reduce-scatter.25.cloned.1.call-start = ((), (), s32[]{:S(2)}) async-start(), calls=%async_computation.18 | async-start | bytes 589824
  1047.7 21.7 %copy-start.17 = (bf16[4,592,4,64]{1,3,2,0:T(8,128)(2,1)S(1)}, bf16[4,592,4,64]{1,3,2,0:T(8,128)(2,1)}, u32[]{:S(2)}) copy-start(bf16[4,592,4,64]{1,3,2,0:T(8,128)(2,1)} %get-tuple-element.532) | copy-start | bytes 3637252 | tf_op jit(solution)/shard_map/while/body/eval_jaxpr/while
  1069.4 7.9 copy-start.5
  1077.3 7.2 copy-start.18
  1128.7 20.2 %copy-start.17 = (bf16[4,592,4,64]{1,3,2,0:T(8,128)(2,1)S(1)}, bf16[4,592,4,64]{1,3,2,0:T(8,128)(2,1)}, u32[]{:S(2)}) copy-start(bf16[4,592,4,64]{1,3,2,0:T(8,128)(2,1)} %get-tuple-element.532) | copy-start | bytes 3637252 | tf_op jit(solution)/shard_map/while/body/eval_jaxpr/while
  1148.9 7.9 copy-start.5
  1208.0 20.2 %copy-start.17 = (bf16[4,592,4,64]{1,3,2,0:T(8,128)(2,1)S(1)}, bf16[4,592,4,64]{1,3,2,0:T(8,128)(2,1)}, u32[]{:S(2)}) copy-start(bf16[4,592,4,64]{1,3,2,0:T(8,128)(2,1)} %get-tuple-element.532) | copy-start | bytes 3637252 | tf_op jit(solution)/shard_map/while/body/eval_jaxpr/while
  1228.3 7.9 copy-start.5
  1287.4 20.2 %copy-start.17 = (bf16[4,592,4,64]{1,3,2,0:T(8,128)(2,1)S(1)}, bf16[4,592,4,64]{1,3,2,0:T(8,128)(2,1)}, u32[]{:S(2)}) copy-start(bf16[4,592,4,64]{1,3,2,0:T(8,128)(2,1)} %get-tuple-element.532) | copy-start | bytes 3637252 | tf_op jit(solution)/shard_map/while/body/eval_jaxpr/while
  1307.7 7.9 copy-start.5
  1315.6 7.1 copy-start.18
  1342.8 8.8 copy-start.11
  1342.8 75.2 %reduce-scatter.21.cloned.1.call-start = ((), (), s32[]{:S(2)}) async-start(), calls=%async_computation.16 | async-start | bytes 1769472 | tf_op jit(solution)/shard_map/reduce_scatter | solution.py:251
  1351.6 156.2 %reduce-scatter.19.cloned.1.call-start = ((), (), s32[]{:S(2)}) async-start(), calls=%async_computation.15 | async-start | bytes 6062080 | tf_op jit(solution)/shard_map/reduce_scatter | solution.py:221
  1366.0 141.7 %copy-start.25 = (f32[592]{0:T(1024)S(1)}, f32[592]{0:T(1024)}, u32[]{:S(2)}) copy-start(f32[592]{0:T(1024)} %copy-done.23) | copy-start | bytes 7108
  1419.8 91.7 %copy-start.33 = (f32[1024]{0:T(1024)S(1)}, f32[1024]{0:T(1024)}, u32[]{:S(2)}) copy-start(f32[1024]{0:T(1024)} %get-tuple-element.279) | copy-start | bytes 12292
  1419.8 91.7 %copy-start.34 = (f32[1024]{0:T(1024)S(1)}, f32[1024]{0:T(1024)}, u32[]{:S(2)}) copy-start(f32[1024]{0:T(1024)} %get-tuple-element.284) | copy-start | bytes 12292
  1419.8 91.7 %copy-start.35 = (f32[1024]{0:T(1024)S(1)}, f32[1024]{0:T(1024)}, u32[]{:S(2)}) copy-start(f32[1024]{0:T(1024)} %get-tuple-element.287) | copy-start | bytes 12292
  1419.8 91.7 %copy-start.37 = (f32[1024]{0:T(1024)S(1)}, f32[1024]{0:T(1024)}, u32[]{:S(2)}) copy-start(f32[1024]{0:T(1024)} %get-tuple-element.281) | copy-start | bytes 12292
  1419.8 91.7 %copy-start.38 = (f32[1024]{0:T(1024)S(1)}, f32[1024]{0:T(1024)}, u32[]{:S(2)}) copy-start(f32[1024]{0:T(1024)} %get-tuple-element.290) | copy-start | bytes 12292
  1507.7 47.1 %copy-start.1 = (bf16[1024,1024]{1,0:T(8,128)(2,1)S(1)}, bf16[1024,1024]{1,0:T(8,128)(2,1)}, u32[]{:S(2)}) copy-start(bf16[1024,1024]{1,0:T(8,128)(2,1)} %param.22) | copy-start | bytes 6291460
  (26 other events, 89.7 us)
Sparse Core Ops, SparseCore 0:
  13.2 94.2 all-gather.4
  296.0 163.8 reduce-scatter.12
  465.4 92.4 all-gather.6
  596.3 85.8 reduce-scatter.14
  691.1 92.0 all-gather.8
  808.6 85.8 reduce-scatter.16
  902.0 92.0 all-gather.10
  997.4 39.6 reduce-scatter.26
  1040.7 41.2 reduce-scatter.22
  1342.9 32.9 reduce-scatter.24
  1379.5 38.4 reduce-scatter.20
  1420.3 87.3 reduce-scatter.18
where the time goes:
time: 1570 us; the launch traced here: 1560 us
  waiting for transfers between devices  822 us (52%)
  matrix products  432 us (28%)
  other arithmetic  178 us (11%)
  local copies, waits for them, and re-layouts  69.2 us (4%)
  blocking collectives  42.1 us (3%)
    reduce_scatter x1, waiting for transfers between devices, body(): lax.psum_scatter(jnp.dot(piece, w_out, preferred_element_type=jnp.float32...  164 us
    all_gather x1, waiting for transfers between devices, body(): lax.all_gather(lifted.astype(jnp.bfloat16), 'mp', axis=0, tiled=True)  93.6 us
    all_gather x1, waiting for transfers between devices, body(): lax.all_gather(first.astype(jnp.bfloat16), 'mp', axis=0, tiled=True)  92.6 us
    all_gather x1, waiting for transfers between devices, body(): lax.all_gather(second_grads.astype(jnp.bfloat16), 'mp', axis=0, tiled=True)  92 us
    reduce_scatter x1, waiting for transfers between devices, body(): lax.psum_scatter(jnp.einsum('tcf,dcf->td', piece, w_qkv, preferred_elemen...  88 us
    dot_general x8, matrix products, one_block(): jnp.einsum('bhe,khe->hbk', query_block, keys, preferred_element_type=jnp....  87.6 us
    reduce_scatter x1, waiting for transfers between devices, body(): lax.psum_scatter(jnp.einsum('tf,df->td', piece, w_up, preferred_element_t...  85.9 us
    reduce_scatter x1, waiting for transfers between devices, body(): lax.psum_scatter(jnp.dot(piece, w_down, preferred_element_type=jnp.float3...  85.9 us
  transfers between devices with their start and end apart: 12, of which 10 were waited for; matrix products, arithmetic and copies ran while one was open for 25% of the time, Pallas kernels for 0%

commit v1 on v0

--- a/solution.py
+++ b/solution.py
@@ -1,6 +1,10 @@
+import functools
+
 import jax
 import jax.numpy as jnp
 from jax import lax
+from jax.experimental import pallas as pl
+from jax.experimental.pallas import tpu as pltpu
 from jax.sharding import PartitionSpec as P
 
 D = 1024
@@ -279,6 +283,536 @@
     )
 
 
+UNIT = 128
+LONG = 4
+MESH = pl.DeviceIdType.MESH
+
+
+def fits_local(mesh):
+    parts = mesh.shape["mp"]
+    return mesh.shape["dp"] == 8 and parts == 4 and LEN % (16 * parts) == 0
+
+
+def window_plan(rows, parts):
+    firsts = [(rows * j) // UNIT - (LONG - 1) for j in range(parts)]
+    offsets = [rows * j - UNIT * first for j, first in enumerate(firsts)]
+    ends = [
+        ((rows * (j + 1) - 1) // UNIT + LONG - firsts[j]) * UNIT for j in range(parts)
+    ]
+    return firsts, offsets, ends
+
+
+def pick(table, index):
+    value = jnp.int32(table[0])
+    for j in range(1, len(table)):
+        value = jnp.where(index == j, jnp.int32(table[j]), value)
+    return value
+
+
+def gather_kernel(
+    rows, window, parts, tokens, w_qkv, w_out, w_up, w_down, win, f_qkv, f_out, f_up, f_down, send, recv, near, far, own
+):
+    d = lax.axis_index("dp")
+    z = lax.axis_index("mp")
+    firsts, offsets, ends = window_plan(rows, parts)
+    shards = (w_qkv, w_out, w_up, w_down)
+    fulls = (f_qkv, f_out, f_up, f_down)
+    sizes = (128, 32, 128, 128)
+    others = (1, 3, 2)
+    peers = [(d, z ^ k) for k in others] + [(d ^ 1, z), (d ^ 2, z), (d ^ 4, z)]
+    barrier = pltpu.get_barrier_semaphore()
+    for peer in peers:
+        pl.semaphore_signal(barrier, inc=1, device_id=peer, device_id_type=MESH)
+    pl.semaphore_wait(barrier, len(peers))
+
+    def part(ref, index, owner, size, half=None):
+        start = owner * size
+        count = size
+        if half is not None:
+            count = size // 2
+            start = start + half * count
+        rows_at = pl.ds(pl.multiple_of(start, 16), count)
+        if len(ref.shape) == 4:
+            return ref.at[index, :, rows_at, :]
+        return ref.at[index, rows_at, :]
+
+    chunks = [(g, k) for g in range(4) for k in others]
+    copies = {}
+
+    def remote(i, kind, src, dst, target):
+        copy = pltpu.make_async_remote_copy(
+            src, dst, send.at[i, kind], recv.at[i, kind], device_id=target, device_id_type=MESH
+        )
+        copy.start()
+        copies[i, kind] = copy
+
+    def first_hop(i):
+        g, k = chunks[i]
+        size = sizes[g]
+        rows_at = pl.ds(pl.multiple_of(d * size, 16), size)
+        src = shards[g].at[:, rows_at, :] if g == 0 else shards[g].at[rows_at, :]
+        remote(i, 0, src, part(fulls[g], z, d, size), (d, z ^ k))
+
+    def place(i, owner, half=None):
+        g, k = chunks[i]
+        return part(fulls[g], z ^ k, owner, sizes[g], half)
+
+    for i in range(3):
+        first_hop(i)
+    left_send = [
+        pltpu.make_async_remote_copy(
+            tokens.at[pl.ds(0, ends[j] - offsets[j] - rows), :],
+            win.at[pl.ds(offsets[j] + rows, ends[j] - offsets[j] - rows), :],
+            near.at[0], near.at[1], device_id=(d, j), device_id_type=MESH,
+        )
+        for j in range(parts - 1)
+    ]
+    right_send = [
+        pltpu.make_async_remote_copy(
+            tokens.at[pl.ds(rows - offsets[j], offsets[j]), :],
+            win.at[pl.ds(0, offsets[j]), :],
+            far.at[0], far.at[1], device_id=(d, j), device_id_type=MESH,
+        )
+        for j in range(1, parts)
+    ]
+    for j in range(parts - 1):
+        @pl.when(z == j + 1)
+        def _(j=j):
+            left_send[j].start()
+    for j in range(1, parts):
+        @pl.when(z == j - 1)
+        def _(j=j):
+            right_send[j - 1].start()
+    locals_ = []
+    for g in range(4):
+        copy = pltpu.make_async_copy(shards[g], fulls[g].at[z], own.at[g])
+        copy.start()
+        locals_.append(copy)
+    offset = pl.multiple_of(pick(offsets, z), 16)
+    copy = pltpu.make_async_copy(tokens, win.at[pl.ds(offset, rows), :], own.at[4])
+    copy.start()
+    locals_.append(copy)
+    fill_first = pltpu.make_async_copy(
+        tokens.at[pl.ds(0, offsets[0]), :], win.at[pl.ds(0, offsets[0]), :], own.at[5]
+    )
+    fills = []
+    for j in range(parts):
+        begin = ends[j] if j < parts - 1 else offsets[j] + rows
+        if begin < window:
+            fills.append(
+                (j, pltpu.make_async_copy(
+                    tokens.at[pl.ds(0, window - begin), :], win.at[pl.ds(begin, window - begin), :], own.at[6]
+                ))
+            )
+
+    @pl.when(z == 0)
+    def _():
+        fill_first.start()
+
+    for j, fill in fills:
+        @pl.when(z == j)
+        def _(fill=fill):
+            fill.start()
+
+    for i in range(3, len(chunks)):
+        first_hop(i)
+
+    def stage_one(i):
+        copies[i, 0].wait_recv()
+        remote(i, 1, place(i, d), place(i, d), (d ^ 2, z))
+        remote(i, 2, place(i, d), place(i, d), (d ^ 4, z))
+        remote(i, 5, place(i, d), place(i, d), (d ^ 1, z))
+
+    def stage_two(i):
+        copies[i, 1].wait_recv()
+        remote(i, 3, place(i, d ^ 2, 0), place(i, d ^ 2, 0), (d ^ 4, z))
+        remote(i, 6, place(i, d ^ 2), place(i, d ^ 2), (d ^ 1, z))
+        copies[i, 2].wait_recv()
+        remote(i, 4, place(i, d ^ 4, 1), place(i, d ^ 4, 1), (d ^ 2, z))
+        remote(i, 7, place(i, d ^ 4), place(i, d ^ 4), (d ^ 1, z))
+
+    def stage_three(i):
+        copies[i, 3].wait_recv()
+        remote(i, 8, place(i, d ^ 6, 0), place(i, d ^ 6, 0), (d ^ 1, z))
+        copies[i, 4].wait_recv()
+        remote(i, 9, place(i, d ^ 6, 1), place(i, d ^ 6, 1), (d ^ 1, z))
+
+    n = len(chunks)
+    for i in range(n + 2):
+        if i < n:
+            stage_one(i)
+        if 0 <= i - 1 < n:
+            stage_two(i - 1)
+        if 0 <= i - 2 < n:
+            stage_three(i - 2)
+    for i in range(n):
+        for kind in range(5, 10):
+            copies[i, kind].wait_recv()
+        for kind in range(10):
+            copies[i, kind].wait_send()
+    for j in range(parts - 1):
+        @pl.when(z == j + 1)
+        def _(j=j):
+            left_send[j].wait_send()
+
+        @pl.when(z == j)
+        def _(j=j):
+            left_send[j].wait_recv()
+    for j in range(1, parts):
+        @pl.when(z == j - 1)
+        def _(j=j):
+            right_send[j - 1].wait_send()
+
+        @pl.when(z == j)
+        def _(j=j):
+            right_send[j - 1].wait_recv()
+    for copy in locals_:
+        copy.wait()
+
+    @pl.when(z == 0)
+    def _():
+        fill_first.wait()
+
+    for j, fill in fills:
+        @pl.when(z == j)
+        def _(fill=fill):
+            fill.wait()
+
+
+def gather(tokens, w_qkv, w_out, w_up, w_down, window, parts):
+    rows = tokens.shape[0]
+    any_ = pl.BlockSpec(memory_space=pl.ANY)
+    low = jnp.bfloat16
+    return pl.pallas_call(
+        functools.partial(gather_kernel, rows, window, parts),
+        out_shape=[
+            jax.ShapeDtypeStruct((window, D), low),
+            jax.ShapeDtypeStruct((parts,) + w_qkv.shape, low),
+            jax.ShapeDtypeStruct((parts,) + w_out.shape, low),
+            jax.ShapeDtypeStruct((parts,) + w_up.shape, low),
+            jax.ShapeDtypeStruct((parts,) + w_down.shape, low),
+        ],
+        in_specs=[any_] * 5,
+        out_specs=[any_] * 5,
+        scratch_shapes=[
+            pltpu.SemaphoreType.DMA((12, 10)),
+            pltpu.SemaphoreType.DMA((12, 10)),
+            pltpu.SemaphoreType.DMA((2,)),
+            pltpu.SemaphoreType.DMA((2,)),
+            pltpu.SemaphoreType.DMA((7,)),
+        ],
+        compiler_params=pltpu.CompilerParams(collective_id=0, has_side_effects=True),
+    )(tokens, w_qkv, w_out, w_up, w_down)
+
+
+NT = (((1,), (1,)), ((), ()))
+TN = (((0,), (0,)), ((), ()))
+FIRST_OWN, LAST_OWN = LONG - 1, LONG + 4
+
+
+def two_heads(block):
+    lane = lax.broadcasted_iota(jnp.int32, block.shape, 1)
+    zero = jnp.zeros_like(block)
+    return jnp.concatenate(
+        [jnp.where(lane < HD, block, zero), jnp.where(lane < HD, zero, block)], axis=0
+    )
+
+
+def from_two(flipped):
+    both = jnp.concatenate([flipped[:HD, :UNIT], flipped[HD:, UNIT:]], axis=0)
+    return both.T
+
+
+def weights_of(keys, pair, valid):
+    scores = lax.dot_general(keys, pair, NT, preferred_element_type=jnp.float32) * HD ** (-0.5)
+    if valid is not None:
+        scores = jnp.where(valid, scores, -1e30)
+    highest = jnp.max(scores, axis=0, keepdims=True)
+    weights = jnp.exp(scores - highest)
+    return weights * (1.0 / jnp.sum(weights, axis=0, keepdims=True))
+
+
+def attend_kernel(kind, start, unit_seg, seg, q, k, v, o):
+    def unit(u, carry):
+        mine = pl.ds(pl.multiple_of(u * UNIT, UNIT), UNIT)
+
+        def run(at, valid):
+            pair = two_heads(q[mine, :])
+            chances = weights_of(k[at, :], pair, valid).astype(jnp.bfloat16)
+            flipped = lax.dot_general(v[at, :], chances, TN, preferred_element_type=jnp.float32)
+            o[mine, :] = from_two(flipped).astype(o.dtype)
+
+        @pl.when(kind[u] == 2)
+        def _():
+            run(pl.ds(pl.multiple_of(start[u], UNIT), LONG * UNIT), None)
+
+        @pl.when(kind[u] == 1)
+        def _():
+            run(mine, seg[mine, :] == unit_seg[u])
+
+        return carry
+
+    lax.fori_loop(FIRST_OWN, LAST_OWN + 1, unit, 0)
+
+
+def attend_back_kernel(kind, start, unit_seg, seg, q, k, v, g, dq, dk, dv, k_sum, v_sum):
+    k_sum[...] = jnp.zeros_like(k_sum)
+    v_sum[...] = jnp.zeros_like(v_sum)
+    scale = HD ** (-0.5)
+
+    def unit(u, carry):
+        mine = pl.ds(pl.multiple_of(u * UNIT, UNIT), UNIT)
+
+        def run(at, valid):
+            pair = two_heads(q[mine, :])
+            grads = two_heads(g[mine, :])
+            keys = k[at, :]
+            chances = weights_of(keys, pair, valid)
+            flow = lax.dot_general(v[at, :], grads, NT, preferred_element_type=jnp.float32)
+            inner = jnp.sum(chances * flow, axis=0, keepdims=True)
+            low = (chances * (flow - inner)).astype(jnp.bfloat16)
+            v_sum[at, :] += jnp.dot(chances.astype(jnp.bfloat16), grads, preferred_element_type=jnp.float32)
+            k_sum[at, :] += jnp.dot(low, pair, preferred_element_type=jnp.float32)
+
+            @pl.when((u >= FIRST_OWN) & (u <= LAST_OWN))
+            def _():
+                flipped = lax.dot_general(keys, low, TN, preferred_element_type=jnp.float32)
+                dq[mine, :] = (from_two(flipped) * scale).astype(dq.dtype)
+
+        @pl.when(kind[u] == 2)
+        def _():
+            run(pl.ds(pl.multiple_of(start[u], UNIT), LONG * UNIT), None)
+
+        @pl.when(kind[u] == 1)
+        def _():
+            run(mine, seg[mine, :] == unit_seg[u])
+
+        return carry
+
+    lax.fori_loop(0, q.shape[0] // UNIT, unit, 0)
+    dk[...] = (k_sum[...] * scale).astype(dk.dtype)
+    dv[...] = v_sum[...].astype(dv.dtype)
+
+
+def attention_call(kernel, window, plan, segs, arrays, outs, scratch):
+    column = pl.BlockSpec((window, 2 * HD), lambda p, *_: (0, p))
+    whole = pl.BlockSpec((window, 1), lambda p, *_: (0, 0))
+    return pl.pallas_call(
+        kernel,
+        grid_spec=pltpu.PrefetchScalarGridSpec(
+            num_scalar_prefetch=3,
+            grid=(D // (2 * HD),),
+            in_specs=[whole] + [column] * len(arrays),
+            out_specs=[column] * outs,
+            scratch_shapes=[pltpu.VMEM((window, 2 * HD), jnp.float32)] * scratch,
+        ),
+        out_shape=[jax.ShapeDtypeStruct((window, D), jnp.bfloat16)] * outs,
+        compiler_params=pltpu.CompilerParams(vmem_limit_bytes=48 * 2**20),
+    )(*plan, segs[:, None], *arrays)
+
+
+def unit_plan(segs, z, offsets, rows, window):
+    units = window // UNIT
+    unit_seg = segs[::UNIT]
+    same = unit_seg[:, None] == unit_seg[None, :]
+    counts = jnp.sum(same.astype(jnp.int32), axis=1)
+    inside = unit_seg < 1000
+    inside = inside & (unit_seg >= 0)
+    index = lax.iota(jnp.int32, units)
+    first = jnp.sum((unit_seg[None, :] < unit_seg[:, None]).astype(jnp.int32), axis=1)
+    own = (index >= FIRST_OWN) & (index <= LAST_OWN)
+    meets = jnp.any(same & own[None, :], axis=1)
+    long = inside & (counts == LONG) & meets
+    kind = jnp.where(long, 2, jnp.where(own, 1, 0))
+    return (
+        kind.astype(jnp.int32),
+        jnp.where(long, first * UNIT, 0).astype(jnp.int32),
+        unit_seg,
+    )
+
+
+def swap(array, axis, bit):
+    size = lax.axis_size(axis)
+    return lax.ppermute(array, axis, [(i, i ^ bit) for i in range(size)])
+
+
+def choose(array, index, axis):
+    return lax.dynamic_index_in_dim(array, index, axis, keepdims=False)
+
+
+def add_low(kept, received):
+    return (kept.astype(jnp.float32) + received.astype(jnp.float32)).astype(jnp.bfloat16)
+
+
+def scatter_sum(make, x_first):
+    d = lax.axis_index("dp")
+    z = lax.axis_index("mp")
+    core, x, y = d % 2, (d // 2) % 2, d // 4
+    low = jnp.bfloat16
+    away = swap(make(1 - core).astype(low), "dp", 1)
+    terms = add_low(make(core), away)
+    order = [(1, x, 2), (0, y, 4)] if x_first else [(0, y, 4), (1, x, 2)]
+    for step, (axis, mine, bit) in enumerate(order):
+        axis = axis if step == 0 else 0
+        away = swap(choose(terms, 1 - mine, axis), "dp", bit)
+        terms = add_low(choose(terms, mine, axis), away)
+    total = choose(terms, z, 0).astype(jnp.float32)
+    for k in (1, 2, 3):
+        total = total + swap(choose(terms, z ^ k, 0), "mp", k).astype(jnp.float32)
+    return total
+
+
+def sum_all(value):
+    for axis, bit in (("dp", 1), ("dp", 2), ("dp", 4), ("mp", 1), ("mp", 2)):
+        value = value + swap(value, axis, bit)
+    return value
+
+
+def local_body(
+    tokens,
+    cotangent,
+    timesteps,
+    item_lengths,
+    w_qkv,
+    bias_qv,
+    w_out,
+    w_up,
+    bias_up,
+    w_down,
+    vectors,
+):
+    rows = tokens.shape[0]
+    parts = lax.axis_size("mp")
+    z = lax.axis_index("mp")
+    low = jnp.bfloat16
+    f32 = jnp.float32
+    firsts, offsets, ends = window_plan(rows, parts)
+    window = -(-max(ends) // UNIT) * UNIT
+    win, f_qkv, f_out, f_up, f_down = gather(
+        tokens, jnp.transpose(w_qkv, (1, 0, 2)), w_out, w_up, w_down, window, parts
+    )
+    bias_qv_all = lax.all_gather(bias_qv, "mp", axis=1, tiled=True).astype(f32)
+    bias_up_all = lax.all_gather(bias_up, "mp", axis=0, tiled=True).astype(f32)
+    offset = pick(offsets, z)
+    first_token = UNIT * pick(firsts, z)
+    positions = first_token + lax.iota(jnp.int32, window)
+    lengths_end = jnp.cumsum(item_lengths[0])
+    segs = jnp.sum((positions[:, None] >= lengths_end[None, :]).astype(jnp.int32), axis=1)
+    segs = jnp.where(positions < 0, -1, jnp.where(positions >= LEN, 1000, segs))
+    plan = unit_plan(segs, z, offsets, rows, window)
+    step_time = timesteps[0].astype(f32) * 0.001
+
+    lifted = tokens.astype(f32) + step_time * vectors[0] + vectors[1]
+    lifted_low = lifted.astype(low)
+    win_low = (win.astype(f32) + step_time * vectors[0] + vectors[1]).astype(low)
+    w3 = jnp.transpose(f_qkv, (1, 2, 0, 3)).reshape(3, D, D)
+    queries = (jnp.dot(win_low, w3[0], preferred_element_type=f32) + bias_qv_all[0]).astype(low)
+    keys = jnp.dot(win_low, w3[1], preferred_element_type=f32).astype(low)
+    values = (jnp.dot(win_low, w3[2], preferred_element_type=f32) + bias_qv_all[1]).astype(low)
+    attended = attention_call(attend_kernel, window, plan, segs, (queries, keys, values), 1, 0)[0]
+    attended = lax.dynamic_slice_in_dim(attended, offset, rows, 0)
+    wo = f_out.reshape(D, D)
+    mixed = jnp.dot(attended, wo, preferred_element_type=f32) + vectors[2]
+    first, normed_one, inverse_one = norm_forward(lifted + mixed, vectors[4], vectors[5])
+    first_low = first.astype(low)
+    wu = jnp.transpose(f_up, (1, 0, 2)).reshape(D, FF)
+    upper = jnp.dot(first_low, wu, preferred_element_type=f32) + bias_up_all
+    activated, gelu_pull = jax.vjp(gelu_exact, upper)
+    activated = activated.astype(low)
+    wd = f_down.reshape(FF, D)
+    down = jnp.dot(activated, wd, preferred_element_type=f32) + vectors[3]
+    output, normed_two, inverse_two = norm_forward(first + down, vectors[6], vectors[7])
+    out_grads = cotangent.astype(f32)
+    second_grads, gain_two, shift_two = norm_backward(out_grads, normed_two, inverse_two, vectors[6])
+    second_low = second_grads.astype(low)
+
+    cut = D // lax.axis_size("dp")
+    fold = (rows, 2, 2, 2, cut)
+
+    def for_core(value, c):
+        return choose(value.reshape(fold), c, 3)
+
+    act4 = activated.reshape(rows, parts, FF // parts)
+    grad_down = scatter_sum(
+        lambda c: jnp.einsum("tzf,tyxk->yxzfk", act4, for_core(second_low, c), preferred_element_type=f32), True
+    )
+    act_grads = jnp.dot(second_low, wd.T, preferred_element_type=f32)
+    (upper_grads,) = gelu_pull(act_grads)
+    upper_low = upper_grads.astype(low)
+    grad_bias_up = jnp.sum(upper_low, axis=0, dtype=f32)
+    upper4 = upper_low.reshape(rows, parts, FF // parts)
+    grad_up = scatter_sum(
+        lambda c: jnp.einsum("tyxk,tzf->yxzkf", for_core(first_low, c), upper4, preferred_element_type=f32), False
+    )
+    first_grads = second_grads + jnp.dot(upper_low, wu.T, preferred_element_type=f32)
+    mixed_grads, gain_one, shift_one = norm_backward(first_grads, normed_one, inverse_one, vectors[4])
+    mixed_low = mixed_grads.astype(low)
+
+    most_left, most_right = max(offsets[1:]), max(e - o - rows for e, o in zip(ends[:-1], offsets[:-1]))
+    from_left = lax.ppermute(mixed_low[rows - most_left :], "mp", [(j, j + 1) for j in range(parts - 1)])
+    from_right = lax.ppermute(mixed_low[:most_right], "mp", [(j + 1, j) for j in range(parts - 1)])
+    tail = jnp.zeros((window - offsets[0] - rows, D), low)
+    joined = jnp.concatenate([from_left, mixed_low, from_right, tail], axis=0)
+    mixed_win = lax.dynamic_slice_in_dim(joined, most_left - offset, window, 0)
+
+    att4 = attended.reshape(rows, parts, D // parts)
+    grad_out = scatter_sum(
+        lambda c: jnp.einsum("tze,tyxk->yxzek", att4, for_core(mixed_low, c), preferred_element_type=f32), True
+    )
+    attended_grads = jnp.dot(mixed_win, wo.T, preferred_element_type=f32).astype(low)
+    dq, dk, dv = attention_call(
+        attend_back_kernel, window, plan, segs, (queries, keys, values, attended_grads), 3, 2
+    )
+    dq, dk, dv = (lax.dynamic_slice_in_dim(value, offset, rows, 0) for value in (dq, dk, dv))
+    grad_bias_qv = jnp.stack([jnp.sum(dq, axis=0, dtype=f32), jnp.sum(dv, axis=0, dtype=f32)])
+    input_sum = (
+        mixed_grads
+        + jnp.dot(dq, w3[0].T, preferred_element_type=f32)
+        + jnp.dot(dk, w3[1].T, preferred_element_type=f32)
+        + jnp.dot(dv, w3[2].T, preferred_element_type=f32)
+    )
+
+    def qkv_terms(value):
+        value4 = value.reshape(rows, parts, D // parts)
+        return lambda c: jnp.einsum("tyxk,tzf->yxzkf", for_core(lifted_low, c), value4, preferred_element_type=f32)
+
+    grad_q = scatter_sum(qkv_terms(dq), True)
+    grad_k = scatter_sum(qkv_terms(dk), False)
+    grad_v = scatter_sum(qkv_terms(dv), False)
+    grad_qkv = jnp.stack([grad_q, grad_k, grad_v], axis=1)
+    input_total = jnp.sum(input_sum, axis=0)
+    rows8 = jnp.stack(
+        [
+            step_time * input_total,
+            input_total,
+            jnp.sum(mixed_grads, axis=0),
+            jnp.sum(second_grads, axis=0),
+            gain_one,
+            shift_one,
+            gain_two,
+            shift_two,
+        ],
+        axis=0,
+    )
+    small = sum_all(
+        jnp.concatenate([rows8, grad_bias_qv, grad_bias_up.reshape(FF // D, D)], axis=0)
+    )
+    grad_vectors = small[:8]
+    grad_bias_qv = lax.dynamic_slice_in_dim(small[8:10], z * (D // parts), D // parts, 1)
+    grad_bias_up = lax.dynamic_slice_in_dim(small[10:].reshape(FF), z * (FF // parts), FF // parts, 0)
+    return (
+        output.astype(low),
+        input_sum.astype(low),
+        grad_qkv,
+        grad_bias_qv,
+        grad_out,
+        grad_up,
+        grad_bias_up,
+        grad_down,
+        grad_vectors,
+    )
+
+
 def solution(mesh):
     in_specs = (
         P(("dp", "mp"), None),
@@ -304,4 +838,5 @@
         P("mp", "dp"),
         P(),
     )
-    return jax.shard_map(body, mesh=mesh, in_specs=in_specs, out_specs=out_specs, check_vma=False)
+    chosen = local_body if fits_local(mesh) else body
+    return jax.shard_map(chosen, mesh=mesh, in_specs=in_specs, out_specs=out_specs, check_vma=False)

time: 1570 us -> 877 us (0.56)
  waiting for transfers between devices: 822 us -> 104 us
  Pallas kernels: 0 us -> 351 us
  matrix products: 432 us -> 160 us
  other arithmetic: 178 us -> 22.3 us
  starting transfers between devices: 1.08 us -> 108 us
  local copies, waits for them, and re-layouts: 69.2 us -> 103 us
  blocking collectives: 42.1 us -> 21.4 us
    reduce_scatter x6 -> x0, waiting for transfers between devices: 464 us -> none  [the longest x1 164 us: body(): lax.psum_scatter(jnp.dot(piece, w_out, preferred_element_type=jnp.float32...]
    pallas_call x0 -> x3, Pallas kernels: none -> 351 us  [the longest x1 265 us: gather(): pl.pallas_call(functools.partial(gather_kernel, rows, window, parts), out...]
    all_gather x4 -> x0, waiting for transfers between devices: 349 us -> none  [the longest x1 93.6 us: body(): lax.all_gather(lifted.astype(jnp.bfloat16), 'mp', axis=0, tiled=True)]
    dot_general x40 -> x24, matrix products: 432 us -> 160 us  [the longest x1 29.7 us: local_body(): upper = jnp.dot(first_low, wu, preferred_element_type=f32) + bias_up_all]
    ppermute x0 -> x43, starting transfers between devices: none -> 108 us  [the longest x41 102 us: swap(): return lax.ppermute(array, axis, [(i, i ^ bit) for i in range(size)])]
    ppermute x0 -> x43, waiting for transfers between devices: none -> 104 us  [the longest x41 104 us: swap(): return lax.ppermute(array, axis, [(i, i ^ bit) for i in range(size)])]
    convert_element_type x15 -> x17, other arithmetic: 101 us -> 7.22 us  [the longest x12 5.03 us: add_low(): (kept.astype(jnp.float32) + received.astype(jnp.float32)).astype(jnp.bflo...]
    reduce_sum x9 -> x5, other arithmetic: 55.7 us -> 5.12 us  [the longest x1 2.1 us: local_body(): jnp.sum(dv, axis=0, dtype=f32)]
  transfers between devices with their start and end apart: 12 -> 43, of which waited for: 10 -> 15; matrix products, arithmetic and copies ran while one was open for 25% -> 18% of each run, Pallas kernels for 0% -> 6%
where the time goes in v1:
time: 877 us; the launch traced here: 872 us
  Pallas kernels  351 us (40%)
  matrix products  160 us (18%)
  starting transfers between devices  108 us (12%)
  waiting for transfers between devices  104 us (12%)
  local copies, waits for them, and re-layouts  103 us (12%)
  other arithmetic  22.3 us (3%)
  blocking collectives  21.4 us (2%)
    pallas_call x1, Pallas kernels, gather(): pl.pallas_call(functools.partial(gather_kernel, rows, window, parts), out...  265 us
    ppermute x41, waiting for transfers between devices, swap(): return lax.ppermute(array, axis, [(i, i ^ bit) for i in range(size)])  104 us
    ppermute x41, starting transfers between devices, swap(): return lax.ppermute(array, axis, [(i, i ^ bit) for i in range(size)])  102 us
    pallas_call x2, Pallas kernels, attention_call(): pl.pallas_call(kernel, grid_spec=pltpu.PrefetchScalarGridSpec(num_scalar_...  86.3 us
    dot_general x1, matrix products, local_body(): upper = jnp.dot(first_low, wu, preferred_element_type=f32) + bias_up_all  29.7 us
    dot_general x2, matrix products, local_body(): jnp.einsum('tyxk,tzf->yxzkf', for_core(first_low, c), upper4, preferred_e...  20.8 us
    dot_general x6, matrix products, qkv_terms(): jnp.einsum('tyxk,tzf->yxzkf', for_core(lifted_low, c), value4, preferred_...  17.9 us
  transfers between devices with their start and end apart: 43, of which 15 were waited for; matrix products, arithmetic and copies ran while one was open for 18% of the time, Pallas kernels for 6%

profile of v1, /device:TPU:0, one launch (start us, length us, event | category | flops | bytes accessed | tf_op | source)
XLA Modules:
  0.0 871.8 jit_solution(14138185581044905779)
XLA Ops:
  2.6 13.7 %all_gather.7 = bf16[4096]{0:T(1024)(128)(2,1)S(1)} all-gather(bf16[1024]{0:T(1024)(128)(2,1)} %param.19), channel_id=1, replica_groups=mesh['dp'=8,'mp'=4] {'mp'}, dimensions={0}, use_global_device_ids=true | all-gather | bytes 10240 | tf_op jit(solution)/shard_map/all_gather | solution.py:695
  16.8 264.6 %shard_map.178 = (bf16[1536,1024]{1,0:T(8,128)(2,1)}, bf16[4,3,1024,256]{3,2,1,0:T(8,128)(2,1)}, bf16[4,256,1024]{2,1,0:T(8,128)(2,1)}, bf16[4,1024,1024]{2,1,0:T(8,128)(2,1)}, bf16[4,1024,1024]{2,1,0:T(8,128)(2,1)}) custom-call(bf16[592,1024]{1,0:T(8,128)(2,1)} %tokens.1, bf16[3,1024,256]{2,1,0:T(8,128)(2,1)} %bitcast.295, bf16[256,1024]{1,0:T(8,128)(2,1)} %w_out.1, ...), custom_call_target="tpu_custom_call" | custom-call | tf_op jit(solution)/shard_map/pallas_call | solution.py:486
  281.4 5.4 fusion.116
  286.8 4.0 copy.109
  290.8 7.7 all_gather.6
  301.0 3.0 copy.111
  304.7 7.8 convolution_convert_fusion.1.k
  312.5 4.9 add_convert_fusion.2.q
  317.5 4.9 add_convert_fusion.1.v
  322.4 32.6 %shard_map.179 = bf16[1536,1024]{1,0:T(8,128)(2,1)S(1)} custom-call(s32[12]{0:T(128)S(1)} %select_select_fusion.1.kind, s32[12]{0:T(128)S(1)} %get-tuple-element.83.start, s32[12]{0:T(128)S(1)} %slice.69.unit_seg, s32[1536,1]{1,0:T(8,128)S(1)} %fusion.62.seg, bf16[1536,1024]{1,0:T(8,128)(2,1)} %add_convert_fusion.2.q, ...), custom_call_target="tpu_custom_call" | custom-call | tf_op jit(solution)/shard_map/pallas_call | solution.py:600
  358.8 11.4 %copy.112 = bf16[1024,4,1024]{0,2,1:T(8,128)(2,1)} copy(bf16[1024,4,1024]{2,0,1:T(8,128)(2,1)} %bitcast.281) | data formatting | bytes 16777216 | tf_op jit(solution)/shard_map/transpose | solution.py:718
  370.7 29.7 %multiply_convert_fusion = (bf16[592,4096]{1,0:T(8,128)(2,1)S(1)}, f32[592,4096]{1,0:T(8,128)}, f32[592,4096]{1,0:T(8,128)}) fusion(f32[4096]{0:T(1024)S(1)} %convert_element_type.394, bf16[592,1024]{1,0:T(8,128)(2,1)S(1)} %fusion.38, bf16[1024,4096]{0,1:T(8,128)(2,1)} %bitcast.282), kind=kOutput, calls=%fused_computation.4 | convolution fusion | flops 5126094848 | bytes 33865728 | tf_op jit(solution)/shard_map/dot_general | solution.py:719
  400.4 9.8 %fusion.121 = (f32[592]{0:T(1024)S(1)}, f32[592,1024]{1,0:T(8,128)S(1)}) fusion(f32[1024]{0:T(1024)S(1)} %bitcast.332, bf16[592,4096]{1,0:T(8,128)(2,1)S(1)} %get-tuple-element.81, bf16[4096,1024]{1,0:T(8,128)(2,1)} %bitcast.337, f32[1024]{0:T(1024)S(1)} %bitcast.325, f32[1024]{0:T(1024)S(1)} %bitcast.303, f32[592]{0:T(1024)S(1)} %add_rsqrt_fusion.1, ...), kind=kOutput, calls=%fused_computation.249 | convolution fusion | flops 4970298880 | bytes 18107328 | tf_op jit(solution)/shard_map/dot_general | solution.py:723
  414.8 16.9 %convert_reduce_fusion = (f32[4096]{0:T(1024)S(1)}, bf16[592,4096]{1,0:T(8,128)(2,1)}) fusion(f32[592,4096]{1,0:T(8,128)} %get-tuple-element.82, f32[592,4096]{1,0:T(8,128)} %get-tuple-element.129, f32[4096]{0:T(1024)S(1)} %convert_element_type.394, bf16[592,1024]{1,0:T(8,128)(2,1)S(1)} %convert_element_type.398, bf16[4096,1024]{1,0:T(8,128)(2,1)} %bitcast.338), kind=kOutput, calls=%fused_computation.2 | convolution fusion | flops 5007273984 | bytes 33882112 | tf_op jit(solution)/shard_map/dot_general | solution.py:739
  431.7 9.8 %multiply_reduce_fusion = (f32[1024]{0:T(1024)S(1)}, f32[592]{0:T(1024)S(1)}, f32[592]{0:T(1024)S(1)}, f32[1024]{0:T(1024)S(1)}, f32[592,1024]{1,0:T(8,128)S(1)}) fusion(f32[592,1024]{1,0:T(8,128)S(1)} %get-tuple-element.128, f32[592]{0:T(1024)S(1)} %add_rsqrt_fusion.1, f32[592]{0:T(1024)S(1)} %broadcast_multiply_fusion.5, f32[1024]{0:T(1024)S(1)} %bitcast.304, ...), kind=kOutput, calls=%fused_computation.59 | convolution fusion | flops 4972114944 | bytes 20534528 | tf_op jit(solution)/shard_map/dot_general | solution.py:747
  444.0 4.9 collective-permute-start
  451.2 2.9 reshape.234
  455.8 5.2 constant_dynamic-slice_fusion.5
  463.0 11.0 %reshape.235 = bf16[592,4,1024]{2,1,0:T(4,128)(2,1)} reshape(bf16[592,4096]{1,0:T(8,128)(2,1)} %get-tuple-element.72) | data formatting | bytes 9699328 | tf_op jit(solution)/shard_map/reshape | solution.py:743
  474.0 3.4 reshape.238
  477.4 4.1 reshape.236
  481.5 7.8 constant_dynamic-slice_fusion.1
  489.3 14.3 %convert_bitcast_fusion.1 = bf16[2,2,4,128,1024]{3,4,1,0,2:T(8,128)(2,1)} fusion(bf16[592,4,1024,1,1]{2,1,0,4,3:T(4,128)(2,1)} %bitcast.287, bf16[592,2,2,1,128]{4,3,2,1,0:T(2,128)(2,1)S(1)} %get-tuple-element.136), kind=kOutput, calls=%fused_computation.41 | convolution fusion | flops 2485125120 | bytes 9650176 | tf_op jit(solution)/shard_map/tyxk,tzf->yxzkf/dot_general | solution.py:745
  504.0 11.0 %reshape.239 = bf16[592,4,1024]{2,1,0:T(4,128)(2,1)} reshape(bf16[592,4096]{1,0:T(8,128)(2,1)} %copy-done.12) | data formatting | bytes 9699328 | tf_op jit(solution)/shard_map/reshape | solution.py:735
  515.0 11.0 %convert_bitcast_fusion = bf16[2,2,4,1024,128]{3,4,2,1,0:T(8,128)(2,1)} fusion(bf16[592,4,1024,1,1]{2,1,0,4,3:T(4,128)(2,1)} %bitcast.275, bf16[592,2,2,1,128]{4,3,2,1,0:T(2,128)(2,1)S(1)} %copy-done.26), kind=kOutput, calls=%fused_computation.40 | convolution fusion | flops 2485125120 | bytes 9650176 | tf_op jit(solution)/shard_map/tzf,tyxk->yxzfk/dot_general | solution.py:737
  526.3 8.1 convolution_convert_fusion.g
  534.4 53.6 %shard_map.180 = (bf16[1536,1024]{1,0:T(8,128)(2,1)S(1)}, bf16[1536,1024]{1,0:T(8,128)(2,1)}, bf16[1536,1024]{1,0:T(8,128)(2,1)}) custom-call(s32[12]{0:T(128)S(1)} %select_select_fusion.1.kind, s32[12]{0:T(128)S(1)} %get-tuple-element.83.start, s32[12]{0:T(128)S(1)} %slice.69.unit_seg, s32[1536,1]{1,0:T(8,128)S(1)} %fusion.62.seg, ...), custom_call_target="tpu_custom_call" | custom-call | tf_op jit(solution)/shard_map/pallas_call | solution.py:600
  599.2 23.5 %collective-permute-start.20 = (f32[14,1024]{1,0:T(8,128)S(1)}, f32[14,1024]{1,0:T(8,128)}, u32[]{:S(2)}, u32[]{:S(2)}) collective-permute-start(f32[14,1024]{1,0:T(8,128)S(1)} %concatenate.7), channel_id=1, source_target_pairs={{0,4},{4,0},{8,12},{12,8},{16,20},{20,16},{24,28},{28,24},{1,5},{5... | collective-permute-start | bytes 172040 | tf_op jit(solution)/shard_map/ppermute | solution.py:636
  626.2 4.8 collective-permute-start.26
  632.4 3.5 reshape.229
  637.0 3.9 constant_dynamic-slice_fusion.8
  641.9 3.1 collective-permute-done.21
  648.0 3.4 fusion.48
  654.0 25.7 %collective-permute-start.23 = (f32[14,1024]{1,0:T(8,128)S(1)}, f32[14,1024]{1,0:T(8,128)}, u32[]{:S(2)}, u32[]{:S(2)}) collective-permute-start(f32[14,1024]{1,0:T(8,128)S(1)} %add.486), channel_id=1, source_target_pairs={{0,1},{1,0},{2,3},{3,2},{4,5},{5,4},{6,7},{7,6},{8,9},{9,8},{10,11... | collective-permute-start | bytes 172040 | tf_op jit(solution)/shard_map/ppermute | solution.py:636
  681.1 3.7 fusion.47
  690.6 4.7 collective-permute-done.24
  695.8 3.4 fusion.46
  702.6 3.9 collective-permute-done.29
  707.1 3.7 collective-permute-done.28
  723.2 6.0 collective-permute-done.15
  731.2 6.5 fusion.7
  739.1 6.3 fusion.6
  750.9 46.9 %collective-permute-done.10 = bf16[4,128,256]{1,2,0:T(8,128)(2,1)S(1)} collective-permute-done((bf16[4,128,256]{1,2,0:T(8,128)(2,1)S(1)}, bf16[4,128,256]{1,2,0:T(8,128)(2,1)S(1)}, u32[]{:S(2)}, u32[]{:S(2)}) %collective-permute-start.10) | collective-permute-done | bytes 262176 | tf_op jit(solution)/shard_map/ppermute | solution.py:636
  817.4 8.3 collective-permute-done.33
  833.3 3.8 collective-permute-done.36
  837.2 14.1 %collective-permute-start.40 = (bf16[1024,128]{0,1:T(8,128)(2,1)S(1)}, bf16[1024,128]{0,1:T(8,128)(2,1)}, u32[]{:S(2)}, u32[]{:S(2)}) collective-permute-start(bf16[1024,128]{0,1:T(8,128)(2,1)S(1)} %get-tuple-element.99), channel_id=1, source_target_pairs={{0,1},{1,0},{2,3},{3,2},{4,5},{5,4},{6,7},{7,6},{8,9},{9,8},{10,11... | collective-permute-start | bytes 786440 | tf_op jit(solution)/shard_map/ppermute | solution.py:636
  852.2 8.7 collective-permute-done.35
  863.1 6.2 collective-permute-done.41
  (270 shorter events, 111.6 us)
Async XLA Ops:
  304.7 50.4 %copy-start.31 = (f32[1,1024]{1,0:T(1,128)}, f32[1,1024]{1,0:T(1,128)S(1)}, u32[]{:S(2)}) copy-start(f32[1,1024]{1,0:T(1,128)S(1)} %get-tuple-element.122) | copy-start | bytes 12292
  304.7 50.4 %copy-start.33 = (f32[1,1024]{1,0:T(1,128)}, f32[1,1024]{1,0:T(1,128)S(1)}, u32[]{:S(2)}) copy-start(f32[1,1024]{1,0:T(1,128)S(1)} %get-tuple-element.123) | copy-start | bytes 12292
  322.4 32.8 %copy-start.39 = (bf16[4,256,1024]{2,1,0:T(8,128)(2,1)S(1)}, bf16[4,256,1024]{2,1,0:T(8,128)(2,1)}, u32[]{:S(2)}) copy-start(bf16[4,256,1024]{2,1,0:T(8,128)(2,1)} %get-tuple-element.19) | copy-start | bytes 6291460
  370.6 29.8 %copy-start.10 = (bf16[592,1024]{1,0:T(8,128)(2,1)}, bf16[592,1024]{1,0:T(8,128)(2,1)S(1)}, u32[]{:S(2)}) copy-start(bf16[592,1024]{1,0:T(8,128)(2,1)S(1)} %fusion.38) | copy-start | bytes 3637252
  370.7 29.7 %copy-start.36 = (f32[1,1024]{1,0:T(1,128)S(1)}, f32[1,1024]{1,0:T(1,128)}, u32[]{:S(2)}) copy-start(f32[1,1024]{1,0:T(1,128)} %get-tuple-element.118) | copy-start | bytes 12292
  444.0 82.3 %collective-permute-start = (bf16[496,1024]{1,0:T(8,128)(2,1)}, bf16[496,1024]{1,0:T(8,128)(2,1)}, u32[]{:S(2)}, u32[]{:S(2)}) collective-permute-start(bf16[496,1024]{1,0:T(8,128)(2,1)} %slice.91), channel_id=1, source_target_pairs={{0,1},{1,2},{2,3},{4,5},{5,6},{6,7},{8,9},{9,10},{10,11},{12,13},{... | collective-permute-start | bytes 3047432 | tf_op jit(solution)/shard_map/ppermute | solution.py:752
  449.9 76.5 %collective-permute-start.1 = (bf16[480,1024]{1,0:T(8,128)(2,1)}, bf16[480,1024]{1,0:T(8,128)(2,1)}, u32[]{:S(2)}, u32[]{:S(2)}) collective-permute-start(bf16[480,1024]{1,0:T(8,128)(2,1)} %slice.92), channel_id=1, source_target_pairs={{1,0},{2,1},{3,2},{5,4},{6,5},{7,6},{9,8},{10,9},{11,10},{13,12},{... | collective-permute-start | bytes 2949128 | tf_op jit(solution)/shard_map/ppermute | solution.py:753
  463.0 159.6 %collective-permute-start.25 = (bf16[2,2,4,256,128]{3,4,2,1,0:T(8,128)(2,1)}, bf16[2,2,4,256,128]{3,4,2,1,0:T(8,128)(2,1)}, u32[]{:S(2)}, u32[]{:S(2)}) collective-permute-start(bf16[2,2,4,256,128]{3,4,2,1,0:T(8,128)(2,1)} %fusion.49), channel_id=1, source_target_pairs={{0,4},{4,0},{8,12},{12,8},{16,20},{20,16},{24,28},{28,24},{1,5},{5... | collective-permute-start | bytes 3145736 | tf_op jit(solution)/shard_map/ppermute | solution.py:636
  503.5 227.7 %collective-permute-start.31 = (bf16[2,2,4,128,1024]{3,4,1,0,2:T(8,128)(2,1)}, bf16[2,2,4,128,1024]{3,4,1,0,2:T(8,128)(2,1)}, u32[]{:S(2)}, u32[]{:S(2)}) collective-permute-start(bf16[2,2,4,128,1024]{3,4,1,0,2:T(8,128)(2,1)} %convert_bitcast_fusion.1), channel_id=1, source_target_pairs={{0,4},{4,0},{8,12},{12,8},{16,20},{20,16},{24,28},{28,24},{1,5},{5... | collective-permute-start | bytes 12582920 | tf_op jit(solution)/shard_map/ppermute | solution.py:636
  526.0 212.5 %collective-permute-start.37 = (bf16[2,2,4,1024,128]{3,4,2,1,0:T(8,128)(2,1)}, bf16[2,2,4,1024,128]{3,4,2,1,0:T(8,128)(2,1)}, u32[]{:S(2)}, u32[]{:S(2)}) collective-permute-start(bf16[2,2,4,1024,128]{3,4,2,1,0:T(8,128)(2,1)} %convert_bitcast_fusion), channel_id=1, source_target_pairs={{0,4},{4,0},{8,12},{12,8},{16,20},{20,16},{24,28},{28,24},{1,5},{5... | collective-permute-start | bytes 12582920 | tf_op jit(solution)/shard_map/ppermute | solution.py:636
  599.2 36.8 %collective-permute-start.20 = (f32[14,1024]{1,0:T(8,128)S(1)}, f32[14,1024]{1,0:T(8,128)}, u32[]{:S(2)}, u32[]{:S(2)}) collective-permute-start(f32[14,1024]{1,0:T(8,128)S(1)} %concatenate.7), channel_id=1, source_target_pairs={{0,4},{4,0},{8,12},{12,8},{16,20},{20,16},{24,28},{28,24},{1,5},{5... | collective-permute-start | bytes 172040 | tf_op jit(solution)/shard_map/ppermute | solution.py:636
  626.2 53.6 %collective-permute-start.26 = (bf16[2,4,256,128]{2,3,1,0:T(8,128)(2,1)}, bf16[2,4,256,128]{2,3,1,0:T(8,128)(2,1)}, u32[]{:S(2)}, u32[]{:S(2)}) collective-permute-start(bf16[2,4,256,128]{2,3,1,0:T(8,128)(2,1)} %dynamic-slice_bitcast_fusion.4), channel_id=1, source_target_pairs={{0,8},{4,12},{8,0},{12,4},{16,24},{20,28},{24,16},{28,20},{1,9},{5... | collective-permute-start | bytes 1572872 | tf_op jit(solution)/shard_map/ppermute | solution.py:636
  636.9 8.0 collective-permute-start.21
  646.4 6.8 collective-permute-start.22
  653.1 58.5 %collective-permute-start.14 = (bf16[2,2,4,128,256]{3,4,2,1,0:T(8,128)(2,1)}, bf16[2,2,4,128,256]{3,4,2,1,0:T(8,128)(2,1)}, u32[]{:S(2)}, u32[]{:S(2)}) collective-permute-start(bf16[2,2,4,128,256]{3,4,2,1,0:T(8,128)(2,1)} %fusion.48), channel_id=1, source_target_pairs={{0,4},{4,0},{8,12},{12,8},{16,20},{20,16},{24,28},{28,24},{1,5},{5... | collective-permute-start | bytes 3145736 | tf_op jit(solution)/shard_map/ppermute | solution.py:636
  654.0 31.9 %collective-permute-start.23 = (f32[14,1024]{1,0:T(8,128)S(1)}, f32[14,1024]{1,0:T(8,128)}, u32[]{:S(2)}, u32[]{:S(2)}) collective-permute-start(f32[14,1024]{1,0:T(8,128)S(1)} %add.486), channel_id=1, source_target_pairs={{0,1},{1,0},{2,3},{3,2},{4,5},{5,4},{6,7},{7,6},{8,9},{9,8},{10,11... | collective-permute-start | bytes 172040 | tf_op jit(solution)/shard_map/ppermute | solution.py:636
  681.0 8.6 collective-permute-start.27
  686.0 29.1 %collective-permute-start.8 = (bf16[2,2,4,128,256]{3,4,2,1,0:T(8,128)(2,1)}, bf16[2,2,4,128,256]{3,4,2,1,0:T(8,128)(2,1)}, u32[]{:S(2)}, u32[]{:S(2)}) collective-permute-start(bf16[2,2,4,128,256]{3,4,2,1,0:T(8,128)(2,1)} %fusion.47), channel_id=1, source_target_pairs={{0,4},{4,0},{8,12},{12,8},{16,20},{20,16},{24,28},{28,24},{1,5},{5... | collective-permute-start | bytes 3145736 | tf_op jit(solution)/shard_map/ppermute | solution.py:636
  689.6 5.7 collective-permute-start.24
  695.3 6.1 collective-permute-start.30
  701.4 5.2 collective-permute-start.29
  706.5 4.3 collective-permute-start.28
  710.8 8.3 collective-permute-start.2
  714.4 14.8 %collective-permute-start.15 = (bf16[2,4,128,256]{2,3,1,0:T(8,128)(2,1)S(1)}, bf16[2,4,128,256]{2,3,1,0:T(8,128)(2,1)S(1)}, u32[]{:S(2)}, u32[]{:S(2)}) collective-permute-start(bf16[2,4,128,256]{2,3,1,0:T(8,128)(2,1)S(1)} %dynamic-slice_bitcast_fusion.5), channel_id=1, source_target_pairs={{0,16},{4,20},{8,24},{12,28},{16,0},{20,4},{24,8},{28,12},{1,17},{... | collective-permute-start | bytes 1572872 | tf_op jit(solution)/shard_map/ppermute | solution.py:636
  717.5 28.6 %collective-permute-start.9 = (bf16[2,4,128,256]{2,3,1,0:T(8,128)(2,1)S(1)}, bf16[2,4,128,256]{2,3,1,0:T(8,128)(2,1)S(1)}, u32[]{:S(2)}, u32[]{:S(2)}) collective-permute-start(bf16[2,4,128,256]{2,3,1,0:T(8,128)(2,1)S(1)} %dynamic-slice_bitcast_fusion.6), channel_id=1, source_target_pairs={{0,16},{4,20},{8,24},{12,28},{16,0},{20,4},{24,8},{28,12},{1,17},{... | collective-permute-start | bytes 1572872 | tf_op jit(solution)/shard_map/ppermute | solution.py:636
  721.4 26.5 %collective-permute-start.3 = (bf16[2,4,128,256]{2,3,0,1:T(8,128)(2,1)S(1)}, bf16[2,4,128,256]{2,3,0,1:T(8,128)(2,1)S(1)}, u32[]{:S(2)}, u32[]{:S(2)}) collective-permute-start(bf16[2,4,128,256]{2,3,0,1:T(8,128)(2,1)S(1)} %dynamic-slice_bitcast_fusion.7), channel_id=1, source_target_pairs={{0,8},{4,12},{8,0},{12,4},{16,24},{20,28},{24,16},{28,20},{1,9},{5... | collective-permute-start | bytes 1572872 | tf_op jit(solution)/shard_map/ppermute | solution.py:636
  729.4 19.8 %collective-permute-start.16 = (bf16[4,128,256]{1,2,0:T(8,128)(2,1)S(1)}, bf16[4,128,256]{1,2,0:T(8,128)(2,1)S(1)}, u32[]{:S(2)}, u32[]{:S(2)}) collective-permute-start(bf16[4,128,256]{1,2,0:T(8,128)(2,1)S(1)} %dynamic-slice_bitcast_fusion.15), channel_id=1, source_target_pairs={{0,8},{4,12},{8,0},{12,4},{16,24},{20,28},{24,16},{28,20},{1,9},{5... | collective-permute-start | bytes 786440 | tf_op jit(solution)/shard_map/ppermute | solution.py:636
  738.0 62.4 %collective-permute-start.32 = (bf16[2,4,128,1024]{2,3,0,1:T(8,128)(2,1)S(1)}, bf16[2,4,128,1024]{2,3,0,1:T(8,128)(2,1)S(1)}, u32[]{:S(2)}, u32[]{:S(2)}) collective-permute-start(bf16[2,4,128,1024]{2,3,0,1:T(8,128)(2,1)S(1)} %dynamic-slice_bitcast_fusion.1), channel_id=1, source_target_pairs={{0,16},{4,20},{8,24},{12,28},{16,0},{20,4},{24,8},{28,12},{1,17},{... | collective-permute-start | bytes 6291464 | tf_op jit(solution)/shard_map/ppermute | solution.py:636
  745.6 57.7 %collective-permute-start.38 = (bf16[2,4,1024,128]{2,3,1,0:T(8,128)(2,1)S(1)}, bf16[2,4,1024,128]{2,3,1,0:T(8,128)(2,1)S(1)}, u32[]{:S(2)}, u32[]{:S(2)}) collective-permute-start(bf16[2,4,1024,128]{2,3,1,0:T(8,128)(2,1)S(1)} %dynamic-slice_bitcast_fusion), channel_id=1, source_target_pairs={{0,8},{4,12},{8,0},{12,4},{16,24},{20,28},{24,16},{28,20},{1,9},{5... | collective-permute-start | bytes 6291464 | tf_op jit(solution)/shard_map/ppermute | solution.py:636
  746.3 51.5 %collective-permute-start.10 = (bf16[4,128,256]{1,2,0:T(8,128)(2,1)S(1)}, bf16[4,128,256]{1,2,0:T(8,128)(2,1)S(1)}, u32[]{:S(2)}, u32[]{:S(2)}) collective-permute-start(bf16[4,128,256]{1,2,0:T(8,128)(2,1)S(1)} %dynamic-slice_bitcast_fusion.16), channel_id=1, source_target_pairs={{0,8},{4,12},{8,0},{12,4},{16,24},{20,28},{24,16},{28,20},{1,9},{5... | collective-permute-start | bytes 786440 | tf_op jit(solution)/shard_map/ppermute | solution.py:636
  748.1 50.0 %collective-permute-start.4 = (bf16[4,128,256]{1,2,0:T(8,128)(2,1)S(1)}, bf16[4,128,256]{1,2,0:T(8,128)(2,1)S(1)}, u32[]{:S(2)}, u32[]{:S(2)}) collective-permute-start(bf16[4,128,256]{1,2,0:T(8,128)(2,1)S(1)} %dynamic-slice_bitcast_fusion.17), channel_id=1, source_target_pairs={{0,16},{4,20},{8,24},{12,28},{16,0},{20,4},{24,8},{28,12},{1,17},{... | collective-permute-start | bytes 786440 | tf_op jit(solution)/shard_map/ppermute | solution.py:636
  749.3 55.6 %collective-permute-start.19 = (bf16[128,256]{0,1:T(8,128)(2,1)S(1)}, bf16[128,256]{0,1:T(8,128)(2,1)S(1)}, u32[]{:S(2)}, u32[]{:S(2)}) collective-permute-start(bf16[128,256]{0,1:T(8,128)(2,1)S(1)} %get-tuple-element.115), channel_id=1, source_target_pairs={{0,3},{1,2},{2,1},{3,0},{4,7},{5,6},{6,5},{7,4},{8,11},{9,10},{10,... | collective-permute-start | bytes 196616 | tf_op jit(solution)/shard_map/ppermute | solution.py:636
  797.9 7.1 collective-permute-start.18
  798.1 9.0 %collective-permute-start.17 = (bf16[128,256]{0,1:T(8,128)(2,1)S(1)}, bf16[128,256]{0,1:T(8,128)(2,1)S(1)}, u32[]{:S(2)}, u32[]{:S(2)}) collective-permute-start(bf16[128,256]{0,1:T(8,128)(2,1)S(1)} %get-tuple-element.114), channel_id=1, source_target_pairs={{0,1},{1,0},{2,3},{3,2},{4,5},{5,4},{6,7},{7,6},{8,9},{9,8},{10,11... | collective-permute-start | bytes 196616 | tf_op jit(solution)/shard_map/ppermute | solution.py:636
  800.3 7.5 collective-permute-start.13
  803.3 22.4 %collective-permute-start.33 = (bf16[4,128,1024]{1,2,0:T(8,128)(2,1)S(1)}, bf16[4,128,1024]{1,2,0:T(8,128)(2,1)S(1)}, u32[]{:S(2)}, u32[]{:S(2)}) collective-permute-start(bf16[4,128,1024]{1,2,0:T(8,128)(2,1)S(1)} %dynamic-slice_bitcast_fusion.3), channel_id=1, source_target_pairs={{0,8},{4,12},{8,0},{12,4},{16,24},{20,28},{24,16},{28,20},{1,9},{5... | collective-permute-start | bytes 3145736 | tf_op jit(solution)/shard_map/ppermute | solution.py:636
  804.9 6.7 collective-permute-start.12
  805.0 6.6 collective-permute-start.11
  807.1 23.4 %collective-permute-start.39 = (bf16[4,1024,128]{1,2,0:T(8,128)(2,1)S(1)}, bf16[4,1024,128]{1,2,0:T(8,128)(2,1)S(1)}, u32[]{:S(2)}, u32[]{:S(2)}) collective-permute-start(bf16[4,1024,128]{1,2,0:T(8,128)(2,1)S(1)} %dynamic-slice_bitcast_fusion.2), channel_id=1, source_target_pairs={{0,16},{4,20},{8,24},{12,28},{16,0},{20,4},{24,8},{28,12},{1,17},{... | collective-permute-start | bytes 3145736 | tf_op jit(solution)/shard_map/ppermute | solution.py:636
  807.9 6.6 collective-permute-start.7
  811.6 5.3 collective-permute-start.6
  811.6 5.8 collective-permute-start.5
  826.0 11.1 %collective-permute-start.36 = (bf16[128,1024]{0,1:T(8,128)(2,1)S(1)}, bf16[128,1024]{0,1:T(8,128)(2,1)S(1)}, u32[]{:S(2)}, u32[]{:S(2)}) collective-permute-start(bf16[128,1024]{0,1:T(8,128)(2,1)S(1)} %get-tuple-element.103), channel_id=1, source_target_pairs={{0,3},{1,2},{2,1},{3,0},{4,7},{5,6},{6,5},{7,4},{8,11},{9,10},{10,... | collective-permute-start | bytes 786440 | tf_op jit(solution)/shard_map/ppermute | solution.py:636
  827.7 33.1 %collective-permute-start.35 = (bf16[128,1024]{0,1:T(8,128)(2,1)S(1)}, bf16[128,1024]{0,1:T(8,128)(2,1)}, u32[]{:S(2)}, u32[]{:S(2)}) collective-permute-start(bf16[128,1024]{0,1:T(8,128)(2,1)S(1)} %get-tuple-element.104), channel_id=1, source_target_pairs={{0,2},{1,3},{2,0},{3,1},{4,6},{5,7},{6,4},{7,5},{8,10},{9,11},{10,... | collective-permute-start | bytes 786440 | tf_op jit(solution)/shard_map/ppermute | solution.py:636
  827.7 33.1 %collective-permute-start.34 = (bf16[128,1024]{0,1:T(8,128)(2,1)S(1)}, bf16[128,1024]{0,1:T(8,128)(2,1)}, u32[]{:S(2)}, u32[]{:S(2)}) collective-permute-start(bf16[128,1024]{0,1:T(8,128)(2,1)S(1)} %get-tuple-element.102), channel_id=1, source_target_pairs={{0,1},{1,0},{2,3},{3,2},{4,5},{5,4},{6,7},{7,6},{8,9},{9,8},{10,11... | collective-permute-start | bytes 786440 | tf_op jit(solution)/shard_map/ppermute | solution.py:636
  831.7 31.4 %collective-permute-start.42 = (bf16[1024,128]{0,1:T(8,128)(2,1)}, bf16[1024,128]{0,1:T(8,128)(2,1)}, u32[]{:S(2)}, u32[]{:S(2)}) collective-permute-start(bf16[1024,128]{0,1:T(8,128)(2,1)} %get-tuple-element.100), channel_id=1, source_target_pairs={{0,3},{1,2},{2,1},{3,0},{4,7},{5,6},{6,5},{7,4},{8,11},{9,10},{10,... | collective-permute-start | bytes 786440 | tf_op jit(solution)/shard_map/ppermute | solution.py:636
  833.3 35.9 %collective-permute-start.41 = (bf16[1024,128]{0,1:T(8,128)(2,1)S(1)}, bf16[1024,128]{0,1:T(8,128)(2,1)}, u32[]{:S(2)}, u32[]{:S(2)}) collective-permute-start(bf16[1024,128]{0,1:T(8,128)(2,1)S(1)} %get-tuple-element.101), channel_id=1, source_target_pairs={{0,2},{1,3},{2,0},{3,1},{4,6},{5,7},{6,4},{7,5},{8,10},{9,11},{10,... | collective-permute-start | bytes 786440 | tf_op jit(solution)/shard_map/ppermute | solution.py:636
  837.2 32.1 %collective-permute-start.40 = (bf16[1024,128]{0,1:T(8,128)(2,1)S(1)}, bf16[1024,128]{0,1:T(8,128)(2,1)}, u32[]{:S(2)}, u32[]{:S(2)}) collective-permute-start(bf16[1024,128]{0,1:T(8,128)(2,1)S(1)} %get-tuple-element.99), channel_id=1, source_target_pairs={{0,1},{1,0},{2,3},{3,2},{4,5},{5,4},{6,7},{7,6},{8,9},{9,8},{10,11... | collective-permute-start | bytes 786440 | tf_op jit(solution)/shard_map/ppermute | solution.py:636
  (39 other events, 294.1 us)

commit v2 on v1

--- a/solution.py
+++ b/solution.py
@@ -1,4 +1,5 @@
 import functools
+import heapq
 
 import jax
 import jax.numpy as jnp
@@ -332,8 +333,6 @@
             count = size // 2
             start = start + half * count
         rows_at = pl.ds(pl.multiple_of(start, 16), count)
-        if len(ref.shape) == 4:
-            return ref.at[index, :, rows_at, :]
         return ref.at[index, rows_at, :]
 
     chunks = [(g, k) for g in range(4) for k in others]
@@ -350,7 +349,7 @@
         g, k = chunks[i]
         size = sizes[g]
         rows_at = pl.ds(pl.multiple_of(d * size, 16), size)
-        src = shards[g].at[:, rows_at, :] if g == 0 else shards[g].at[rows_at, :]
+        src = shards[g].at[rows_at, :]
         remote(i, 0, src, part(fulls[g], z, d, size), (d, z ^ k))
 
     def place(i, owner, half=None):
@@ -414,8 +413,6 @@
         def _(fill=fill):
             fill.start()
 
-    for i in range(3, len(chunks)):
-        first_hop(i)
 
     def stage_one(i):
         copies[i, 0].wait_recv()
@@ -441,6 +438,8 @@
     for i in range(n + 2):
         if i < n:
             stage_one(i)
+            if i + 3 < n:
+                first_hop(i + 3)
         if 0 <= i - 1 < n:
             stage_two(i - 1)
         if 0 <= i - 2 < n:
@@ -492,7 +491,7 @@
             jax.ShapeDtypeStruct((parts,) + w_up.shape, low),
             jax.ShapeDtypeStruct((parts,) + w_down.shape, low),
         ],
-        in_specs=[any_] * 5,
+        in_specs=[pl.BlockSpec(memory_space=pltpu.VMEM)] * 5,
         out_specs=[any_] * 5,
         scratch_shapes=[
             pltpu.SemaphoreType.DMA((12, 10)),
@@ -501,7 +500,7 @@
             pltpu.SemaphoreType.DMA((2,)),
             pltpu.SemaphoreType.DMA((7,)),
         ],
-        compiler_params=pltpu.CompilerParams(collective_id=0, has_side_effects=True),
+        compiler_params=pltpu.CompilerParams(collective_id=0, has_side_effects=True, vmem_limit_bytes=32 * 2**20),
     )(tokens, w_qkv, w_out, w_up, w_down)
 
 
@@ -555,60 +554,22 @@
     lax.fori_loop(FIRST_OWN, LAST_OWN + 1, unit, 0)
 
 
-def attend_back_kernel(kind, start, unit_seg, seg, q, k, v, g, dq, dk, dv, k_sum, v_sum):
-    k_sum[...] = jnp.zeros_like(k_sum)
-    v_sum[...] = jnp.zeros_like(v_sum)
-    scale = HD ** (-0.5)
-
-    def unit(u, carry):
-        mine = pl.ds(pl.multiple_of(u * UNIT, UNIT), UNIT)
-
-        def run(at, valid):
-            pair = two_heads(q[mine, :])
-            grads = two_heads(g[mine, :])
-            keys = k[at, :]
-            chances = weights_of(keys, pair, valid)
-            flow = lax.dot_general(v[at, :], grads, NT, preferred_element_type=jnp.float32)
-            inner = jnp.sum(chances * flow, axis=0, keepdims=True)
-            low = (chances * (flow - inner)).astype(jnp.bfloat16)
-            v_sum[at, :] += jnp.dot(chances.astype(jnp.bfloat16), grads, preferred_element_type=jnp.float32)
-            k_sum[at, :] += jnp.dot(low, pair, preferred_element_type=jnp.float32)
-
-            @pl.when((u >= FIRST_OWN) & (u <= LAST_OWN))
-            def _():
-                flipped = lax.dot_general(keys, low, TN, preferred_element_type=jnp.float32)
-                dq[mine, :] = (from_two(flipped) * scale).astype(dq.dtype)
-
-        @pl.when(kind[u] == 2)
-        def _():
-            run(pl.ds(pl.multiple_of(start[u], UNIT), LONG * UNIT), None)
-
-        @pl.when(kind[u] == 1)
-        def _():
-            run(mine, seg[mine, :] == unit_seg[u])
-
-        return carry
-
-    lax.fori_loop(0, q.shape[0] // UNIT, unit, 0)
-    dk[...] = (k_sum[...] * scale).astype(dk.dtype)
-    dv[...] = v_sum[...].astype(dv.dtype)
-
-
-def attention_call(kernel, window, plan, segs, arrays, outs, scratch):
-    column = pl.BlockSpec((window, 2 * HD), lambda p, *_: (0, p))
-    whole = pl.BlockSpec((window, 1), lambda p, *_: (0, 0))
+def attention_call(window, parts, plan, segs, qkv):
+    cut = D // parts
+    pairs = cut // (2 * HD)
+    spec = lambda base: pl.BlockSpec((None, window, 2 * HD), lambda c, p, *_: (c, 0, base * pairs + p))
+    whole = pl.BlockSpec((window, 1), lambda c, p, *_: (0, 0))
     return pl.pallas_call(
-        kernel,
+        attend_kernel,
         grid_spec=pltpu.PrefetchScalarGridSpec(
             num_scalar_prefetch=3,
-            grid=(D // (2 * HD),),
-            in_specs=[whole] + [column] * len(arrays),
-            out_specs=[column] * outs,
-            scratch_shapes=[pltpu.VMEM((window, 2 * HD), jnp.float32)] * scratch,
+            grid=(parts, pairs),
+            in_specs=[whole, spec(0), spec(1), spec(2)],
+            out_specs=pl.BlockSpec((window, 2 * HD), lambda c, p, *_: (0, c * pairs + p)),
         ),
-        out_shape=[jax.ShapeDtypeStruct((window, D), jnp.bfloat16)] * outs,
+        out_shape=jax.ShapeDtypeStruct((window, D), jnp.bfloat16),
         compiler_params=pltpu.CompilerParams(vmem_limit_bytes=48 * 2**20),
-    )(*plan, segs[:, None], *arrays)
+    )(*plan, segs[:, None], qkv, qkv, qkv)
 
 
 def unit_plan(segs, z, offsets, rows, window):
@@ -636,36 +597,587 @@
     return lax.ppermute(array, axis, [(i, i ^ bit) for i in range(size)])
 
 
-def choose(array, index, axis):
-    return lax.dynamic_index_in_dim(array, index, axis, keepdims=False)
-
-
-def add_low(kept, received):
-    return (kept.astype(jnp.float32) + received.astype(jnp.float32)).astype(jnp.bfloat16)
-
-
-def scatter_sum(make, x_first):
+class Clock:
+    def __init__(self):
+        self.now = 0.0
+        self.free = {}
+        self.queue = []
+        self.count = 0
+
+    def send(self, link, size, action, share=1.0):
+        rate = {"c": 400e3, "x": 44e3, "y": 44e3, "z": 44e3}[link]
+        begin = max(self.now, self.free.get(link, 0.0))
+        end = begin + share * size / rate
+        self.free[link] = end
+        self.count += 1
+        heapq.heappush(self.queue, (end + 1.5, self.count, action))
+
+    def work(self, time):
+        self.now += time
+        while self.queue and self.queue[0][0] <= self.now:
+            heapq.heappop(self.queue)[2]()
+
+    def drain(self):
+        while self.queue:
+            ready, _, action = heapq.heappop(self.queue)
+            self.now = max(self.now, ready)
+            action()
+
+
+def block_owners(d, core, x_first):
+    x, y = lax.rem(d // 2, 2), d // 4
+    if x_first:
+        return [4 * b + 2 * a + core for a in (1 - x, x) for b in (1 - y, y)]
+    return [4 * b + 2 * a + core for b in (1 - y, y) for a in (1 - x, x)]
+
+
+RING = (2, 3, 1, 0)
+
+
+def back_kernel(
+    rows, window, parts, perm, back, sec_low, sec2, inverse, gain, small_in, kf, qf,
+    first_t, lift_t, second_grads, normed_one, act2, dgelu, att2, qkv, f_qkv, f_out, f_up, f_down,
+    input_grad, g_qkv, g_out, g_up, g_down, small_out,
+    acc, normed, turned, arena, act, slope, y, up2, w_in, mixed2, stage, mixed_win, small, small_in_far,
+    s_down, s_up, s_out, s_qkv, k_down, k_up, k_out, k_qkv,
+    r_down, r_up, r_out, r_qkv, t_down, t_up, t_out, t_qkv, z_down, z_up, z_out, z_qkv,
+    local, hop_send, hop_recv, pair_send, pair_recv, halo_send, halo_recv, small_send, small_recv,
+):
+    f32, low = jnp.float32, jnp.bfloat16
     d = lax.axis_index("dp")
     z = lax.axis_index("mp")
-    core, x, y = d % 2, (d // 2) % 2, d // 4
-    low = jnp.bfloat16
-    away = swap(make(1 - core).astype(low), "dp", 1)
-    terms = add_low(make(core), away)
-    order = [(1, x, 2), (0, y, 4)] if x_first else [(0, y, 4), (1, x, 2)]
-    for step, (axis, mine, bit) in enumerate(order):
-        axis = axis if step == 0 else 0
-        away = swap(choose(terms, 1 - mine, axis), "dp", bit)
-        terms = add_low(choose(terms, mine, axis), away)
-    total = choose(terms, z, 0).astype(jnp.float32)
-    for k in (1, 2, 3):
-        total = total + swap(choose(terms, z ^ k, 0), "mp", k).astype(jnp.float32)
-    return total
-
-
-def sum_all(value):
-    for axis, bit in (("dp", 1), ("dp", 2), ("dp", 4), ("mp", 1), ("mp", 2)):
-        value = value + swap(value, axis, bit)
-    return value
+    core = lax.rem(d, 2)
+    firsts, offsets, ends = window_plan(rows, parts)
+    offset = pl.multiple_of(pick(offsets, z), 16)
+    partner = (d ^ 1, z)
+    peers = [(d, z ^ k) for k in (1, 2, 3)] + [partner, (d ^ 2, z), (d ^ 4, z)]
+    barrier = pltpu.get_barrier_semaphore()
+    for peer in peers:
+        pl.semaphore_signal(barrier, inc=1, device_id=peer, device_id_type=MESH)
+    pl.semaphore_wait(barrier, len(peers))
+    clock = Clock()
+    tail = []
+
+    wide = 2 * rows
+    wd = arena.at[pl.ds(0, D), :]
+    wu = arena.at[pl.ds(D, D), :]
+
+    def fetch(index, source, target):
+        copy = pltpu.make_async_copy(source, target, local.at[index])
+        copy.start()
+        return copy
+
+    chunk = lambda k: z ^ k
+    hidden = lambda k: pl.ds(pl.multiple_of(chunk(k) * D, D), D)
+    load_wd = lambda i: fetch(0, f_down.at[chunk(RING[i])], wd)
+    load_wu = lambda i: fetch(1, f_up.at[chunk(RING[i])], wu)
+    load_act = lambda i: fetch(2, act2.at[:, hidden(RING[i])], act)
+    load_slope = lambda i: fetch(3, dgelu.at[:, hidden(RING[i])], slope)
+    at_wd, at_slope, at_act, at_wu = load_wd(0), load_slope(0), load_act(0), load_wu(0)
+    at_acc = fetch(4, second_grads, acc)
+    at_normed = fetch(5, normed_one, normed)
+    at_turned = fetch(6, first_t, turned)
+
+    zero = jnp.zeros((16, D), low)
+    for j in range(parts):
+        spans = []
+        if j == 0:
+            spans.append((0, offsets[0]))
+        begin = ends[j] if j < parts - 1 else offsets[j] + rows
+        if begin < window:
+            spans.append((begin, window))
+        if spans:
+            @pl.when(z == j)
+            def _(spans=spans):
+                for begin, end in spans:
+                    def clear(i, c):
+                        mixed_win[pl.ds(pl.multiple_of(begin + i * 16, 16), 16), :] = zero
+                        return c
+                    lax.fori_loop(0, (end - begin) // 16, clear, 0)
+
+    groups = {
+        "down": (s_down, k_down, r_down, t_down, z_down, g_down, 0),
+        "up": (s_up, k_up, r_up, t_up, z_up, g_up, 1),
+        "out": (s_out, k_out, r_out, t_out, z_out, g_out, 2),
+        "qkv": (s_qkv, k_qkv, r_qkv, t_qkv, z_qkv, g_qkv, 3),
+    }
+    hops = {}
+
+    def x_ahead(g, i):
+        return (i + groups[g][6]) % 2 == 0
+
+    def put(g, i, j, at, value):
+        if not x_ahead(g, i):
+            j = (0, 2, 1, 3)[j]
+        if j < 2:
+            groups[g][0][(i % 2, j) + at] = value
+        else:
+            groups[g][1][(i, j - 2) + at] = value
+
+    def hop(g, i, kind, source, target, device):
+        index = groups[g][6]
+        copy = pltpu.make_async_remote_copy(
+            source, target, hop_send.at[index, i, kind], hop_recv.at[index, i, kind],
+            device_id=device, device_id_type=MESH,
+        )
+        copy.start()
+        hops[g, i, kind] = copy
+
+    def add_into(ref, other):
+        count = ref.shape[0]
+        step = min(count, 64)
+
+        def body(j, c):
+            at = pl.ds(pl.multiple_of(j * step, step), step)
+            ref[at, :] = (ref[at, :].astype(f32) + other[at, :].astype(f32)).astype(low)
+            return c
+
+        lax.fori_loop(0, count // step, body, 0)
+
+    def launch(g, i):
+        s, kept, r, t, zb, out, index = groups[g]
+        x_first = x_ahead(g, i)
+        n1, n2 = ((d ^ 2, z), (d ^ 4, z)) if x_first else ((d ^ 4, z), (d ^ 2, z))
+        l1, l2 = ("x", "y") if x_first else ("y", "x")
+        block = s.shape[2] * s.shape[3] * 2
+        k = RING[i]
+        hop(g, i, 0, s.at[i % 2], r.at[i], n1)
+
+        def second():
+            hops[g, i, 0].wait_recv()
+            add_into(kept.at[i, 0], r.at[i, 0])
+            hop(g, i, 1, kept.at[i, 0], t.at[i], n2)
+            clock.send(l2, block, third)
+            add_into(kept.at[i, 1], r.at[i, 1])
+
+        def third():
+            hops[g, i, 1].wait_recv()
+            add_into(kept.at[i, 1], t.at[i])
+            if k:
+                hop(g, i, 2, kept.at[i, 1], zb.at[k - 1], (d, z ^ k))
+                clock.send("z", block, fourth, 1.0 if k == 1 else 2.0)
+
+        def fourth():
+            hops[g, i, 2].wait_recv()
+
+        clock.send(l1, 2 * block, second)
+
+    def free_slot(g, i):
+        if i >= 2:
+            hops[g, i - 2, 0].wait_send()
+
+    def finish(g):
+        s, kept, r, t, zb, out, index = groups[g]
+        own = RING.index(0)
+        count = s.shape[2]
+        step = min(count, 64)
+        pieces = kept.at[own, 1]
+
+        def body(j, c):
+            at = pl.ds(pl.multiple_of(j * step, step), step)
+            total = pieces[at, :].astype(f32)
+            for k in range(parts - 1):
+                total = total + zb[k, at, :].astype(f32)
+            out[at, :] = total
+            return c
+
+        lax.fori_loop(0, count // step, body, 0)
+
+    def exchange(index, source, target):
+        copy = pltpu.make_async_remote_copy(
+            source, target, pair_send.at[index], pair_recv.at[index], device_id=partner, device_id_type=MESH
+        )
+        copy.start()
+        return copy
+
+    small[...] = small_in[...]
+
+    pending = {}
+
+    def grad_up_chunk(i):
+        pending.pop(i).wait_recv()
+        if i == 0:
+            at_turned.wait()
+        free_slot("up", i)
+
+        def body(n, c):
+            at = pl.ds(pl.multiple_of(n * 256, 256), 256)
+            tile = jnp.dot(turned[...], up2[i, :, at], preferred_element_type=f32).astype(low)
+            for j in range(4):
+                put("up", i, j, (slice(None), at), tile[j * 128 : (j + 1) * 128])
+            return c
+
+        lax.fori_loop(0, 4, body, 0)
+        launch("up", i)
+        clock.work(2.0)
+
+    exchanges = []
+    loads = {"wd": at_wd, "wu": at_wu, "slope": at_slope, "act": at_act}
+
+    def upper_chunk(i):
+        loads["wd"].wait()
+        loads["slope"].wait()
+        bias_row = chunk(RING[i])
+
+        def body(n, c):
+            at = pl.ds(pl.multiple_of(n * 256, 256), 256)
+            grads = lax.dot_general(sec_low[...], wd[at, :], NT, preferred_element_type=f32)
+            value = (grads * slope[:, at].astype(f32)).astype(low)
+            up2[i, pl.ds(0, rows), at] = value
+            small[pl.ds(10 + bias_row, 1), at] = jnp.sum(value.astype(f32), axis=0, keepdims=True)
+            return c
+
+        lax.fori_loop(0, 4, body, 0)
+        pending[i] = exchange(i, up2.at[i, pl.ds(0, rows), :], up2.at[i, pl.ds(rows, rows), :])
+        exchanges.append(pending[i])
+        clock.work(2.5)
+        if i + 1 < parts:
+            loads["wd"], loads["slope"] = load_wd(i + 1), load_slope(i + 1)
+
+    def grad_down_chunk(i):
+        loads["act"].wait()
+        free_slot("down", i)
+
+        def body(n, c):
+            at = pl.ds(pl.multiple_of(n * 256, 256), 256)
+            tile = lax.dot_general(act[:, at], sec2[...], TN, preferred_element_type=f32).astype(low)
+            for j in range(4):
+                put("down", i, j, (at, slice(None)), tile[:, j * 128 : (j + 1) * 128])
+            return c
+
+        lax.fori_loop(0, 4, body, 0)
+        launch("down", i)
+        clock.work(2.0)
+        if i + 1 < parts:
+            loads["act"] = load_act(i + 1)
+
+    def first_chunk(i):
+        loads["wu"].wait()
+        if i == 0:
+            at_acc.wait()
+
+        def body(n, c):
+            at = pl.ds(pl.multiple_of(n * 256, 256), 256)
+            acc[:, at] += lax.dot_general(
+                up2[i, pl.ds(0, rows), :], wu[at, :], NT, preferred_element_type=f32
+            )
+            return c
+
+        lax.fori_loop(0, 4, body, 0)
+        clock.work(2.0)
+        if i + 1 < parts:
+            loads["wu"] = load_wu(i + 1)
+
+    grad_down_chunk(0)
+    for i in range(parts):
+        upper_chunk(i)
+        first_chunk(i)
+        if i == 1:
+            grad_down_chunk(1)
+
+    at_normed.wait()
+    zero_row = jnp.zeros((16, D), f32)
+
+    def norm_body(i, sums):
+        at = pl.ds(pl.multiple_of(i * 16, 16), 16)
+        grads, unit = acc[at, :], normed[at, :]
+        scaled = grads * gain[0:1, :]
+        result = inverse[at, :] * (
+            scaled
+            - jnp.mean(scaled, axis=-1, keepdims=True)
+            - unit * jnp.mean(scaled * unit, axis=-1, keepdims=True)
+        )
+        acc[at, :] = result
+        mixed_win[pl.ds(pl.multiple_of(offset + i * 16, 16), 16), :] = result.astype(low)
+        return (sums[0] + grads * unit, sums[1] + grads, sums[2] + result)
+
+    sums = lax.fori_loop(0, rows // 16, norm_body, (zero_row, zero_row, zero_row))
+    small[4:5, :] = jnp.sum(sums[0], axis=0, keepdims=True)
+    small[5:6, :] = jnp.sum(sums[1], axis=0, keepdims=True)
+    small[2:3, :] = jnp.sum(sums[2], axis=0, keepdims=True)
+    halos = []
+    for j in range(parts - 1):
+        count = ends[j] - offsets[j] - rows
+        halos.append((j + 1, j, pltpu.make_async_remote_copy(
+            mixed_win.at[pl.ds(offsets[j + 1], count), :],
+            mixed_win.at[pl.ds(offsets[j] + rows, count), :],
+            halo_send.at[0], halo_recv.at[0], device_id=(d, j), device_id_type=MESH,
+        )))
+    for j in range(1, parts):
+        halos.append((j - 1, j, pltpu.make_async_remote_copy(
+            mixed_win.at[pl.ds(offsets[j - 1] + rows - offsets[j], offsets[j]), :],
+            mixed_win.at[pl.ds(0, offsets[j]), :],
+            halo_send.at[1], halo_recv.at[1], device_id=(d, j), device_id_type=MESH,
+        )))
+    for sender, receiver, copy in halos:
+        @pl.when(z == sender)
+        def _(copy=copy):
+            copy.start()
+    clock.work(4.0)
+    for i in range(parts):
+        grad_up_chunk(i)
+        if i + 2 < parts:
+            grad_down_chunk(i + 2)
+    own_at = pl.ds(offset, rows)
+    for j, owner in enumerate(block_owners(d, 1 - core, True)):
+        stage[:, j * 128 : (j + 1) * 128] = mixed_win[own_at, pl.ds(pl.multiple_of(owner * 128, 128), 128)]
+    exchanges.append(exchange(parts, stage, mixed2.at[pl.ds(rows, rows), :]))
+    for j, owner in enumerate(block_owners(d, core, True)):
+        mixed2[pl.ds(0, rows), j * 128 : (j + 1) * 128] = mixed_win[
+            own_at, pl.ds(pl.multiple_of(owner * 128, 128), 128)
+        ]
+    clock.work(4.0)
+
+    cut = D // parts
+    three = 3 * cut
+    pairs = cut // (2 * HD)
+    x = arena
+    wo = slope.at[pl.ds(0, cut), :]
+    load_x = lambda i: fetch(0, qkv.at[chunk(RING[i])], arena.at[pl.ds(0, window), pl.ds(0, three)])
+    load_wo = lambda i: fetch(1, f_out.at[chunk(RING[i])], wo)
+    load_att = lambda i: fetch(
+        2, att2.at[:, pl.ds(pl.multiple_of(chunk(RING[i]) * cut, cut), cut)], act.at[:, pl.ds(0, cut)]
+    )
+    load_wi = lambda i: fetch(3, f_qkv.at[chunk(RING[i])], w_in)
+    at_turned = fetch(6, lift_t, turned)
+    at_x, at_wo, at_att, at_wi = load_x(0), load_wo(0), load_att(0), load_wi(0)
+    exchanges[-1].wait_recv()
+    scale = HD ** (-0.5)
+
+    def take_halo():
+        for sender, receiver, copy in halos:
+            @pl.when(z == receiver)
+            def _(copy=copy):
+                copy.wait_recv()
+
+    def grad_qkv_chunk(i):
+        pending.pop(i).wait_recv()
+        if i == 0:
+            at_turned.wait()
+        free_slot("qkv", i)
+
+        def body(n, c):
+            at = pl.ds(pl.multiple_of(n * 256, 256), 256)
+            tile = jnp.dot(turned[...], up2[i, :, at], preferred_element_type=f32).astype(low)
+            for j in range(4):
+                put("qkv", i, j, (slice(None), at), tile[j * 128 : (j + 1) * 128])
+            return c
+
+        lax.fori_loop(0, three // 256, body, 0)
+        launch("qkv", i)
+        clock.work(1.8)
+
+    for i in range(parts):
+        at_att.wait()
+        free_slot("out", i)
+        tile = lax.dot_general(act[:, 0:cut], mixed2[...], TN, preferred_element_type=f32).astype(low)
+        for j in range(4):
+            put("out", i, j, (slice(None), slice(None)), tile[:, j * 128 : (j + 1) * 128])
+        launch("out", i)
+        clock.work(0.8)
+        if i == 0:
+            take_halo()
+        at_wo.wait()
+        at_x.wait()
+
+        def flow_body(n, c):
+            at = pl.ds(pl.multiple_of(n * 512, 512), 512)
+            x[at, three : three + cut] = lax.dot_general(
+                mixed_win[at, :], wo[...], NT, preferred_element_type=f32
+            ).astype(low)
+            return c
+
+        lax.fori_loop(0, window // 512, flow_body, 0)
+        clock.work(1.2)
+        if i + 1 < parts:
+            at_wo, at_att = load_wo(i + 1), load_att(i + 1)
+
+        def attend_body(step, c):
+            p, slot = step // 3, lax.rem(step, 3)
+            lanes = lambda base: pl.ds(pl.multiple_of(base + p * 2 * HD, 2 * HD), 2 * HD)
+            unit_at = [
+                pl.ds(perm[slot * LONG + m] * UNIT, UNIT) for m in range(LONG)
+            ]
+            keys = jnp.concatenate([x[at, lanes(cut)] for at in unit_at], axis=0)
+            values = jnp.concatenate([x[at, lanes(2 * cut)] for at in unit_at], axis=0)
+            marks = jnp.concatenate([kf[at, :] for at in unit_at], axis=0)
+            wide_keys = jnp.concatenate([keys, marks], axis=1)
+            k_sum = jnp.zeros((LONG * UNIT, 2 * HD), f32)
+            v_sum = jnp.zeros((LONG * UNIT, 2 * HD), f32)
+            for m in range(LONG):
+                pair = two_heads(x[unit_at[m], lanes(0)])
+                grads = two_heads(x[unit_at[m], lanes(three)])
+                mark = qf[unit_at[m], :]
+                wide_pair = jnp.concatenate([pair, jnp.concatenate([mark, mark], axis=0)], axis=1)
+                scores = lax.dot_general(wide_keys, wide_pair, NT, preferred_element_type=f32) * scale
+                weights = jnp.exp(scores - jnp.max(scores, axis=0, keepdims=True))
+                chances = weights * (1.0 / jnp.sum(weights, axis=0, keepdims=True))
+                flow = lax.dot_general(values, grads, NT, preferred_element_type=f32)
+                inner = jnp.sum(chances * flow, axis=0, keepdims=True)
+                slopes = (chances * (flow - inner)).astype(low)
+                v_sum = v_sum + jnp.dot(chances.astype(low), grads, preferred_element_type=f32)
+                k_sum = k_sum + jnp.dot(slopes, pair, preferred_element_type=f32)
+                flipped = lax.dot_general(keys, slopes, TN, preferred_element_type=f32)
+                at = pl.ds(pl.multiple_of(slot * LONG * UNIT + m * UNIT, UNIT), UNIT)
+                y[at, lanes(0)] = (from_two(flipped) * scale).astype(low)
+            at = pl.ds(pl.multiple_of(slot * LONG * UNIT, UNIT), LONG * UNIT)
+            y[at, lanes(cut)] = (k_sum * scale).astype(low)
+            y[at, lanes(2 * cut)] = v_sum.astype(low)
+            return c
+
+        lax.fori_loop(0, pairs * 3, attend_body, 0)
+        clock.work(9.0)
+        if i + 1 < parts:
+            at_x = load_x(i + 1)
+        for u in range(FIRST_OWN, LAST_OWN + 1):
+            at = pl.ds(back[u] * UNIT, UNIT)
+            act[pl.ds((u - FIRST_OWN) * UNIT, UNIT), cut:] = y[at, :]
+        exchanges[i].wait_send()
+        inner_at = pl.ds(pl.multiple_of(offset - FIRST_OWN * UNIT, 16), rows)
+        up2[i, pl.ds(0, rows), 0:three] = act[inner_at, cut:]
+        pending[i] = exchange(
+            parts + 1 + i, up2.at[i, pl.ds(0, rows), pl.ds(0, three)], up2.at[i, pl.ds(rows, rows), pl.ds(0, three)]
+        )
+        exchanges.append(pending[i])
+        place = pl.multiple_of(chunk(RING[i]) * cut, cut)
+        small[8:9, pl.ds(place, cut)] = jnp.sum(up2[i, pl.ds(0, rows), 0:cut].astype(f32), axis=0, keepdims=True)
+        small[9:10, pl.ds(place, cut)] = jnp.sum(
+            up2[i, pl.ds(0, rows), 2 * cut : three].astype(f32), axis=0, keepdims=True
+        )
+        at_wi.wait()
+
+        def input_body(n, c, i=i):
+            at = pl.ds(pl.multiple_of(n * 256, 256), 256)
+            acc[:, at] += lax.dot_general(
+                up2[i, pl.ds(0, rows), 0:three], w_in[at, :], NT, preferred_element_type=f32
+            )
+            return c
+
+        lax.fori_loop(0, 4, input_body, 0)
+        clock.work(2.0)
+        if i + 1 < parts:
+            at_wi = load_wi(i + 1)
+        grad_qkv_chunk(i)
+
+    def last_body(i, total):
+        at = pl.ds(pl.multiple_of(i * 16, 16), 16)
+        value = acc[at, :]
+        arena[at, :] = value.astype(low)
+        return total + value
+
+    total = jnp.sum(lax.fori_loop(0, rows // 16, last_body, zero_row), axis=0, keepdims=True)
+    store = fetch(4, arena.at[pl.ds(0, rows), :], input_grad)
+    small[0:1, :] = total * small_in[15:16, :]
+    small[1:2, :] = total
+    clock.work(2.0)
+    small_copies = []
+
+    def small_step(n):
+        copy = pltpu.make_async_remote_copy(
+            small, small_in_far.at[n], small_send.at[n], small_recv.at[n],
+            device_id=[partner, (d ^ 2, z), (d ^ 4, z), (d, z ^ 1), (d, z ^ 2)][n], device_id_type=MESH,
+        )
+        copy.start()
+
+        def take():
+            copy.wait()
+            small[...] += small_in_far[n]
+            if n < 4:
+                small_step(n + 1)
+
+        clock.send("c", 0.4e6, take)
+
+    small_step(0)
+    clock.drain()
+    for g in groups:
+        finish(g)
+    small_out[...] = small[...]
+    store.wait()
+    for (g, i, kind), copy in hops.items():
+        if kind or i >= 2:
+            copy.wait_send()
+    for copy in exchanges[parts:]:
+        copy.wait_send()
+    for sender, receiver, copy in halos:
+        @pl.when(z == sender)
+        def _(copy=copy):
+            copy.wait_send()
+
+
+def back_call(rows, window, parts, perm, back, vmem_in, hbm_in):
+    f32, low = jnp.float32, jnp.bfloat16
+    any_ = pl.BlockSpec(memory_space=pl.ANY)
+    vmem = pl.BlockSpec(memory_space=pltpu.VMEM)
+    smem = pl.BlockSpec(memory_space=pltpu.SMEM)
+    cut = D // parts
+    shapes = {"down": (D, 128), "up": (128, D), "out": (cut, 128), "qkv": (128, 3 * cut)}
+    outs = [jax.ShapeDtypeStruct((rows, D), low)]
+    outs += [jax.ShapeDtypeStruct(shape, f32) for shape in (shapes["qkv"], shapes["out"], shapes["up"], shapes["down"])]
+    outs += [jax.ShapeDtypeStruct((16, D), f32)]
+    order = ("down", "up", "out", "qkv")
+    buffers = [pltpu.VMEM((2, 2) + shapes[g], low) for g in order]
+    buffers += [pltpu.VMEM((parts, 2) + shapes[g], low) for g in order]
+    buffers += [pltpu.VMEM((parts, 2) + shapes[g], low) for g in order]
+    buffers += [pltpu.VMEM((parts,) + shapes[g], low) for g in order]
+    buffers += [pltpu.VMEM((parts - 1,) + shapes[g], low) for g in order]
+    dma = pltpu.SemaphoreType.DMA
+    return pl.pallas_call(
+        functools.partial(back_kernel, rows, window, parts),
+        out_shape=outs,
+        in_specs=[smem, smem] + [vmem] * len(vmem_in) + [any_] * len(hbm_in),
+        out_specs=[any_] + [vmem] * 5,
+        scratch_shapes=[
+            pltpu.VMEM((rows, D), f32),
+            pltpu.VMEM((rows, D), f32),
+            pltpu.VMEM((512, 2 * rows), low),
+            pltpu.VMEM((2 * D, D), low),
+            pltpu.VMEM((2 * rows, D), low),
+            pltpu.VMEM((rows, D), low),
+            pltpu.VMEM((window, 3 * cut), low),
+            pltpu.VMEM((parts, 2 * rows, D), low),
+            pltpu.VMEM((D, 3 * cut), low),
+            pltpu.VMEM((2 * rows, 512), low),
+            pltpu.VMEM((rows, 512), low),
+            pltpu.VMEM((window, D), low),
+            pltpu.VMEM((16, D), f32),
+            pltpu.VMEM((5, 16, D), f32),
+        ]
+        + buffers
+        + [
+            dma((7,)),
+            dma((4, parts, 3)),
+            dma((4, parts, 3)),
+            dma((2 * parts + 1,)),
+            dma((2 * parts + 1,)),
+            dma((2,)),
+            dma((2,)),
+            dma((5,)),
+            dma((5,)),
+        ],
+        compiler_params=pltpu.CompilerParams(
+            collective_id=1, has_side_effects=True, vmem_limit_bytes=60 * 2**20
+        ),
+    )(perm, back, *vmem_in, *hbm_in)
+
+
+def unit_order(segs, window):
+    units = window // UNIT
+    unit_seg = segs[::UNIT]
+    index = lax.iota(jnp.int32, units)
+    counts = jnp.sum((unit_seg[:, None] == unit_seg[None, :]).astype(jnp.int32), axis=1)
+    short = jnp.where((counts == LONG) & (unit_seg >= 0) & (unit_seg < 1000), 0, 1) * units + index
+    back = jnp.sum((short[None, :] < short[:, None]).astype(jnp.int32), axis=1)
+    perm = jnp.sum(jnp.where(back[None, :] == index[:, None], index[None, :], 0), axis=1)
+    return perm.astype(jnp.int32), back.astype(jnp.int32)
+
+
+def marks_of(segs):
+    lane = lax.iota(jnp.int32, 2 * HD)
+    seg = jnp.where(segs < 0, 2 * HD - 1, jnp.where(segs >= 1000, 2 * HD - 2, segs))
+    same = seg[:, None] == lane[None, :]
+    keys = jnp.where(same, 1.0, 0.0).astype(jnp.bfloat16)
+    queries = jnp.where(same, 0.0, -8e30).astype(jnp.bfloat16)
+    return keys, queries
 
 
 def local_body(
@@ -684,12 +1196,15 @@
     rows = tokens.shape[0]
     parts = lax.axis_size("mp")
     z = lax.axis_index("mp")
+    d = lax.axis_index("dp")
+    core = lax.rem(d, 2)
     low = jnp.bfloat16
     f32 = jnp.float32
+    cut = D // parts
     firsts, offsets, ends = window_plan(rows, parts)
     window = -(-max(ends) // UNIT) * UNIT
     win, f_qkv, f_out, f_up, f_down = gather(
-        tokens, jnp.transpose(w_qkv, (1, 0, 2)), w_out, w_up, w_down, window, parts
+        tokens, w_qkv.reshape(D, 3 * cut), w_out, w_up, w_down, window, parts
     )
     bias_qv_all = lax.all_gather(bias_qv, "mp", axis=1, tiled=True).astype(f32)
     bias_up_all = lax.all_gather(bias_up, "mp", axis=0, tiled=True).astype(f32)
@@ -700,25 +1215,29 @@
     segs = jnp.sum((positions[:, None] >= lengths_end[None, :]).astype(jnp.int32), axis=1)
     segs = jnp.where(positions < 0, -1, jnp.where(positions >= LEN, 1000, segs))
     plan = unit_plan(segs, z, offsets, rows, window)
+    perm, back = unit_order(segs, window)
+    kf, qf = marks_of(segs)
     step_time = timesteps[0].astype(f32) * 0.001
 
     lifted = tokens.astype(f32) + step_time * vectors[0] + vectors[1]
     lifted_low = lifted.astype(low)
     win_low = (win.astype(f32) + step_time * vectors[0] + vectors[1]).astype(low)
-    w3 = jnp.transpose(f_qkv, (1, 2, 0, 3)).reshape(3, D, D)
-    queries = (jnp.dot(win_low, w3[0], preferred_element_type=f32) + bias_qv_all[0]).astype(low)
-    keys = jnp.dot(win_low, w3[1], preferred_element_type=f32).astype(low)
-    values = (jnp.dot(win_low, w3[2], preferred_element_type=f32) + bias_qv_all[1]).astype(low)
-    attended = attention_call(attend_kernel, window, plan, segs, (queries, keys, values), 1, 0)[0]
+    bias3 = jnp.stack([bias_qv_all[0], jnp.zeros((D,), f32), bias_qv_all[1]])
+    bias3 = jnp.transpose(bias3.reshape(3, parts, cut), (1, 0, 2)).reshape(parts, 1, 3 * cut)
+    qkv = (jnp.einsum("td,zde->zte", win_low, f_qkv, preferred_element_type=f32) + bias3).astype(low)
+    attended = attention_call(window, parts, plan, segs, qkv)
     attended = lax.dynamic_slice_in_dim(attended, offset, rows, 0)
     wo = f_out.reshape(D, D)
     mixed = jnp.dot(attended, wo, preferred_element_type=f32) + vectors[2]
     first, normed_one, inverse_one = norm_forward(lifted + mixed, vectors[4], vectors[5])
     first_low = first.astype(low)
-    wu = jnp.transpose(f_up, (1, 0, 2)).reshape(D, FF)
-    upper = jnp.dot(first_low, wu, preferred_element_type=f32) + bias_up_all
-    activated, gelu_pull = jax.vjp(gelu_exact, upper)
-    activated = activated.astype(low)
+    upper = jnp.concatenate(
+        [jnp.dot(first_low, f_up[j], preferred_element_type=f32) for j in range(parts)], axis=1
+    )
+    upper = upper + bias_up_all
+    chance = 0.5 * (1.0 + lax.erf(upper * (0.5**0.5)))
+    activated = (upper * chance).astype(low)
+    slope = (chance + upper * jnp.exp(-0.5 * upper * upper) * (0.5 / jnp.pi) ** 0.5).astype(low)
     wd = f_down.reshape(FF, D)
     down = jnp.dot(activated, wd, preferred_element_type=f32) + vectors[3]
     output, normed_two, inverse_two = norm_forward(first + down, vectors[6], vectors[7])
@@ -726,90 +1245,43 @@
     second_grads, gain_two, shift_two = norm_backward(out_grads, normed_two, inverse_two, vectors[6])
     second_low = second_grads.astype(low)
 
-    cut = D // lax.axis_size("dp")
-    fold = (rows, 2, 2, 2, cut)
-
-    def for_core(value, c):
-        return choose(value.reshape(fold), c, 3)
-
-    act4 = activated.reshape(rows, parts, FF // parts)
-    grad_down = scatter_sum(
-        lambda c: jnp.einsum("tzf,tyxk->yxzfk", act4, for_core(second_low, c), preferred_element_type=f32), True
-    )
-    act_grads = jnp.dot(second_low, wd.T, preferred_element_type=f32)
-    (upper_grads,) = gelu_pull(act_grads)
-    upper_low = upper_grads.astype(low)
-    grad_bias_up = jnp.sum(upper_low, axis=0, dtype=f32)
-    upper4 = upper_low.reshape(rows, parts, FF // parts)
-    grad_up = scatter_sum(
-        lambda c: jnp.einsum("tyxk,tzf->yxzkf", for_core(first_low, c), upper4, preferred_element_type=f32), False
-    )
-    first_grads = second_grads + jnp.dot(upper_low, wu.T, preferred_element_type=f32)
-    mixed_grads, gain_one, shift_one = norm_backward(first_grads, normed_one, inverse_one, vectors[4])
-    mixed_low = mixed_grads.astype(low)
-
-    most_left, most_right = max(offsets[1:]), max(e - o - rows for e, o in zip(ends[:-1], offsets[:-1]))
-    from_left = lax.ppermute(mixed_low[rows - most_left :], "mp", [(j, j + 1) for j in range(parts - 1)])
-    from_right = lax.ppermute(mixed_low[:most_right], "mp", [(j + 1, j) for j in range(parts - 1)])
-    tail = jnp.zeros((window - offsets[0] - rows, D), low)
-    joined = jnp.concatenate([from_left, mixed_low, from_right, tail], axis=0)
-    mixed_win = lax.dynamic_slice_in_dim(joined, most_left - offset, window, 0)
-
-    att4 = attended.reshape(rows, parts, D // parts)
-    grad_out = scatter_sum(
-        lambda c: jnp.einsum("tze,tyxk->yxzek", att4, for_core(mixed_low, c), preferred_element_type=f32), True
-    )
-    attended_grads = jnp.dot(mixed_win, wo.T, preferred_element_type=f32).astype(low)
-    dq, dk, dv = attention_call(
-        attend_back_kernel, window, plan, segs, (queries, keys, values, attended_grads), 3, 2
-    )
-    dq, dk, dv = (lax.dynamic_slice_in_dim(value, offset, rows, 0) for value in (dq, dk, dv))
-    grad_bias_qv = jnp.stack([jnp.sum(dq, axis=0, dtype=f32), jnp.sum(dv, axis=0, dtype=f32)])
-    input_sum = (
-        mixed_grads
-        + jnp.dot(dq, w3[0].T, preferred_element_type=f32)
-        + jnp.dot(dk, w3[1].T, preferred_element_type=f32)
-        + jnp.dot(dv, w3[2].T, preferred_element_type=f32)
-    )
-
-    def qkv_terms(value):
-        value4 = value.reshape(rows, parts, D // parts)
-        return lambda c: jnp.einsum("tyxk,tzf->yxzkf", for_core(lifted_low, c), value4, preferred_element_type=f32)
-
-    grad_q = scatter_sum(qkv_terms(dq), True)
-    grad_k = scatter_sum(qkv_terms(dk), False)
-    grad_v = scatter_sum(qkv_terms(dv), False)
-    grad_qkv = jnp.stack([grad_q, grad_k, grad_v], axis=1)
-    input_total = jnp.sum(input_sum, axis=0)
-    rows8 = jnp.stack(
-        [
-            step_time * input_total,
-            input_total,
-            jnp.sum(mixed_grads, axis=0),
-            jnp.sum(second_grads, axis=0),
-            gain_one,
-            shift_one,
-            gain_two,
-            shift_two,
-        ],
-        axis=0,
-    )
-    small = sum_all(
-        jnp.concatenate([rows8, grad_bias_qv, grad_bias_up.reshape(FF // D, D)], axis=0)
-    )
-    grad_vectors = small[:8]
-    grad_bias_qv = lax.dynamic_slice_in_dim(small[8:10], z * (D // parts), D // parts, 1)
-    grad_bias_up = lax.dynamic_slice_in_dim(small[10:].reshape(FF), z * (FF // parts), FF // parts, 0)
+    def arranged(value, c):
+        return jnp.concatenate(
+            [lax.dynamic_slice_in_dim(value, owner * 128, 128, 1) for owner in block_owners(d, c, True)], axis=1
+        )
+
+    def both(mine, sent):
+        return jnp.concatenate([mine, swap(sent, "dp", 1)], axis=0)
+
+    sec2 = both(arranged(second_low, core), arranged(second_low, 1 - core))
+    first_t = both(arranged(first_low, core), arranged(first_low, 1 - core)).T
+    lift_t = both(arranged(lifted_low, core), arranged(lifted_low, 1 - core)).T
+    act2 = both(activated, activated)
+    att2 = both(attended, attended)
+    zero_row = jnp.zeros((D,), f32)
+    small_in = jnp.stack(
+        [zero_row] * 3
+        + [jnp.sum(second_grads, axis=0), zero_row, zero_row, gain_two, shift_two]
+        + [zero_row] * 7
+        + [jnp.broadcast_to(step_time, (D,))]
+    )
+    input_grad, grad_qkv, grad_out, grad_up, grad_down, small = back_call(
+        rows, window, parts, perm, back,
+        (second_low, sec2, inverse_one, vectors[4:5], small_in, kf, qf),
+        (first_t, lift_t, second_grads, normed_one, act2, slope, att2, qkv, f_qkv, f_out, f_up, f_down),
+    )
+    grad_bias_qv = lax.dynamic_slice_in_dim(small[8:10], z * cut, cut, 1)
+    grad_bias_up = lax.dynamic_slice_in_dim(small[10:14].reshape(FF), z * (FF // parts), FF // parts, 0)
     return (
         output.astype(low),
-        input_sum.astype(low),
-        grad_qkv,
+        input_grad,
+        grad_qkv.reshape(-1, 3, cut),
         grad_bias_qv,
         grad_out,
         grad_up,
         grad_bias_up,
         grad_down,
-        grad_vectors,
+        small[:8],
     )
 
 

time: 877 us -> 486 us (0.55)
  matrix products: 160 us -> 30 us
  waiting for transfers between devices: 104 us -> 0.01 us
  starting transfers between devices: 108 us -> 4.95 us
  local copies, waits for them, and re-layouts: 103 us -> 30.2 us
  other arithmetic: 22.3 us -> 34.2 us
    pallas_call x1, Pallas kernels: 265 us -> 120 us  [gather(): pl.pallas_call(functools.partial(gather_kernel, rows, window, parts), out...]
    pallas_call x2, Pallas kernels: 86.3 us -> 230 us  [the longest x1 197 us: back_call(): pl.pallas_call(functools.partial(back_kernel, rows, window, parts), out_s...]
    dot_general x22 -> x5, matrix products: 148 us -> 17.7 us  [the longest x1 11.9 us: local_body(): jnp.einsum('td,zde->zte', win_low, f_qkv, preferred_element_type=f32)]
    ppermute x41 -> x5, waiting for transfers between devices: 104 us -> 0.01 us  [swap(): return lax.ppermute(array, axis, [(i, i ^ bit) for i in range(size)])]
    ppermute x41 -> x5, starting transfers between devices: 102 us -> 4.95 us  [swap(): return lax.ppermute(array, axis, [(i, i ^ bit) for i in range(size)])]
    reshape x11 -> x2, local copies, waits for them, and re-layouts: 41.4 us -> 1.86 us  [the longest x1 1.84 us: local_body(): w_qkv.reshape(D, 3 * cut)]
    dynamic_slice x7 -> x4, local copies, waits for them, and re-layouts: 19.7 us -> 4.06 us  [the longest x2 2.88 us: arranged(): lax.dynamic_slice_in_dim(value, owner * 128, 128, 1)]
    slice x9 -> x3, local copies, waits for them, and re-layouts: 17.7 us -> 2.14 us  [the longest x1 1.37 us: local_body(): small[:8]]
  transfers between devices with their start and end apart: 43 -> 5, of which waited for: 15 -> 0; matrix products, arithmetic and copies ran while one was open for 18% -> 11% of each run, Pallas kernels for 6% -> 0%
where the time goes in v2:
time: 486 us; the launch traced here: 477 us
  Pallas kernels  351 us (72%)
  other arithmetic  34.2 us (7%)
  local copies, waits for them, and re-layouts  30.2 us (6%)
  matrix products  30 us (6%)
  blocking collectives  24.7 us (5%)
  starting transfers between devices  4.95 us (1%)
    pallas_call x1, Pallas kernels, back_call(): pl.pallas_call(functools.partial(back_kernel, rows, window, parts), out_s...  197 us
    pallas_call x1, Pallas kernels, gather(): pl.pallas_call(functools.partial(gather_kernel, rows, window, parts), out...  120 us
    pallas_call x1, Pallas kernels, attention_call(): pl.pallas_call(attend_kernel, grid_spec=pltpu.PrefetchScalarGridSpec(num_...  32.8 us
    unnamed x54, local copies, waits for them, and re-layouts  13.9 us
    concatenate x3, other arithmetic, both(): return jnp.concatenate([mine, swap(sent, 'dp', 1)], axis=0)  13.4 us
    all_gather x1, blocking collectives, local_body(): bias_qv_all = lax.all_gather(bias_qv, 'mp', axis=1, tiled=True).astype(f32)  12.6 us
    all_gather x1, blocking collectives, local_body(): bias_up_all = lax.all_gather(bias_up, 'mp', axis=0, tiled=True).astype(f32)  12.1 us
    dot_general x1, matrix products, local_body(): jnp.einsum('td,zde->zte', win_low, f_qkv, preferred_element_type=f32)  11.9 us
  transfers between devices with their start and end apart: 5, of which 0 were waited for; matrix products, arithmetic and copies ran while one was open for 11% of the time, Pallas kernels for 0%

profile of v2, /device:TPU:0, one launch (start us, length us, event | category | flops | bytes accessed | tf_op | source)
XLA Modules:
  0.0 476.5 jit_solution(850935491958775459)
XLA Ops:
  0.7 0.7 copy.49
  1.7 1.2 fusion.31.seg
  4.0 2.6 copy.51
  6.6 1.8 copy.52.w_qkv
  8.5 12.6 %all_gather.6 = bf16[2,1024]{1,0:T(2,128)(2,1)S(1)} all-gather(bf16[2,256]{1,0:T(2,128)(2,1)S(1)} %copy-done.19), channel_id=1, replica_groups=mesh['dp'=8,'mp'=4] {'mp'}, dimensions={1}, use_global_device_ids=true | all-gather | bytes 5120 | tf_op jit(solution)/shard_map/all_gather | solution.py:1209
  21.3 1.6 copy-done.3
  22.9 1.6 copy-done.4
  24.5 120.3 %shard_map.178 = (bf16[1536,1024]{1,0:T(8,128)(2,1)S(1)}, bf16[4,1024,768]{2,1,0:T(8,128)(2,1)S(1)}, bf16[4,256,1024]{2,1,0:T(8,128)(2,1)S(1)}, bf16[4,1024,1024]{2,1,0:T(8,128)(2,1)}, bf16[4,1024,1024]{2,1,0:T(8,128)(2,1)}) custom-call(bf16[592,1024]{1,0:T(8,128)(2,1)S(1)} %copy-done.1, bf16[1024,768]{1,0:T(8,128)(2,1)S(1)} %copy.52.w_qkv, ...), custom_call_target="tpu_custom_call" | custom-call | tf_op jit(solution)/shard_map/pallas_call | solution.py:485
  144.8 11.9 %fusion.5.q.k.v.qkv = bf16[4,1536,768]{2,1,0:T(8,128)(2,1)} fusion(f32[4,768]{1,0:T(4,128)S(1)} %bitcast.78, bf16[4,1024,768]{2,1,0:T(8,128)(2,1)S(1)} %get-tuple-element.20.f_qkv, bf16[1536,1024]{1,0:T(8,128)(2,1)S(1)} %get-tuple-element.21, f32[1024]{0:T(1024)S(1)} %bitcast.69, f32[1024]{0:T(1024)S(1)} %bitcast.72), kind=kOutput, calls=%fused_computation.11 | convolution fusion | flops 9679405056 | bytes 18894848 | tf_op jit(solution)/shard_map/td,zde->zte/dot_general | solution.py:1227
  156.8 32.8 %shard_map.179 = bf16[1536,1024]{1,0:T(8,128)(2,1)S(1)} custom-call(s32[12]{0:T(128)S(1)} %select_select_fusion.1.kind, s32[12]{0:T(128)S(1)} %get-tuple-element.79.start, s32[12]{0:T(128)S(1)} %slice.61.unit_seg, s32[1536,1]{1,0:T(8,128)S(1)} %copy-done.2, bf16[4,1536,768]{2,1,0:T(8,128)(2,1)} %fusion.5.q.k.v.qkv, bf16[4,1536,768]{2,1,0:T(8,128)(2,1)} %fusion.5.q.k.v.qkv, ...), custom_call_target="tpu_custom_call" | custom-call | tf_op jit(solution)/shard_map/pallas_call | solution.py:562
  189.6 1.1 constant_dynamic-slice_fusion.25
  190.7 3.7 collective-permute-start.4
  194.4 3.0 fusion.41
  197.9 2.0 fusion.18
  199.8 1.4 fusion.25
  201.3 1.4 fusion.23
  202.7 1.4 fusion.21
  204.2 1.4 fusion.19
  205.7 12.1 %all_gather.7 = bf16[4096]{0:T(1024)(128)(2,1)S(1)} all-gather(bf16[1024]{0:T(1024)(128)(2,1)S(1)} %copy-done.18), channel_id=1, replica_groups=mesh['dp'=8,'mp'=4] {'mp'}, dimensions={0}, use_global_device_ids=true | all-gather | bytes 10240 | tf_op jit(solution)/shard_map/all_gather | solution.py:1210
  217.8 7.7 %fusion.4 = (bf16[592,4096]{1,0:T(8,128)(2,1)}, bf16[592,4096]{1,0:T(8,128)(2,1)}) fusion(f32[4096]{0:T(1024)S(1)} %convert_element_type.75, f32[592,1024]{1,0:T(8,128)S(1)} %fusion.19, f32[592,1024]{1,0:T(8,128)S(1)} %fusion.21, f32[592,1024]{1,0:T(8,128)S(1)} %fusion.23, f32[592,1024]{1,0:T(8,128)S(1)} %fusion.25), kind=kLoop, calls=%fused_computation.6 | loop fusion | flops 36372480 | bytes 19415040 | tf_op jit(solution)/shard_map/convert_element_type | solution.py:1240
  225.9 2.5 constant_dynamic-slice_fusion.8
  229.3 0.9 copy-done.9
  230.1 9.3 %fusion.42 = (f32[592]{0:T(1024)S(1)}, f32[592,1024]{1,0:T(8,128)S(1)}) fusion(f32[1024]{0:T(1024)S(1)} %bitcast.79, bf16[592,4096]{1,0:T(8,128)(2,1)} %get-tuple-element.82, bf16[4096,1024]{1,0:T(8,128)(2,1)} %bitcast.58, f32[1024]{0:T(1024)S(1)} %bitcast.68, f32[592,1024]{1,0:T(8,128)S(1)} %copy-done.9, f32[1024]{0:T(1024)S(1)} %bitcast.62), kind=kOutput, calls=%fused_computation.123 | convolution fusion | flops 4969086464 | bytes 18102592 | tf_op jit(solution)/shard_map/dot_general | solution.py:1242
  239.8 0.9 copy-done.10
  240.7 1.1 fusion.16
  241.8 2.0 fusion.37
  244.3 0.9 copy-done.7
  246.2 1.1 select_convert_fusion
  247.6 0.6 select_reduce_fusion.perm
  248.2 0.9 rsqrt.16.inverse
  249.1 1.3 stack.23.small_in
  250.4 1.4 maximum_bitcast_fusion.1
  251.8 1.4 copy.57.lift_t
  253.2 1.2 maximum_bitcast_fusion
  254.5 1.5 copy.56.first_t
  255.9 2.2 pad_maximum_fusion.2.sec2
  258.1 3.4 pad_maximum_fusion.1.att2
  261.5 7.9 %pad_maximum_fusion.act2 = bf16[1184,4096]{1,0:T(8,128)(2,1)} fusion(bf16[592,4096]{1,0:T(8,128)(2,1)} %collective-permute-done.3, bf16[592,4096]{1,0:T(8,128)(2,1)} %get-tuple-element.82), kind=kLoop, calls=%fused_computation.8 | loop fusion | flops 19398656 | bytes 19398656 | tf_op jit(solution)/shard_map/concatenate | solution.py:1254
  269.4 197.4 %shard_map.180 = (bf16[592,1024]{1,0:T(8,128)(2,1)}, f32[128,768]{1,0:T(8,128)}, f32[256,128]{1,0:T(8,128)}, f32[128,1024]{1,0:T(8,128)}, f32[1024,128]{1,0:T(8,128)}, /*index=5*/f32[16,1024]{1,0:T(8,128)}) custom-call(s32[12]{0:T(128)} %select_reduce_fusion.perm, s32[12]{0:T(128)} %copy-done.20, bf16[592,1024]{1,0:T(8,128)(2,1)} %copy-done.8, ...), custom_call_target="tpu_custom_call" | custom-call | tf_op jit(solution)/shard_map/pallas_call | solution.py:1124
  466.8 0.9 slice_bitcast_fusion
  467.7 1.4 slice.76
  469.1 0.8 slice.74
  469.8 1.1 copy.58
  471.0 0.9 copy.59
  473.1 1.0 copy.70
  474.1 0.7 copy.71
  474.8 0.8 copy.72
  475.6 0.8 copy.73
  (88 shorter events, 5.7 us)
Async XLA Ops:
  4.0 4.5 copy-start.19
  4.0 17.2 %copy-start.17 = (f32[8,1024]{1,0:T(8,128)S(1)}, f32[8,1024]{1,0:T(8,128)}, u32[]{:S(2)}) copy-start(f32[8,1024]{1,0:T(8,128)} %param.21) | copy-start | bytes 98308
  6.6 14.6 %copy-start.1 = (bf16[592,1024]{1,0:T(8,128)(2,1)S(1)}, bf16[592,1024]{1,0:T(8,128)(2,1)}, u32[]{:S(2)}) copy-start(bf16[592,1024]{1,0:T(8,128)(2,1)} %tokens.1) | copy-start | bytes 3637252
  6.6 14.6 %copy-start.6 = (bf16[256,1024]{1,0:T(8,128)(2,1)S(1)}, bf16[256,1024]{1,0:T(8,128)(2,1)}, u32[]{:S(2)}) copy-start(bf16[256,1024]{1,0:T(8,128)(2,1)} %w_out.1) | copy-start | bytes 1572868
  21.2 208.0 %copy-start.16 = (f32[1,1024]{1,0:T(1,128)}, f32[1,1024]{1,0:T(1,128)S(1)}, u32[]{:S(2)}) copy-start(f32[1,1024]{1,0:T(1,128)S(1)} %get-tuple-element.111.gain) | copy-start | bytes 12292
  21.3 1.6 copy-start.3
  22.9 1.6 copy-start.4
  144.8 12.0 %copy-start = (bf16[4,1024,768]{2,1,0:T(8,128)(2,1)}, bf16[4,1024,768]{2,1,0:T(8,128)(2,1)S(1)}, u32[]{:S(2)}) copy-start(bf16[4,1024,768]{2,1,0:T(8,128)(2,1)S(1)} %get-tuple-element.20.f_qkv) | copy-start | bytes 18874372
  144.8 49.6 %copy-start.5 = (bf16[4,256,1024]{2,1,0:T(8,128)(2,1)}, bf16[4,256,1024]{2,1,0:T(8,128)(2,1)S(1)}, u32[]{:S(2)}) copy-start(bf16[4,256,1024]{2,1,0:T(8,128)(2,1)S(1)} %get-tuple-element.22.f_out) | copy-start | bytes 6291460
  144.8 12.0 %copy-start.2 = (s32[1536,1]{1,0:T(8,128)S(1)}, s32[1536,1]{1,0:T(8,128)}, u32[]{:S(2)}) copy-start(s32[1536,1]{1,0:T(8,128)} %fusion.31.seg) | copy-start | bytes 18436
  189.6 10.3 %slice-start = ((s8[8388608]{0:T(1024)(128)(4,1)}), s8[4194304]{0:T(1024)(128)(4,1)S(1)}, s32[]{:S(2)}) async-start(s8[8388608]{0:T(1024)(128)(4,1)} %bitcast.56), calls=%async_computation | async-start | bytes 8388608
  190.7 67.4 %collective-permute-start.4 = (bf16[592,1024]{1,0:T(8,128)(2,1)}, bf16[592,1024]{1,0:T(8,128)(2,1)}, u32[]{:S(2)}, u32[]{:S(2)}) collective-permute-start(bf16[592,1024]{1,0:T(8,128)(2,1)} %constant_dynamic-slice_fusion.25), channel_id=1, source_target_pairs={{0,4},{4,0},{8,12},{12,8},{16,20},{20,16},{24,28},{28,24},{1,5},{5... | collective-permute-start | bytes 3637256 | tf_op jit(solution)/shard_map/ppermute | solution.py:597
  194.4 5.4 %slice-start.1 = ((s8[8388608]{0:T(1024)(128)(4,1)}), s8[4194304]{0:T(1024)(128)(4,1)S(1)}, s32[]{:S(2)}) async-start(s8[8388608]{0:T(1024)(128)(4,1)} %bitcast.56), calls=%async_computation.1 | async-start | bytes 8388608
  199.8 4.4 copy-start.11
  204.2 1.5 copy-start.18
  225.5 36.0 %collective-permute-start.3 = (bf16[592,4096]{1,0:T(8,128)(2,1)}, bf16[592,4096]{1,0:T(8,128)(2,1)}, u32[]{:S(2)}, u32[]{:S(2)}) collective-permute-start(bf16[592,4096]{1,0:T(8,128)(2,1)} %get-tuple-element.82), channel_id=1, source_target_pairs={{0,4},{4,0},{8,12},{12,8},{16,20},{20,16},{24,28},{28,24},{1,5},{5... | collective-permute-start | bytes 14549000 | tf_op jit(solution)/shard_map/ppermute | solution.py:597
  228.4 1.7 copy-start.9
  228.5 21.8 %collective-permute-start.2 = (bf16[592,512]{1,0:T(8,128)(2,1)S(1)}, bf16[592,512]{1,0:T(8,128)(2,1)}, u32[]{:S(2)}, u32[]{:S(2)}) collective-permute-start(bf16[592,512]{1,0:T(8,128)(2,1)S(1)} %pad_maximum_fusion.5), channel_id=1, source_target_pairs={{0,4},{4,0},{8,12},{12,8},{16,20},{20,16},{24,28},{28,24},{1,5},{5... | collective-permute-start | bytes 1818632 | tf_op jit(solution)/shard_map/ppermute | solution.py:597
  229.2 24.1 %collective-permute-start.1 = (bf16[592,512]{1,0:T(8,128)(2,1)S(1)}, bf16[592,512]{1,0:T(8,128)(2,1)}, u32[]{:S(2)}, u32[]{:S(2)}) collective-permute-start(bf16[592,512]{1,0:T(8,128)(2,1)S(1)} %pad_maximum_fusion.4), channel_id=1, source_target_pairs={{0,4},{4,0},{8,12},{12,8},{16,20},{20,16},{24,28},{28,24},{1,5},{5... | collective-permute-start | bytes 1818632 | tf_op jit(solution)/shard_map/ppermute | solution.py:597
  239.4 1.3 copy-start.10
  243.8 1.5 copy-start.7
  244.0 1.6 copy-start.8
  245.7 10.2 %collective-permute-start = (bf16[592,512]{1,0:T(8,128)(2,1)S(1)}, bf16[592,512]{1,0:T(8,128)(2,1)}, u32[]{:S(2)}, u32[]{:S(2)}) collective-permute-start(bf16[592,512]{1,0:T(8,128)(2,1)S(1)} %pad_maximum_fusion.3), channel_id=1, source_target_pairs={{0,4},{4,0},{8,12},{12,8},{16,20},{20,16},{24,28},{28,24},{1,5},{5... | collective-permute-start | bytes 1818632 | tf_op jit(solution)/shard_map/ppermute | solution.py:597
  247.6 5.7 %copy-start.20 = (s32[12]{0:T(128)}, s32[12]{0:T(128)S(1)}, u32[]{:S(2)}) copy-start(s32[12]{0:T(128)S(1)} %convert_reduce_fusion.2.back) | copy-start | bytes 148
  466.8 6.3 %copy-start.12 = (bf16[592,1024]{1,0:T(8,128)(2,1)S(1)}, bf16[592,1024]{1,0:T(8,128)(2,1)}, u32[]{:S(2)}) copy-start(bf16[592,1024]{1,0:T(8,128)(2,1)} %get-tuple-element.145) | copy-start | bytes 3637252
  466.8 7.3 %copy-start.15 = (f32[256,128]{1,0:T(8,128)S(1)}, f32[256,128]{1,0:T(8,128)}, u32[]{:S(2)}) copy-start(f32[256,128]{1,0:T(8,128)} %get-tuple-element.148) | copy-start | bytes 393220
  466.8 8.0 %copy-start.14 = (f32[128,1024]{1,0:T(8,128)S(1)}, f32[128,1024]{1,0:T(8,128)}, u32[]{:S(2)}) copy-start(f32[128,1024]{1,0:T(8,128)} %get-tuple-element.149) | copy-start | bytes 1572868
  471.0 4.6 copy-start.13

commit v3 on v2

--- a/solution.py
+++ b/solution.py
@@ -310,200 +310,6 @@
     return value
 
 
-def gather_kernel(
-    rows, window, parts, tokens, w_qkv, w_out, w_up, w_down, win, f_qkv, f_out, f_up, f_down, send, recv, near, far, own
-):
-    d = lax.axis_index("dp")
-    z = lax.axis_index("mp")
-    firsts, offsets, ends = window_plan(rows, parts)
-    shards = (w_qkv, w_out, w_up, w_down)
-    fulls = (f_qkv, f_out, f_up, f_down)
-    sizes = (128, 32, 128, 128)
-    others = (1, 3, 2)
-    peers = [(d, z ^ k) for k in others] + [(d ^ 1, z), (d ^ 2, z), (d ^ 4, z)]
-    barrier = pltpu.get_barrier_semaphore()
-    for peer in peers:
-        pl.semaphore_signal(barrier, inc=1, device_id=peer, device_id_type=MESH)
-    pl.semaphore_wait(barrier, len(peers))
-
-    def part(ref, index, owner, size, half=None):
-        start = owner * size
-        count = size
-        if half is not None:
-            count = size // 2
-            start = start + half * count
-        rows_at = pl.ds(pl.multiple_of(start, 16), count)
-        return ref.at[index, rows_at, :]
-
-    chunks = [(g, k) for g in range(4) for k in others]
-    copies = {}
-
-    def remote(i, kind, src, dst, target):
-        copy = pltpu.make_async_remote_copy(
-            src, dst, send.at[i, kind], recv.at[i, kind], device_id=target, device_id_type=MESH
-        )
-        copy.start()
-        copies[i, kind] = copy
-
-    def first_hop(i):
-        g, k = chunks[i]
-        size = sizes[g]
-        rows_at = pl.ds(pl.multiple_of(d * size, 16), size)
-        src = shards[g].at[rows_at, :]
-        remote(i, 0, src, part(fulls[g], z, d, size), (d, z ^ k))
-
-    def place(i, owner, half=None):
-        g, k = chunks[i]
-        return part(fulls[g], z ^ k, owner, sizes[g], half)
-
-    for i in range(3):
-        first_hop(i)
-    left_send = [
-        pltpu.make_async_remote_copy(
-            tokens.at[pl.ds(0, ends[j] - offsets[j] - rows), :],
-            win.at[pl.ds(offsets[j] + rows, ends[j] - offsets[j] - rows), :],
-            near.at[0], near.at[1], device_id=(d, j), device_id_type=MESH,
-        )
-        for j in range(parts - 1)
-    ]
-    right_send = [
-        pltpu.make_async_remote_copy(
-            tokens.at[pl.ds(rows - offsets[j], offsets[j]), :],
-            win.at[pl.ds(0, offsets[j]), :],
-            far.at[0], far.at[1], device_id=(d, j), device_id_type=MESH,
-        )
-        for j in range(1, parts)
-    ]
-    for j in range(parts - 1):
-        @pl.when(z == j + 1)
-        def _(j=j):
-            left_send[j].start()
-    for j in range(1, parts):
-        @pl.when(z == j - 1)
-        def _(j=j):
-            right_send[j - 1].start()
-    locals_ = []
-    for g in range(4):
-        copy = pltpu.make_async_copy(shards[g], fulls[g].at[z], own.at[g])
-        copy.start()
-        locals_.append(copy)
-    offset = pl.multiple_of(pick(offsets, z), 16)
-    copy = pltpu.make_async_copy(tokens, win.at[pl.ds(offset, rows), :], own.at[4])
-    copy.start()
-    locals_.append(copy)
-    fill_first = pltpu.make_async_copy(
-        tokens.at[pl.ds(0, offsets[0]), :], win.at[pl.ds(0, offsets[0]), :], own.at[5]
-    )
-    fills = []
-    for j in range(parts):
-        begin = ends[j] if j < parts - 1 else offsets[j] + rows
-        if begin < window:
-            fills.append(
-                (j, pltpu.make_async_copy(
-                    tokens.at[pl.ds(0, window - begin), :], win.at[pl.ds(begin, window - begin), :], own.at[6]
-                ))
-            )
-
-    @pl.when(z == 0)
-    def _():
-        fill_first.start()
-
-    for j, fill in fills:
-        @pl.when(z == j)
-        def _(fill=fill):
-            fill.start()
-
-
-    def stage_one(i):
-        copies[i, 0].wait_recv()
-        remote(i, 1, place(i, d), place(i, d), (d ^ 2, z))
-        remote(i, 2, place(i, d), place(i, d), (d ^ 4, z))
-        remote(i, 5, place(i, d), place(i, d), (d ^ 1, z))
-
-    def stage_two(i):
-        copies[i, 1].wait_recv()
-        remote(i, 3, place(i, d ^ 2, 0), place(i, d ^ 2, 0), (d ^ 4, z))
-        remote(i, 6, place(i, d ^ 2), place(i, d ^ 2), (d ^ 1, z))
-        copies[i, 2].wait_recv()
-        remote(i, 4, place(i, d ^ 4, 1), place(i, d ^ 4, 1), (d ^ 2, z))
-        remote(i, 7, place(i, d ^ 4), place(i, d ^ 4), (d ^ 1, z))
-
-    def stage_three(i):
-        copies[i, 3].wait_recv()
-        remote(i, 8, place(i, d ^ 6, 0), place(i, d ^ 6, 0), (d ^ 1, z))
-        copies[i, 4].wait_recv()
-        remote(i, 9, place(i, d ^ 6, 1), place(i, d ^ 6, 1), (d ^ 1, z))
-
-    n = len(chunks)
-    for i in range(n + 2):
-        if i < n:
-            stage_one(i)
-            if i + 3 < n:
-                first_hop(i + 3)
-        if 0 <= i - 1 < n:
-            stage_two(i - 1)
-        if 0 <= i - 2 < n:
-            stage_three(i - 2)
-    for i in range(n):
-        for kind in range(5, 10):
-            copies[i, kind].wait_recv()
-        for kind in range(10):
-            copies[i, kind].wait_send()
-    for j in range(parts - 1):
-        @pl.when(z == j + 1)
-        def _(j=j):
-            left_send[j].wait_send()
-
-        @pl.when(z == j)
-        def _(j=j):
-            left_send[j].wait_recv()
-    for j in range(1, parts):
-        @pl.when(z == j - 1)
-        def _(j=j):
-            right_send[j - 1].wait_send()
-
-        @pl.when(z == j)
-        def _(j=j):
-            right_send[j - 1].wait_recv()
-    for copy in locals_:
-        copy.wait()
-
-    @pl.when(z == 0)
-    def _():
-        fill_first.wait()
-
-    for j, fill in fills:
-        @pl.when(z == j)
-        def _(fill=fill):
-            fill.wait()
-
-
-def gather(tokens, w_qkv, w_out, w_up, w_down, window, parts):
-    rows = tokens.shape[0]
-    any_ = pl.BlockSpec(memory_space=pl.ANY)
-    low = jnp.bfloat16
-    return pl.pallas_call(
-        functools.partial(gather_kernel, rows, window, parts),
-        out_shape=[
-            jax.ShapeDtypeStruct((window, D), low),
-            jax.ShapeDtypeStruct((parts,) + w_qkv.shape, low),
-            jax.ShapeDtypeStruct((parts,) + w_out.shape, low),
-            jax.ShapeDtypeStruct((parts,) + w_up.shape, low),
-            jax.ShapeDtypeStruct((parts,) + w_down.shape, low),
-        ],
-        in_specs=[pl.BlockSpec(memory_space=pltpu.VMEM)] * 5,
-        out_specs=[any_] * 5,
-        scratch_shapes=[
-            pltpu.SemaphoreType.DMA((12, 10)),
-            pltpu.SemaphoreType.DMA((12, 10)),
-            pltpu.SemaphoreType.DMA((2,)),
-            pltpu.SemaphoreType.DMA((2,)),
-            pltpu.SemaphoreType.DMA((7,)),
-        ],
-        compiler_params=pltpu.CompilerParams(collective_id=0, has_side_effects=True, vmem_limit_bytes=32 * 2**20),
-    )(tokens, w_qkv, w_out, w_up, w_down)
-
-
 NT = (((1,), (1,)), ((), ()))
 TN = (((0,), (0,)), ((), ()))
 FIRST_OWN, LAST_OWN = LONG - 1, LONG + 4
@@ -520,81 +326,6 @@
 def from_two(flipped):
     both = jnp.concatenate([flipped[:HD, :UNIT], flipped[HD:, UNIT:]], axis=0)
     return both.T
-
-
-def weights_of(keys, pair, valid):
-    scores = lax.dot_general(keys, pair, NT, preferred_element_type=jnp.float32) * HD ** (-0.5)
-    if valid is not None:
-        scores = jnp.where(valid, scores, -1e30)
-    highest = jnp.max(scores, axis=0, keepdims=True)
-    weights = jnp.exp(scores - highest)
-    return weights * (1.0 / jnp.sum(weights, axis=0, keepdims=True))
-
-
-def attend_kernel(kind, start, unit_seg, seg, q, k, v, o):
-    def unit(u, carry):
-        mine = pl.ds(pl.multiple_of(u * UNIT, UNIT), UNIT)
-
-        def run(at, valid):
-            pair = two_heads(q[mine, :])
-            chances = weights_of(k[at, :], pair, valid).astype(jnp.bfloat16)
-            flipped = lax.dot_general(v[at, :], chances, TN, preferred_element_type=jnp.float32)
-            o[mine, :] = from_two(flipped).astype(o.dtype)
-
-        @pl.when(kind[u] == 2)
-        def _():
-            run(pl.ds(pl.multiple_of(start[u], UNIT), LONG * UNIT), None)
-
-        @pl.when(kind[u] == 1)
-        def _():
-            run(mine, seg[mine, :] == unit_seg[u])
-
-        return carry
-
-    lax.fori_loop(FIRST_OWN, LAST_OWN + 1, unit, 0)
-
-
-def attention_call(window, parts, plan, segs, qkv):
-    cut = D // parts
-    pairs = cut // (2 * HD)
-    spec = lambda base: pl.BlockSpec((None, window, 2 * HD), lambda c, p, *_: (c, 0, base * pairs + p))
-    whole = pl.BlockSpec((window, 1), lambda c, p, *_: (0, 0))
-    return pl.pallas_call(
-        attend_kernel,
-        grid_spec=pltpu.PrefetchScalarGridSpec(
-            num_scalar_prefetch=3,
-            grid=(parts, pairs),
-            in_specs=[whole, spec(0), spec(1), spec(2)],
-            out_specs=pl.BlockSpec((window, 2 * HD), lambda c, p, *_: (0, c * pairs + p)),
-        ),
-        out_shape=jax.ShapeDtypeStruct((window, D), jnp.bfloat16),
-        compiler_params=pltpu.CompilerParams(vmem_limit_bytes=48 * 2**20),
-    )(*plan, segs[:, None], qkv, qkv, qkv)
-
-
-def unit_plan(segs, z, offsets, rows, window):
-    units = window // UNIT
-    unit_seg = segs[::UNIT]
-    same = unit_seg[:, None] == unit_seg[None, :]
-    counts = jnp.sum(same.astype(jnp.int32), axis=1)
-    inside = unit_seg < 1000
-    inside = inside & (unit_seg >= 0)
-    index = lax.iota(jnp.int32, units)
-    first = jnp.sum((unit_seg[None, :] < unit_seg[:, None]).astype(jnp.int32), axis=1)
-    own = (index >= FIRST_OWN) & (index <= LAST_OWN)
-    meets = jnp.any(same & own[None, :], axis=1)
-    long = inside & (counts == LONG) & meets
-    kind = jnp.where(long, 2, jnp.where(own, 1, 0))
-    return (
-        kind.astype(jnp.int32),
-        jnp.where(long, first * UNIT, 0).astype(jnp.int32),
-        unit_seg,
-    )
-
-
-def swap(array, axis, bit):
-    size = lax.axis_size(axis)
-    return lax.ppermute(array, axis, [(i, i ^ bit) for i in range(size)])
 
 
 class Clock:
@@ -617,11 +348,14 @@
         while self.queue and self.queue[0][0] <= self.now:
             heapq.heappop(self.queue)[2]()
 
+    def step(self):
+        ready, _, action = heapq.heappop(self.queue)
+        self.now = max(self.now, ready)
+        action()
+
     def drain(self):
         while self.queue:
-            ready, _, action = heapq.heappop(self.queue)
-            self.now = max(self.now, ready)
-            action()
+            self.step()
 
 
 def block_owners(d, core, x_first):
@@ -632,10 +366,514 @@
 
 
 RING = (2, 3, 1, 0)
+FORE = (0, 1, 3, 2)
+
+
+def fore_kernel(
+    rows, window, parts, perm, back, tokens, cotangent, w_qkv, w_out, w_up, w_down, biases, vectors, kf, qf,
+    f_qkv, f_out, f_up, f_down, qkv, lse, att2, act2, slopes, first_t, lift_t, sec2, normed_out, second_low,
+    second_grads, output, inverse, small,
+    win, xq, yq, own_rows, attended, mixed, first, first_low, down, in_low, out_low, wu, wd, wq, wo, act, slope, lift2, first2,
+    turned, stage, bias_all, send, recv, near, far, own, bias_send, bias_recv, local, pair_send, pair_recv,
+):
+    f32, low = jnp.float32, jnp.bfloat16
+    d = lax.axis_index("dp")
+    z = lax.axis_index("mp")
+    core = lax.rem(d, 2)
+    cut = D // parts
+    three = 3 * cut
+    pairs = cut // (2 * HD)
+    firsts, offsets, ends = window_plan(rows, parts)
+    offset = pl.multiple_of(pick(offsets, z), 16)
+    shards = (w_qkv, w_out, w_up, w_down)
+    fulls = (f_qkv, f_out, f_up, f_down)
+    sizes = tuple(shard.shape[0] // 8 for shard in shards)
+    partner = (d ^ 1, z)
+    peers = [(d, z ^ k) for k in (1, 2, 3)] + [partner, (d ^ 2, z), (d ^ 4, z)]
+    barrier = pltpu.get_barrier_semaphore()
+    for peer in peers:
+        pl.semaphore_signal(barrier, inc=1, device_id=peer, device_id_type=MESH)
+    pl.semaphore_wait(barrier, len(peers))
+    clock = Clock()
+
+    others = (1, 3, 2)
+    chunks = [(g, k) for k in others for g in (0, 1)] + [(g, k) for k in others for g in (2, 3)]
+    index_of = {chunk: i for i, chunk in enumerate(chunks)}
+    copies, done = {}, {}
+
+    def part(ref, index, owner, size, half=None):
+        start, count = owner * size, size
+        if half is not None:
+            count = size // 2
+            start = start + half * count
+        return ref.at[index, pl.ds(pl.multiple_of(start, 16), count), :]
+
+    def remote(i, kind, src, dst, target):
+        copy = pltpu.make_async_remote_copy(
+            src, dst, send.at[i, kind], recv.at[i, kind], device_id=target, device_id_type=MESH
+        )
+        copy.start()
+        copies[i, kind] = copy
+
+    def place(i, owner, half=None):
+        g, k = chunks[i]
+        return part(fulls[g], z ^ k, owner, sizes[g], half)
+
+    def bytes_of(i):
+        g, k = chunks[i]
+        return sizes[g] * shards[g].shape[1] * 2
+
+    def pass_on(i, kind, owner, target, half=None):
+        remote(i, kind, place(i, owner, half), place(i, owner, half), target)
+
+    def hop_one(i):
+        g, k = chunks[i]
+        rows_at = pl.ds(pl.multiple_of(d * sizes[g], 16), sizes[g])
+        remote(i, 0, shards[g].at[rows_at, :], part(fulls[g], z, d, sizes[g]), (d, z ^ k))
+        clock.send("z", bytes_of(i), lambda: hop_two(i), 1.0 if k == 1 else 1.5)
+
+    def hop_two(i):
+        copies[i, 0].wait_recv()
+        if i + 4 < len(chunks):
+            hop_one(i + 4)
+        pass_on(i, 1, d, (d ^ 2, z))
+        pass_on(i, 2, d, (d ^ 4, z))
+        pass_on(i, 5, d, partner)
+        clock.send("c", bytes_of(i), lambda: None)
+        clock.send("x", bytes_of(i), lambda: hop_three(i))
+        clock.send("y", bytes_of(i), lambda: hop_four(i))
+
+    def hop_three(i):
+        copies[i, 1].wait_recv()
+        pass_on(i, 3, d ^ 2, (d ^ 4, z), 0)
+        pass_on(i, 6, d ^ 2, partner)
+        clock.send("y", bytes_of(i) // 2, lambda: hop_five(i))
+
+    def hop_four(i):
+        copies[i, 2].wait_recv()
+        pass_on(i, 4, d ^ 4, (d ^ 2, z), 1)
+        pass_on(i, 7, d ^ 4, partner)
+        clock.send("x", bytes_of(i) // 2, lambda: hop_six(i))
+
+    def hop_five(i):
+        copies[i, 3].wait_recv()
+        pass_on(i, 8, d ^ 6, partner, 0)
+        finish(i)
+
+    def hop_six(i):
+        copies[i, 4].wait_recv()
+        pass_on(i, 9, d ^ 6, partner, 1)
+        finish(i)
+
+    def finish(i):
+        done[i] = done.get(i, 0) + 1
+
+    def arrive(i):
+        while done.get(i, 0) < 2:
+            clock.step()
+        for kind in range(5, 10):
+            copies[i, kind].wait_recv()
+
+    for i in range(4):
+        hop_one(i)
+
+    halos = []
+    for j in range(parts - 1):
+        count = ends[j] - offsets[j] - rows
+        halos.append((j + 1, j, pltpu.make_async_remote_copy(
+            tokens.at[pl.ds(0, count), :], win.at[pl.ds(offsets[j] + rows, count), :],
+            near.at[0], near.at[1], device_id=(d, j), device_id_type=MESH,
+        )))
+    for j in range(1, parts):
+        halos.append((j - 1, j, pltpu.make_async_remote_copy(
+            tokens.at[pl.ds(rows - offsets[j], offsets[j]), :], win.at[pl.ds(0, offsets[j]), :],
+            far.at[0], far.at[1], device_id=(d, j), device_id_type=MESH,
+        )))
+    for sender, receiver, copy in halos:
+        @pl.when(z == sender)
+        def _(copy=copy):
+            copy.start()
+    bias_copies = []
+    for k in (1, 2, 3):
+        copy = pltpu.make_async_remote_copy(
+            biases, bias_all.at[z], bias_send.at[k - 1], bias_recv.at[k - 1], device_id=(d, z ^ k), device_id_type=MESH
+        )
+        copy.start()
+        bias_copies.append(copy)
+    bias_all[pl.ds(z, 1)] = biases[...][None]
+    owns = []
+    for g in range(4):
+        copy = pltpu.make_async_copy(shards[g], fulls[g].at[z], own.at[g])
+        copy.start()
+        owns.append(copy)
+
+    def lift(value):
+        return value.astype(f32) + vectors[8:9, :] + vectors[1:2, :]
+
+    def own_body(i, c):
+        at = pl.ds(pl.multiple_of(i * 16, 16), 16)
+        win[pl.ds(pl.multiple_of(offset + i * 16, 16), 16), :] = lift(tokens[at, :]).astype(low)
+        return c
+
+    lax.fori_loop(0, rows // 16, own_body, 0)
+    zero = jnp.zeros((16, D), low)
+
+    def spans_of(j):
+        end = ends[j] if j < parts - 1 else offsets[j] + rows
+        empty = [(0, offsets[0])] if j == 0 else []
+        if end < window:
+            empty.append((end, window))
+        filled = [(0, offsets[j])] if j else []
+        if j < parts - 1:
+            filled.append((offsets[j] + rows, ends[j]))
+        return empty, filled
+
+    for j in range(parts):
+        @pl.when(z == j)
+        def _(j=j):
+            for begin, end in spans_of(j)[0]:
+                def clear(i, c, begin=begin):
+                    win[pl.ds(pl.multiple_of(begin + i * 16, 16), 16), :] = zero
+                    return c
+                lax.fori_loop(0, (end - begin) // 16, clear, 0)
+
+    pair_copies = []
+
+    def exchange(source, target):
+        index = len(pair_copies)
+        copy = pltpu.make_async_remote_copy(
+            source, target, pair_send.at[index], pair_recv.at[index], device_id=partner, device_id_type=MESH
+        )
+        copy.start()
+        pair_copies.append(copy)
+        return copy
+
+    def columns(read, c, write):
+        for j, owner in enumerate(block_owners(d, c, True)):
+            write(slice(j * 128, (j + 1) * 128), read(pl.ds(pl.multiple_of(owner * 128, 128), 128)))
+
+    own_at = pl.ds(offset, rows)
+    mine = pl.ds(0, rows)
+    theirs = pl.ds(rows, rows)
+    columns(lambda at: win[own_at, at], 1 - core, lambda at, v: stage.__setitem__((0, slice(None), at), v))
+    lift_copy = exchange(stage.at[0], lift2.at[theirs, :])
+    columns(lambda at: win[own_at, at], core, lambda at, v: lift2.__setitem__((mine, at), v))
+
+    def fetch(index, source, target):
+        copy = pltpu.make_async_copy(source, target, local.at[index])
+        copy.start()
+        return copy
+
+    clock.work(4.0)
+    for copy in bias_copies:
+        copy.wait_recv()
+    while clock.now < 30.0 and clock.queue:
+        clock.step()
+    for sender, receiver, copy in halos:
+        @pl.when(z == receiver)
+        def _(copy=copy):
+            copy.wait_recv()
+    for j in range(parts):
+        @pl.when(z == j)
+        def _(j=j):
+            for begin, end in spans_of(j)[1]:
+                def convert(i, c, begin=begin):
+                    at = pl.ds(pl.multiple_of(begin + i * 16, 16), 16)
+                    win[at, :] = lift(win[at, :]).astype(low)
+                    return c
+                lax.fori_loop(0, (end - begin) // 16, convert, 0)
+    clock.work(2.0)
+    lift_copy.wait_recv()
+    turned[...] = lift2[...].T
+    turned_out = fetch(0, turned, lift_t)
+    clock.work(2.0)
+
+    stores = {}
+    for i in range(parts):
+        k = FORE[i]
+        at_z = z ^ k
+        if k == 0:
+            wq_ref, wo_ref = w_qkv, w_out
+        else:
+            arrive(index_of[0, k])
+            arrive(index_of[1, k])
+            load_q, load_o = fetch(1, f_qkv.at[at_z], wq), fetch(2, f_out.at[at_z], wo)
+            wq_ref, wo_ref = wq, wo
+            load_q.wait()
+        slot_i = i % 2
+        if i >= 2:
+            stores[i - 2].wait()
+        row = bias_all.at[at_z]
+
+        def project(n, c):
+            at = pl.ds(pl.multiple_of(n * 512, 512), 512)
+            for c3 in range(3):
+                lanes = slice(c3 * cut, (c3 + 1) * cut)
+                value = jnp.dot(win[at, :], wq_ref[:, lanes], preferred_element_type=f32)
+                value = (value + row[1:2, lanes]).astype(low)
+                if c3 == 0:
+                    value = value * jnp.array(HD ** (-0.5), low)
+                xq[slot_i, at, lanes] = value
+            return c
+
+        lax.fori_loop(0, window // 512, project, 0)
+        stores[i] = fetch(3 + slot_i, xq.at[slot_i], qkv.at[at_z])
+        clock.work(4.0)
+
+        def attend(step, c):
+            p, slot = step // 3, lax.rem(step, 3)
+            lanes = lambda base: pl.ds(pl.multiple_of(base + p * 2 * HD, 2 * HD), 2 * HD)
+            unit_at = [pl.ds(perm[slot * LONG + m] * UNIT, UNIT) for m in range(LONG)]
+            keys = jnp.concatenate([xq[slot_i, at, lanes(cut)] for at in unit_at], axis=0)
+            values = jnp.concatenate([xq[slot_i, at, lanes(2 * cut)] for at in unit_at], axis=0)
+            marks = jnp.concatenate([kf[at, :] for at in unit_at], axis=0)
+            wide_keys = jnp.concatenate([keys, marks], axis=1)
+            for m in range(LONG):
+                pair = two_heads(xq[slot_i, unit_at[m], lanes(0)])
+                mark = qf[unit_at[m], :]
+                wide_pair = jnp.concatenate([pair, jnp.concatenate([mark, mark], axis=0)], axis=1)
+                scores = lax.dot_general(wide_keys, wide_pair, NT, preferred_element_type=f32)
+                highest = jnp.max(scores, axis=0, keepdims=True)
+                weights = jnp.exp(scores - highest)
+                total = jnp.sum(weights, axis=0, keepdims=True)
+                chances = (weights * (1.0 / total)).astype(low)
+                flipped = lax.dot_general(values, chances, TN, preferred_element_type=f32)
+                at = pl.ds(pl.multiple_of(slot * LONG * UNIT + m * UNIT, UNIT), UNIT)
+                yq[at, lanes(0)] = from_two(flipped).astype(low)
+                lse[at_z, pl.ds(step * LONG + m, 1), :] = highest + jnp.log(total)
+            return c
+
+        lax.fori_loop(0, pairs * 3, attend, 0)
+        clock.work(9.0)
+        for u in range(FIRST_OWN, LAST_OWN + 1):
+            own_rows[pl.ds((u - FIRST_OWN) * UNIT, UNIT), :] = yq[pl.ds(back[u] * UNIT, UNIT), :]
+        lanes_z = pl.ds(pl.multiple_of(at_z * cut, cut), cut)
+        attended[i] = own_rows[pl.ds(pl.multiple_of(offset - FIRST_OWN * UNIT, 16), rows), :]
+        exchange(attended.at[i], att2.at[theirs, lanes_z])
+        stores["a", i] = fetch(5 + i, attended.at[i], att2.at[mine, lanes_z])
+        if k:
+            load_o.wait()
+
+        def out_body(n, c):
+            at = pl.ds(pl.multiple_of(n * 256, 256), 256)
+            value = jnp.dot(attended[i], wo_ref[:, at], preferred_element_type=f32)
+            if i == 0:
+                mixed[:, at] = value
+            else:
+                mixed[:, at] += value
+            return c
+
+        lax.fori_loop(0, D // 256, out_body, 0)
+        clock.work(1.0)
+
+    def norm_one(i, c):
+        at = pl.ds(pl.multiple_of(i * 16, 16), 16)
+        value = lift(tokens[at, :]) + (mixed[at, :] + vectors[2:3, :])
+        centred = value - jnp.mean(value, axis=-1, keepdims=True)
+        scale = lax.rsqrt(jnp.mean(centred * centred, axis=-1, keepdims=True) + 1e-05)
+        normed = centred * scale
+        mixed[at, :] = normed
+        inverse[at, :] = scale
+        result = normed * vectors[4:5, :] + vectors[5:6, :]
+        first[at, :] = result
+        first_low[at, :] = result.astype(low)
+        return c
+
+    lax.fori_loop(0, rows // 16, norm_one, 0)
+    normed_store = fetch(9, mixed, normed_out)
+    columns(lambda at: first_low[:, at], 1 - core, lambda at, v: stage.__setitem__((1, slice(None), at), v))
+    first_copy = exchange(stage.at[1], first2.at[theirs, :])
+    columns(lambda at: first_low[:, at], core, lambda at, v: first2.__setitem__((mine, at), v))
+    clock.work(4.0)
+
+    for i in range(parts):
+        k = FORE[i]
+        at_z = z ^ k
+        slot_i = i % 2
+        if k == 0:
+            up_ref, down_ref = w_up, w_down
+        else:
+            arrive(index_of[2, k])
+            load_u = fetch(1, f_up.at[at_z], wu)
+            arrive(index_of[3, k])
+            load_d = fetch(2, f_down.at[at_z], wd)
+            up_ref, down_ref = wu, wd
+            load_u.wait()
+        if i >= 2:
+            for copy in stores["f", i - 2]:
+                copy.wait()
+            stores["r", i - 2].wait_send()
+        row = bias_all.at[at_z]
+
+        def upper_body(n, c):
+            at = pl.ds(pl.multiple_of(n * 256, 256), 256)
+            value = jnp.dot(first_low[...], up_ref[:, at], preferred_element_type=f32) + row[0:1, at]
+            chance = 0.5 + 0.5 * lax.erf(value * (0.5**0.5))
+            act[slot_i, :, at] = (value * chance).astype(low)
+            density = jnp.exp(-0.5 * value * value) * (0.5 / jnp.pi) ** 0.5
+            slope[slot_i, :, at] = (chance + value * density).astype(low)
+            return c
+
+        lax.fori_loop(0, D // 256, upper_body, 0)
+        hidden = pl.ds(pl.multiple_of(at_z * D, D), D)
+        stores["r", i] = exchange(act.at[slot_i], act2.at[theirs, hidden])
+        stores["f", i] = (
+            fetch(14 + slot_i, act.at[slot_i], act2.at[mine, hidden]),
+            fetch(10 + slot_i, slope.at[slot_i], slopes.at[:, hidden]),
+        )
+        clock.work(4.0)
+        if k:
+            load_d.wait()
+
+        def down_body(n, c):
+            at = pl.ds(pl.multiple_of(n * 256, 256), 256)
+            value = jnp.dot(act[slot_i], down_ref[:, at], preferred_element_type=f32)
+            if i == 0:
+                down[:, at] = value
+            else:
+                down[:, at] += value
+            return c
+
+        lax.fori_loop(0, D // 256, down_body, 0)
+        clock.work(2.0)
+        if i == 0:
+            first_copy.wait_recv()
+            turned_out.wait()
+            turned[...] = first2[...].T
+            turned_out = fetch(0, turned, first_t)
+            clock.work(2.0)
+
+    zero_row = jnp.zeros((16, D), f32)
+
+    def norm_two(i, sums):
+        at = pl.ds(pl.multiple_of(i * 16, 16), 16)
+        value = first[at, :] + (down[at, :] + vectors[3:4, :])
+        centred = value - jnp.mean(value, axis=-1, keepdims=True)
+        scale = lax.rsqrt(jnp.mean(centred * centred, axis=-1, keepdims=True) + 1e-05)
+        normed = centred * scale
+        out_low[at, :] = (normed * vectors[6:7, :] + vectors[7:8, :]).astype(low)
+        grads = cotangent[at, :].astype(f32)
+        scaled = grads * vectors[6:7, :]
+        result = scale * (
+            scaled
+            - jnp.mean(scaled, axis=-1, keepdims=True)
+            - normed * jnp.mean(scaled * normed, axis=-1, keepdims=True)
+        )
+        down[at, :] = result
+        in_low[at, :] = result.astype(low)
+        return (sums[0] + result, sums[1] + grads * normed, sums[2] + grads)
+
+    sums = lax.fori_loop(0, rows // 16, norm_two, (zero_row, zero_row, zero_row))
+    last = [fetch(1, out_low, output), fetch(2, in_low, second_low), fetch(12, down, second_grads)]
+    small[...] = jnp.zeros_like(small)
+    small[3:4, :] = jnp.sum(sums[0], axis=0, keepdims=True)
+    small[6:7, :] = jnp.sum(sums[1], axis=0, keepdims=True)
+    small[7:8, :] = jnp.sum(sums[2], axis=0, keepdims=True)
+    small[15:16, :] = vectors[9:10, :]
+    columns(lambda at: in_low[:, at], 1 - core, lambda at, v: stage.__setitem__((2, slice(None), at), v))
+    exchange(stage.at[2], sec2.at[theirs, :])
+    columns(lambda at: in_low[:, at], core, lambda at, v: stage.__setitem__((3, slice(None), at), v))
+    last.append(fetch(13, stage.at[3], sec2.at[mine, :]))
+    clock.drain()
+    for copy in last + owns + [turned_out, normed_store, stores[2], stores[3]]:
+        copy.wait()
+    for i in range(parts):
+        stores["a", i].wait()
+        if i >= 2:
+            for copy in stores["f", i]:
+                copy.wait()
+    waited = [stores["r", 0], stores["r", 1]]
+    for copy in pair_copies:
+        if not any(copy is other for other in waited):
+            copy.wait_send()
+        if copy is not lift_copy and copy is not first_copy:
+            copy.wait_recv()
+    for copy in copies.values():
+        copy.wait_send()
+    for copy in bias_copies:
+        copy.wait_send()
+    for sender, receiver, copy in halos:
+        @pl.when(z == sender)
+        def _(copy=copy):
+            copy.wait_send()
+
+
+def fore_call(rows, window, parts, perm, back, *arrays):
+    f32, low = jnp.float32, jnp.bfloat16
+    any_ = pl.BlockSpec(memory_space=pl.ANY)
+    vmem = pl.BlockSpec(memory_space=pltpu.VMEM)
+    smem = pl.BlockSpec(memory_space=pltpu.SMEM)
+    cut = D // parts
+    three = 3 * cut
+    shape = jax.ShapeDtypeStruct
+    marks = cut // (2 * HD) * 3 * LONG
+    dma = pltpu.SemaphoreType.DMA
+    return pl.pallas_call(
+        functools.partial(fore_kernel, rows, window, parts),
+        out_shape=[
+            shape((parts, D, three), low),
+            shape((parts, cut, D), low),
+            shape((parts, D, D), low),
+            shape((parts, D, D), low),
+            shape((parts, window, three), low),
+            shape((parts, marks, 2 * UNIT), f32),
+            shape((2 * rows, D), low),
+            shape((2 * rows, FF), low),
+            shape((rows, FF), low),
+            shape((512, 2 * rows), low),
+            shape((512, 2 * rows), low),
+            shape((2 * rows, 512), low),
+            shape((rows, D), f32),
+            shape((rows, D), low),
+            shape((rows, D), f32),
+            shape((rows, D), low),
+            shape((rows, 1), f32),
+            shape((16, D), f32),
+        ],
+        in_specs=[smem, smem] + [vmem] * len(arrays),
+        out_specs=[any_] * 5 + [vmem] + [any_] * 10 + [vmem] * 2,
+        scratch_shapes=[
+            pltpu.VMEM((window, D), low),
+            pltpu.VMEM((2, window, three), low),
+            pltpu.VMEM((window, cut), low),
+            pltpu.VMEM(((LAST_OWN + 1 - FIRST_OWN) * UNIT, cut), low),
+            pltpu.VMEM((parts, rows, cut), low),
+            pltpu.VMEM((rows, D), f32),
+            pltpu.VMEM((rows, D), f32),
+            pltpu.VMEM((rows, D), low),
+            pltpu.VMEM((rows, D), f32),
+            pltpu.VMEM((rows, D), low),
+            pltpu.VMEM((rows, D), low),
+            pltpu.VMEM((D, D), low),
+            pltpu.VMEM((D, D), low),
+            pltpu.VMEM((D, three), low),
+            pltpu.VMEM((cut, D), low),
+            pltpu.VMEM((2, rows, D), low),
+            pltpu.VMEM((2, rows, D), low),
+            pltpu.VMEM((2 * rows, 512), low),
+            pltpu.VMEM((2 * rows, 512), low),
+            pltpu.VMEM((512, 2 * rows), low),
+            pltpu.VMEM((4, rows, 512), low),
+            pltpu.VMEM((parts, 8, D), f32),
+            dma((12, 10)),
+            dma((12, 10)),
+            dma((2,)),
+            dma((2,)),
+            dma((4,)),
+            dma((3,)),
+            dma((3,)),
+            dma((16,)),
+            dma((2 * parts + 3,)),
+            dma((2 * parts + 3,)),
+        ],
+        compiler_params=pltpu.CompilerParams(
+            collective_id=0, has_side_effects=True, vmem_limit_bytes=56 * 2**20
+        ),
+    )(perm, back, *arrays)
 
 
 def back_kernel(
-    rows, window, parts, perm, back, sec_low, sec2, inverse, gain, small_in, kf, qf,
+    rows, window, parts, perm, back, sec_low, sec2, inverse, gain, small_in, kf, qf, lse,
     first_t, lift_t, second_grads, normed_one, act2, dgelu, att2, qkv, f_qkv, f_out, f_up, f_down,
     input_grad, g_qkv, g_out, g_up, g_down, small_out,
     acc, normed, turned, arena, act, slope, y, up2, w_in, mixed2, stage, mixed_win, small, small_in_far,
@@ -1009,9 +1247,8 @@
                 grads = two_heads(x[unit_at[m], lanes(three)])
                 mark = qf[unit_at[m], :]
                 wide_pair = jnp.concatenate([pair, jnp.concatenate([mark, mark], axis=0)], axis=1)
-                scores = lax.dot_general(wide_keys, wide_pair, NT, preferred_element_type=f32) * scale
-                weights = jnp.exp(scores - jnp.max(scores, axis=0, keepdims=True))
-                chances = weights * (1.0 / jnp.sum(weights, axis=0, keepdims=True))
+                scores = lax.dot_general(wide_keys, wide_pair, NT, preferred_element_type=f32)
+                chances = jnp.exp(scores - lse[chunk(RING[i]), pl.ds(step * LONG + m, 1), :])
                 flow = lax.dot_general(values, grads, NT, preferred_element_type=f32)
                 inner = jnp.sum(chances * flow, axis=0, keepdims=True)
                 slopes = (chances * (flow - inner)).astype(low)
@@ -1021,7 +1258,7 @@
                 at = pl.ds(pl.multiple_of(slot * LONG * UNIT + m * UNIT, UNIT), UNIT)
                 y[at, lanes(0)] = (from_two(flipped) * scale).astype(low)
             at = pl.ds(pl.multiple_of(slot * LONG * UNIT, UNIT), LONG * UNIT)
-            y[at, lanes(cut)] = (k_sum * scale).astype(low)
+            y[at, lanes(cut)] = k_sum.astype(low)
             y[at, lanes(2 * cut)] = v_sum.astype(low)
             return c
 
@@ -1176,7 +1413,7 @@
     seg = jnp.where(segs < 0, 2 * HD - 1, jnp.where(segs >= 1000, 2 * HD - 2, segs))
     same = seg[:, None] == lane[None, :]
     keys = jnp.where(same, 1.0, 0.0).astype(jnp.bfloat16)
-    queries = jnp.where(same, 0.0, -8e30).astype(jnp.bfloat16)
+    queries = jnp.where(same, 0.0, -1e30).astype(jnp.bfloat16)
     return keys, queries
 
 
@@ -1196,84 +1433,41 @@
     rows = tokens.shape[0]
     parts = lax.axis_size("mp")
     z = lax.axis_index("mp")
-    d = lax.axis_index("dp")
-    core = lax.rem(d, 2)
     low = jnp.bfloat16
     f32 = jnp.float32
     cut = D // parts
     firsts, offsets, ends = window_plan(rows, parts)
     window = -(-max(ends) // UNIT) * UNIT
-    win, f_qkv, f_out, f_up, f_down = gather(
-        tokens, w_qkv.reshape(D, 3 * cut), w_out, w_up, w_down, window, parts
-    )
-    bias_qv_all = lax.all_gather(bias_qv, "mp", axis=1, tiled=True).astype(f32)
-    bias_up_all = lax.all_gather(bias_up, "mp", axis=0, tiled=True).astype(f32)
-    offset = pick(offsets, z)
     first_token = UNIT * pick(firsts, z)
     positions = first_token + lax.iota(jnp.int32, window)
     lengths_end = jnp.cumsum(item_lengths[0])
     segs = jnp.sum((positions[:, None] >= lengths_end[None, :]).astype(jnp.int32), axis=1)
     segs = jnp.where(positions < 0, -1, jnp.where(positions >= LEN, 1000, segs))
-    plan = unit_plan(segs, z, offsets, rows, window)
     perm, back = unit_order(segs, window)
     kf, qf = marks_of(segs)
     step_time = timesteps[0].astype(f32) * 0.001
-
-    lifted = tokens.astype(f32) + step_time * vectors[0] + vectors[1]
-    lifted_low = lifted.astype(low)
-    win_low = (win.astype(f32) + step_time * vectors[0] + vectors[1]).astype(low)
-    bias3 = jnp.stack([bias_qv_all[0], jnp.zeros((D,), f32), bias_qv_all[1]])
-    bias3 = jnp.transpose(bias3.reshape(3, parts, cut), (1, 0, 2)).reshape(parts, 1, 3 * cut)
-    qkv = (jnp.einsum("td,zde->zte", win_low, f_qkv, preferred_element_type=f32) + bias3).astype(low)
-    attended = attention_call(window, parts, plan, segs, qkv)
-    attended = lax.dynamic_slice_in_dim(attended, offset, rows, 0)
-    wo = f_out.reshape(D, D)
-    mixed = jnp.dot(attended, wo, preferred_element_type=f32) + vectors[2]
-    first, normed_one, inverse_one = norm_forward(lifted + mixed, vectors[4], vectors[5])
-    first_low = first.astype(low)
-    upper = jnp.concatenate(
-        [jnp.dot(first_low, f_up[j], preferred_element_type=f32) for j in range(parts)], axis=1
-    )
-    upper = upper + bias_up_all
-    chance = 0.5 * (1.0 + lax.erf(upper * (0.5**0.5)))
-    activated = (upper * chance).astype(low)
-    slope = (chance + upper * jnp.exp(-0.5 * upper * upper) * (0.5 / jnp.pi) ** 0.5).astype(low)
-    wd = f_down.reshape(FF, D)
-    down = jnp.dot(activated, wd, preferred_element_type=f32) + vectors[3]
-    output, normed_two, inverse_two = norm_forward(first + down, vectors[6], vectors[7])
-    out_grads = cotangent.astype(f32)
-    second_grads, gain_two, shift_two = norm_backward(out_grads, normed_two, inverse_two, vectors[6])
-    second_low = second_grads.astype(low)
-
-    def arranged(value, c):
-        return jnp.concatenate(
-            [lax.dynamic_slice_in_dim(value, owner * 128, 128, 1) for owner in block_owners(d, c, True)], axis=1
-        )
-
-    def both(mine, sent):
-        return jnp.concatenate([mine, swap(sent, "dp", 1)], axis=0)
-
-    sec2 = both(arranged(second_low, core), arranged(second_low, 1 - core))
-    first_t = both(arranged(first_low, core), arranged(first_low, 1 - core)).T
-    lift_t = both(arranged(lifted_low, core), arranged(lifted_low, 1 - core)).T
-    act2 = both(activated, activated)
-    att2 = both(attended, attended)
-    zero_row = jnp.zeros((D,), f32)
-    small_in = jnp.stack(
-        [zero_row] * 3
-        + [jnp.sum(second_grads, axis=0), zero_row, zero_row, gain_two, shift_two]
-        + [zero_row] * 7
-        + [jnp.broadcast_to(step_time, (D,))]
+    bias_q, bias_v = bias_qv[0].astype(f32), bias_qv[1].astype(f32)
+    bias_row = jnp.concatenate([bias_q, jnp.zeros((cut,), f32), bias_v, jnp.zeros((D - 3 * cut,), f32)])
+    biases = jnp.concatenate([jnp.stack([bias_up.astype(f32), bias_row]), jnp.zeros((6, D), f32)])
+    rows16 = jnp.concatenate(
+        [vectors, (step_time * vectors[0])[None], jnp.full((7, D), step_time, f32)], axis=0
+    )
+    (
+        f_qkv, f_out, f_up, f_down, qkv, lse, att2, act2, slope, first_t, lift_t, sec2, normed_one,
+        second_low, second_grads, output, inverse_one, small_in,
+    ) = fore_call(
+        rows, window, parts, perm, back, tokens, cotangent,
+        w_qkv.reshape(D, 3 * cut), w_out, w_up, w_down, biases, rows16, kf, qf,
     )
     input_grad, grad_qkv, grad_out, grad_up, grad_down, small = back_call(
         rows, window, parts, perm, back,
-        (second_low, sec2, inverse_one, vectors[4:5], small_in, kf, qf),
+        (second_low, sec2, inverse_one, vectors[4:5], small_in, kf, qf, lse),
         (first_t, lift_t, second_grads, normed_one, act2, slope, att2, qkv, f_qkv, f_out, f_up, f_down),
     )
     grad_bias_qv = lax.dynamic_slice_in_dim(small[8:10], z * cut, cut, 1)
     grad_bias_up = lax.dynamic_slice_in_dim(small[10:14].reshape(FF), z * (FF // parts), FF // parts, 0)
     return (
-        output.astype(low),
+        output,
         input_grad,
         grad_qkv.reshape(-1, 3, cut),
         grad_bias_qv,

time: 486 us -> 399 us (0.82); the launches traced: 477 us -> 396 us
  matrix products: 30 us -> 0 us
  other arithmetic: 34.2 us -> 4.43 us
  Pallas kernels: 351 us -> 377 us
  blocking collectives: 24.7 us -> 0 us
  local copies, waits for them, and re-layouts: 30.2 us -> 12.6 us
  starting transfers between devices: 4.95 us -> 0 us
    pallas_call x2 -> x1, Pallas kernels: 153 us -> 192 us  [fore_call(): pl.pallas_call(functools.partial(fore_kernel, rows, window, parts), out_s...]
    dot_general x7 -> x0, matrix products: 30 us -> none  [the longest x1 11.9 us: local_body(): jnp.einsum('td,zde->zte', win_low, f_qkv, preferred_element_type=f32)]
    all_gather x2 -> x0, blocking collectives: 24.7 us -> none  [the longest x1 12.6 us: local_body(): bias_qv_all = lax.all_gather(bias_qv, 'mp', axis=1, tiled=True).astype(f32)]
    concatenate x6 -> x3, other arithmetic: 13.7 us -> 1.4 us  [the longest x1 0.71 us: local_body(): jnp.concatenate([vectors, (step_time * vectors[0])[None], jnp.full((7, D)...]
    pallas_call x1, Pallas kernels: 197 us -> 185 us  [back_call(): pl.pallas_call(functools.partial(back_kernel, rows, window, parts), out_s...]
    convert_element_type x6 -> x2, other arithmetic: 11.4 us -> 1.15 us  [the longest x1 1.15 us: marks_of(): queries = jnp.where(same, 0.0, -1e+30).astype(jnp.bfloat16)]
    unnamed x54 -> x29, local copies, waits for them, and re-layouts: 13.9 us -> 6.98 us
    ppermute x5 -> x0, starting transfers between devices: 4.95 us -> none  [swap(): return lax.ppermute(array, axis, [(i, i ^ bit) for i in range(size)])]
  transfers between devices with their start and end apart: 5 -> 0, of which waited for: 0 -> 0; matrix products, arithmetic and copies ran while one was open for 11% -> 0% of each run, Pallas kernels for 0% -> 0%
where the time goes in v3:
time: 399 us; the launch traced here: 396 us
  Pallas kernels  377 us (94%)
  local copies, waits for them, and re-layouts  12.6 us (3%)
  other arithmetic  4.43 us (1%)
    pallas_call x1, Pallas kernels, fore_call(): pl.pallas_call(functools.partial(fore_kernel, rows, window, parts), out_s...  192 us
    pallas_call x1, Pallas kernels, back_call(): pl.pallas_call(functools.partial(back_kernel, rows, window, parts), out_s...  185 us

profile of v3, /device:TPU:0, one launch (start us, length us, event | category | flops | bytes accessed | tf_op | source)
XLA Modules:
  0.0 395.9 jit_solution(612887257755748908)
XLA Ops:
  0.7 0.7 copy.28
  1.5 0.1 reduce
  1.6 0.1 convert_reduce_fusion
  1.7 0.1 slice.24
  1.8 0.2 convert_reduce_fusion.2
  2.0 0.2 convert_reduce_fusion.1.back
  2.2 0.0 copy-start.9
  2.2 0.6 select_reduce_fusion.perm
  2.8 1.7 copy.29
  4.5 0.0 copy-done.9
  4.5 0.0 copy-start.7
  4.5 0.0 copy-start.8
  4.6 0.0 copy-start.5
  4.6 1.6 copy.30.w_qkv
  6.2 0.0 copy-done.7
  6.2 0.0 copy-done.8
  6.2 0.1 pad.5.clone
  6.3 0.7 maximum_maximum_fusion.1.biases
  7.6 0.0 copy-done.5
  7.7 0.6 fusion.1
  8.3 0.1 pad.2.clone
  8.3 0.7 maximum_maximum_fusion.vectors
  9.0 1.1 select_convert_fusion
  10.2 191.9 %shard_map.178 = (bf16[4,1024,768]{2,1,0:T(8,128)(2,1)}, bf16[4,256,1024]{2,1,0:T(8,128)(2,1)}, bf16[4,1024,1024]{2,1,0:T(8,128)(2,1)}, bf16[4,1024,1024]{2,1,0:...) custom-call(s32[12]{0:T(128)} %select_reduce_fusion.perm, ...), custom_call_target="tpu_custom_call" | custom-call | tf_op jit(solution)/shard_map/pallas_call | solution.py:811
  202.1 185.3 %shard_map.179 = (bf16[592,1024]{1,0:T(8,128)(2,1)}, f32[128,768]{1,0:T(8,128)}, f32[256,128]{1,0:T(8,128)}, f32[128,1024]{1,0:T(8,128)}, f32[1024,128]{1,0:T(8,128)}, /*index=5*/f32[16,1024]{1,0:T(8,128)}) custom-call(s32[12]{0:T(128)} %select_reduce_fusion.perm, s32[12]{0:T(128)} %copy-done.9, bf16[592,1024]{1,0:T(8,128)(2,1)} %get-tuple-element.34.sec_low, ...), custom_call_target="tpu_custom_call" | custom-call | tf_op jit(solution)/shard_map/pallas_call | solution.py:1361
  387.4 0.0 copy-start.6
  387.4 0.0 copy-start
  387.4 1.3 copy.31
  388.7 0.0 copy-start.1
  388.7 0.9 copy.32
  389.6 0.0 copy-done.6
  389.6 0.6 constant_dynamic-slice_fusion
  390.2 0.6 dynamic_slice.7
  390.8 0.6 slice.31
  391.4 0.0 copy-done
  391.4 1.0 copy.42
  392.4 0.0 copy-done.1
  392.4 0.0 copy-start.4
  392.5 0.0 copy-start.3
  392.5 0.0 copy-start.2
  392.5 1.0 copy.43
  393.5 0.0 copy-done.4
  393.5 0.7 copy.44
  394.1 0.0 copy-done.3
  394.1 0.8 copy.45
  394.9 0.0 copy-done.2
  394.9 0.8 copy.46
  (13 shorter events, 0.1 us)
Async XLA Ops:
  2.2 2.4 copy-start.9
  4.5 1.6 copy-start.7
  4.5 1.6 copy-start.8
  4.6 3.1 copy-start.5
  387.4 2.2 copy-start.6
  387.4 4.0 %copy-start = (bf16[592,1024]{1,0:T(8,128)(2,1)S(1)}, bf16[592,1024]{1,0:T(8,128)(2,1)}, u32[]{:S(2)}) copy-start(bf16[592,1024]{1,0:T(8,128)(2,1)} %get-tuple-element.101) | copy-start | bytes 3637252
  388.7 3.8 copy-start.1
  392.4 1.0 copy-start.4
  392.5 1.7 copy-start.3
  392.5 2.5 copy-start.2

commit v4 on v3

--- a/solution.py
+++ b/solution.py
@@ -328,6 +328,20 @@
     return both.T
 
 
+def by_rows(rows, body, carry):
+    count = rows // 32
+
+    def step(i, c):
+        return body(pl.multiple_of(i * 32, 32), 32, c)
+
+    carry = lax.fori_loop(0, count, step, carry)
+    return body(count * 32, rows - count * 32, carry) if rows % 32 else carry
+
+
+def fold(value):
+    return value if value.shape[0] == 16 else value[:16] + value[16:]
+
+
 class Clock:
     def __init__(self):
         self.now = 0.0
@@ -366,7 +380,7 @@
 
 
 RING = (2, 3, 1, 0)
-FORE = (0, 1, 3, 2)
+HALO_TIME = 34.0
 
 
 def fore_kernel(
@@ -374,7 +388,7 @@
     f_qkv, f_out, f_up, f_down, qkv, lse, att2, act2, slopes, first_t, lift_t, sec2, normed_out, second_low,
     second_grads, output, inverse, small,
     win, xq, yq, own_rows, attended, mixed, first, first_low, down, in_low, out_low, wu, wd, wq, wo, act, slope, lift2, first2,
-    turned, stage, bias_all, send, recv, near, far, own, bias_send, bias_recv, local, pair_send, pair_recv,
+    turned, stage, bias_all, send, recv, own_sent, near, far, own, bias_send, bias_recv, local, pair_send, pair_recv,
 ):
     f32, low = jnp.float32, jnp.bfloat16
     d = lax.axis_index("dp")
@@ -396,8 +410,9 @@
     pl.semaphore_wait(barrier, len(peers))
     clock = Clock()
 
-    others = (1, 3, 2)
-    chunks = [(g, k) for k in others for g in (0, 1)] + [(g, k) for k in others for g in (2, 3)]
+    order = [sorted((o for o in range(parts) if o != j), key=lambda o: (abs(o - j), o)) for j in range(parts)]
+    source = [pick([order[j][n] for j in range(parts)], z) for n in range(parts - 1)]
+    chunks = [(g, n) for n in range(parts - 1) for g in (0, 1)] + [(g, n) for n in range(parts - 1) for g in (2, 3)]
     index_of = {chunk: i for i, chunk in enumerate(chunks)}
     copies, done = {}, {}
 
@@ -416,26 +431,53 @@
         copies[i, kind] = copy
 
     def place(i, owner, half=None):
-        g, k = chunks[i]
-        return part(fulls[g], z ^ k, owner, sizes[g], half)
+        g, n = chunks[i]
+        return part(fulls[g], source[n], owner, sizes[g], half)
 
     def bytes_of(i):
-        g, k = chunks[i]
+        g, n = chunks[i]
         return sizes[g] * shards[g].shape[1] * 2
 
     def pass_on(i, kind, owner, target, half=None):
         remote(i, kind, place(i, owner, half), place(i, owner, half), target)
 
-    def hop_one(i):
-        g, k = chunks[i]
+    column = []
+
+    def along(owner, place_of, here, there, sent, g):
+        i = index_of[g, order[there].index(owner)]
+        copy = pltpu.make_async_remote_copy(
+            place_of, part(fulls[g], owner, d, sizes[g]), sent, recv.at[i, 0],
+            device_id=(d, there), device_id_type=MESH,
+        )
+
+        @pl.when(z == here)
+        def _():
+            copy.start()
+
+        column.append((here, copy))
+
+    def send_own(g):
         rows_at = pl.ds(pl.multiple_of(d * sizes[g], 16), sizes[g])
-        remote(i, 0, shards[g].at[rows_at, :], part(fulls[g], z, d, sizes[g]), (d, z ^ k))
-        clock.send("z", bytes_of(i), lambda: hop_two(i), 1.0 if k == 1 else 1.5)
+        for here in range(parts):
+            for n, there in enumerate((here - 1, here + 1)):
+                if 0 <= there < parts:
+                    along(here, shards[g].at[rows_at, :], here, there, own_sent.at[g, n], g)
+        for n in range(parts - 1):
+            i = index_of[g, n]
+            clock.send("z", bytes_of(i), lambda i=i: hop_two(i))
 
     def hop_two(i):
-        copies[i, 0].wait_recv()
-        if i + 4 < len(chunks):
-            hop_one(i + 4)
+        g, n = chunks[i]
+        pltpu.make_async_remote_copy(
+            place(i, d), place(i, d), send.at[i, 0], recv.at[i, 0], device_id=partner, device_id_type=MESH
+        ).wait_recv()
+        for here in range(parts):
+            owner = order[here][n]
+            there = here + 1 if owner < here else here - 1
+            if 0 <= there < parts:
+                along(owner, part(fulls[g], owner, d, sizes[g]), here, there, send.at[i, 0], g)
+        if n == 0 and g < 2:
+            send_own(g + 2)
         pass_on(i, 1, d, (d ^ 2, z))
         pass_on(i, 2, d, (d ^ 4, z))
         pass_on(i, 5, d, partner)
@@ -474,8 +516,8 @@
         for kind in range(5, 10):
             copies[i, kind].wait_recv()
 
-    for i in range(4):
-        hop_one(i)
+    send_own(0)
+    send_own(1)
 
     halos = []
     for j in range(parts - 1):
@@ -493,6 +535,7 @@
         @pl.when(z == sender)
         def _(copy=copy):
             copy.start()
+    clock.send("z", max(offsets) * D * 2, lambda: None)
     bias_copies = []
     for k in (1, 2, 3):
         copy = pltpu.make_async_remote_copy(
@@ -567,8 +610,7 @@
     clock.work(4.0)
     for copy in bias_copies:
         copy.wait_recv()
-    while clock.now < 30.0 and clock.queue:
-        clock.step()
+    clock.work(max(0.0, HALO_TIME - clock.now))
     for sender, receiver, copy in halos:
         @pl.when(z == receiver)
         def _(copy=copy):
@@ -590,13 +632,13 @@
 
     stores = {}
     for i in range(parts):
-        k = FORE[i]
-        at_z = z ^ k
+        k = i
+        at_z = source[i - 1] if i else z
         if k == 0:
             wq_ref, wo_ref = w_qkv, w_out
         else:
-            arrive(index_of[0, k])
-            arrive(index_of[1, k])
+            arrive(index_of[0, k - 1])
+            arrive(index_of[1, k - 1])
             load_q, load_o = fetch(1, f_qkv.at[at_z], wq), fetch(2, f_out.at[at_z], wo)
             wq_ref, wo_ref = wq, wo
             load_q.wait()
@@ -628,23 +670,24 @@
             values = jnp.concatenate([xq[slot_i, at, lanes(2 * cut)] for at in unit_at], axis=0)
             marks = jnp.concatenate([kf[at, :] for at in unit_at], axis=0)
             wide_keys = jnp.concatenate([keys, marks], axis=1)
+            pair = jnp.concatenate([two_heads(xq[slot_i, at, lanes(0)]) for at in unit_at], axis=0)
+            mark = jnp.concatenate([qf[at, :] for at in unit_at for _ in range(2)], axis=0)
+            wide_pair = jnp.concatenate([pair, mark], axis=1)
+            scores = lax.dot_general(wide_keys, wide_pair, NT, preferred_element_type=f32)
+            highest = jnp.max(scores, axis=0, keepdims=True)
+            weights = jnp.exp(scores - highest)
+            total = jnp.sum(weights, axis=0, keepdims=True)
+            flipped = lax.dot_general(values, weights.astype(low), TN, preferred_element_type=f32) * (1.0 / total)
+            logsum = highest + jnp.log(total)
             for m in range(LONG):
-                pair = two_heads(xq[slot_i, unit_at[m], lanes(0)])
-                mark = qf[unit_at[m], :]
-                wide_pair = jnp.concatenate([pair, jnp.concatenate([mark, mark], axis=0)], axis=1)
-                scores = lax.dot_general(wide_keys, wide_pair, NT, preferred_element_type=f32)
-                highest = jnp.max(scores, axis=0, keepdims=True)
-                weights = jnp.exp(scores - highest)
-                total = jnp.sum(weights, axis=0, keepdims=True)
-                chances = (weights * (1.0 / total)).astype(low)
-                flipped = lax.dot_general(values, chances, TN, preferred_element_type=f32)
+                two = slice(m * 2 * UNIT, (m + 1) * 2 * UNIT)
                 at = pl.ds(pl.multiple_of(slot * LONG * UNIT + m * UNIT, UNIT), UNIT)
-                yq[at, lanes(0)] = from_two(flipped).astype(low)
-                lse[at_z, pl.ds(step * LONG + m, 1), :] = highest + jnp.log(total)
+                yq[at, lanes(0)] = from_two(flipped[:, two]).astype(low)
+                lse[at_z, pl.ds(step * LONG + m, 1), :] = logsum[:, two]
             return c
 
-        lax.fori_loop(0, pairs * 3, attend, 0)
-        clock.work(9.0)
+        lax.fori_loop(0, pairs * 3, attend, 0, unroll=2)
+        clock.work(7.5)
         for u in range(FIRST_OWN, LAST_OWN + 1):
             own_rows[pl.ds((u - FIRST_OWN) * UNIT, UNIT), :] = yq[pl.ds(back[u] * UNIT, UNIT), :]
         lanes_z = pl.ds(pl.multiple_of(at_z * cut, cut), cut)
@@ -666,8 +709,8 @@
         lax.fori_loop(0, D // 256, out_body, 0)
         clock.work(1.0)
 
-    def norm_one(i, c):
-        at = pl.ds(pl.multiple_of(i * 16, 16), 16)
+    def norm_one(begin, count, c):
+        at = pl.ds(begin, count)
         value = lift(tokens[at, :]) + (mixed[at, :] + vectors[2:3, :])
         centred = value - jnp.mean(value, axis=-1, keepdims=True)
         scale = lax.rsqrt(jnp.mean(centred * centred, axis=-1, keepdims=True) + 1e-05)
@@ -679,7 +722,7 @@
         first_low[at, :] = result.astype(low)
         return c
 
-    lax.fori_loop(0, rows // 16, norm_one, 0)
+    by_rows(rows, norm_one, 0)
     normed_store = fetch(9, mixed, normed_out)
     columns(lambda at: first_low[:, at], 1 - core, lambda at, v: stage.__setitem__((1, slice(None), at), v))
     first_copy = exchange(stage.at[1], first2.at[theirs, :])
@@ -687,15 +730,15 @@
     clock.work(4.0)
 
     for i in range(parts):
-        k = FORE[i]
-        at_z = z ^ k
+        k = i
+        at_z = source[i - 1] if i else z
         slot_i = i % 2
         if k == 0:
             up_ref, down_ref = w_up, w_down
         else:
-            arrive(index_of[2, k])
+            arrive(index_of[2, k - 1])
             load_u = fetch(1, f_up.at[at_z], wu)
-            arrive(index_of[3, k])
+            arrive(index_of[3, k - 1])
             load_d = fetch(2, f_down.at[at_z], wd)
             up_ref, down_ref = wu, wd
             load_u.wait()
@@ -745,8 +788,8 @@
 
     zero_row = jnp.zeros((16, D), f32)
 
-    def norm_two(i, sums):
-        at = pl.ds(pl.multiple_of(i * 16, 16), 16)
+    def norm_two(begin, count, sums):
+        at = pl.ds(begin, count)
         value = first[at, :] + (down[at, :] + vectors[3:4, :])
         centred = value - jnp.mean(value, axis=-1, keepdims=True)
         scale = lax.rsqrt(jnp.mean(centred * centred, axis=-1, keepdims=True) + 1e-05)
@@ -761,9 +804,9 @@
         )
         down[at, :] = result
         in_low[at, :] = result.astype(low)
-        return (sums[0] + result, sums[1] + grads * normed, sums[2] + grads)
-
-    sums = lax.fori_loop(0, rows // 16, norm_two, (zero_row, zero_row, zero_row))
+        return (sums[0] + fold(result), sums[1] + fold(grads * normed), sums[2] + fold(grads))
+
+    sums = by_rows(rows, norm_two, (zero_row, zero_row, zero_row))
     last = [fetch(1, out_low, output), fetch(2, in_low, second_low), fetch(12, down, second_grads)]
     small[...] = jnp.zeros_like(small)
     small[3:4, :] = jnp.sum(sums[0], axis=0, keepdims=True)
@@ -790,6 +833,10 @@
             copy.wait_recv()
     for copy in copies.values():
         copy.wait_send()
+    for here, copy in column:
+        @pl.when(z == here)
+        def _(copy=copy):
+            copy.wait_send()
     for copy in bias_copies:
         copy.wait_send()
     for sender, receiver, copy in halos:
@@ -857,6 +904,7 @@
             pltpu.VMEM((parts, 8, D), f32),
             dma((12, 10)),
             dma((12, 10)),
+            dma((4, 2)),
             dma((2,)),
             dma((2,)),
             dma((4,)),
@@ -876,7 +924,7 @@
     rows, window, parts, perm, back, sec_low, sec2, inverse, gain, small_in, kf, qf, lse,
     first_t, lift_t, second_grads, normed_one, act2, dgelu, att2, qkv, f_qkv, f_out, f_up, f_down,
     input_grad, g_qkv, g_out, g_up, g_down, small_out,
-    acc, normed, turned, arena, act, slope, y, up2, w_in, mixed2, stage, mixed_win, small, small_in_far,
+    acc, normed, turned, arena, act, slope, y, up2, w_in, mixed2, mixed_win, small, small_in_far,
     s_down, s_up, s_out, s_qkv, k_down, k_up, k_out, k_qkv,
     r_down, r_up, r_out, r_qkv, t_down, t_up, t_out, t_qkv, z_down, z_up, z_out, z_qkv,
     local, hop_send, hop_recv, pair_send, pair_recv, halo_send, halo_recv, small_send, small_recv,
@@ -888,7 +936,7 @@
     firsts, offsets, ends = window_plan(rows, parts)
     offset = pl.multiple_of(pick(offsets, z), 16)
     partner = (d ^ 1, z)
-    peers = [(d, z ^ k) for k in (1, 2, 3)] + [partner, (d ^ 2, z), (d ^ 4, z)]
+    peers = [(d, z ^ k) for k in (1, 2, 3)] + [partner, (d ^ 2, z), (d ^ 4, z), (d ^ 6, z)]
     barrier = pltpu.get_barrier_semaphore()
     for peer in peers:
         pl.semaphore_signal(barrier, inc=1, device_id=peer, device_id_type=MESH)
@@ -911,7 +959,7 @@
     load_wu = lambda i: fetch(1, f_up.at[chunk(RING[i])], wu)
     load_act = lambda i: fetch(2, act2.at[:, hidden(RING[i])], act)
     load_slope = lambda i: fetch(3, dgelu.at[:, hidden(RING[i])], slope)
-    at_wd, at_slope, at_act, at_wu = load_wd(0), load_slope(0), load_act(0), load_wu(0)
+    at_act, at_wd, at_slope, at_wu = load_act(0), load_wd(0), load_slope(0), load_wu(0)
     at_acc = fetch(4, second_grads, acc)
     at_normed = fetch(5, normed_one, normed)
     at_turned = fetch(6, first_t, turned)
@@ -939,7 +987,7 @@
         "out": (s_out, k_out, r_out, t_out, z_out, g_out, 2),
         "qkv": (s_qkv, k_qkv, r_qkv, t_qkv, z_qkv, g_qkv, 3),
     }
-    hops = {}
+    hops, finished = {}, {}
 
     def x_ahead(g, i):
         return (i + groups[g][6]) % 2 == 0
@@ -994,9 +1042,17 @@
             if k:
                 hop(g, i, 2, kept.at[i, 1], zb.at[k - 1], (d, z ^ k))
                 clock.send("z", block, fourth, 1.0 if k == 1 else 2.0)
+            else:
+                ended()
 
         def fourth():
             hops[g, i, 2].wait_recv()
+            ended()
+
+        def ended():
+            finished[g] = finished.get(g, 0) + 1
+            if finished[g] == parts:
+                finish(g)
 
         clock.send(l1, 2 * block, second)
 
@@ -1116,8 +1172,8 @@
     at_normed.wait()
     zero_row = jnp.zeros((16, D), f32)
 
-    def norm_body(i, sums):
-        at = pl.ds(pl.multiple_of(i * 16, 16), 16)
+    def norm_body(begin, count, sums):
+        at = pl.ds(begin, count)
         grads, unit = acc[at, :], normed[at, :]
         scaled = grads * gain[0:1, :]
         result = inverse[at, :] * (
@@ -1126,10 +1182,10 @@
             - unit * jnp.mean(scaled * unit, axis=-1, keepdims=True)
         )
         acc[at, :] = result
-        mixed_win[pl.ds(pl.multiple_of(offset + i * 16, 16), 16), :] = result.astype(low)
-        return (sums[0] + grads * unit, sums[1] + grads, sums[2] + result)
-
-    sums = lax.fori_loop(0, rows // 16, norm_body, (zero_row, zero_row, zero_row))
+        mixed_win[pl.ds(pl.multiple_of(offset + begin, 16), count), :] = result.astype(low)
+        return (sums[0] + fold(grads * unit), sums[1] + fold(grads), sums[2] + fold(result))
+
+    sums = by_rows(rows, norm_body, (zero_row, zero_row, zero_row))
     small[4:5, :] = jnp.sum(sums[0], axis=0, keepdims=True)
     small[5:6, :] = jnp.sum(sums[1], axis=0, keepdims=True)
     small[2:3, :] = jnp.sum(sums[2], axis=0, keepdims=True)
@@ -1158,8 +1214,8 @@
             grad_down_chunk(i + 2)
     own_at = pl.ds(offset, rows)
     for j, owner in enumerate(block_owners(d, 1 - core, True)):
-        stage[:, j * 128 : (j + 1) * 128] = mixed_win[own_at, pl.ds(pl.multiple_of(owner * 128, 128), 128)]
-    exchanges.append(exchange(parts, stage, mixed2.at[pl.ds(rows, rows), :]))
+        y[0:rows, j * 128 : (j + 1) * 128] = mixed_win[own_at, pl.ds(pl.multiple_of(owner * 128, 128), 128)]
+    exchanges.append(exchange(parts, y.at[pl.ds(0, rows), pl.ds(0, 512)], mixed2.at[pl.ds(rows, rows), :]))
     for j, owner in enumerate(block_owners(d, core, True)):
         mixed2[pl.ds(0, rows), j * 128 : (j + 1) * 128] = mixed_win[
             own_at, pl.ds(pl.multiple_of(owner * 128, 128), 128)
@@ -1216,7 +1272,6 @@
         if i == 0:
             take_halo()
         at_wo.wait()
-        at_x.wait()
 
         def flow_body(n, c):
             at = pl.ds(pl.multiple_of(n * 512, 512), 512)
@@ -1226,7 +1281,12 @@
             return c
 
         lax.fori_loop(0, window // 512, flow_body, 0)
-        clock.work(1.2)
+        clock.work(1.5)
+        if i:
+            grad_qkv_chunk(i - 1)
+        at_x.wait()
+        if i == 0:
+            exchanges[parts].wait_send()
         if i + 1 < parts:
             at_wo, at_att = load_wo(i + 1), load_att(i + 1)
 
@@ -1240,30 +1300,32 @@
             values = jnp.concatenate([x[at, lanes(2 * cut)] for at in unit_at], axis=0)
             marks = jnp.concatenate([kf[at, :] for at in unit_at], axis=0)
             wide_keys = jnp.concatenate([keys, marks], axis=1)
-            k_sum = jnp.zeros((LONG * UNIT, 2 * HD), f32)
-            v_sum = jnp.zeros((LONG * UNIT, 2 * HD), f32)
+            pair = jnp.concatenate([two_heads(x[at, lanes(0)]) for at in unit_at], axis=0)
+            grads = jnp.concatenate([two_heads(x[at, lanes(three)]) for at in unit_at], axis=0)
+            mark = jnp.concatenate([qf[at, :] for at in unit_at for _ in range(2)], axis=0)
+            wide_pair = jnp.concatenate([pair, mark], axis=1)
+            logsum = jnp.concatenate(
+                [lse[chunk(RING[i]), pl.ds(step * LONG + m, 1), :] for m in range(LONG)], axis=1
+            )
+            scores = lax.dot_general(wide_keys, wide_pair, NT, preferred_element_type=f32)
+            chances = jnp.exp(scores - logsum)
+            flow = lax.dot_general(values, grads, NT, preferred_element_type=f32)
+            terms = chances * flow
+            slopes = (chances * (flow - jnp.sum(terms, axis=0, keepdims=True))).astype(low)
+            v_sum = jnp.dot(chances.astype(low), grads, preferred_element_type=f32)
+            k_sum = jnp.dot(slopes, pair, preferred_element_type=f32)
+            flipped = lax.dot_general(keys, slopes, TN, preferred_element_type=f32)
             for m in range(LONG):
-                pair = two_heads(x[unit_at[m], lanes(0)])
-                grads = two_heads(x[unit_at[m], lanes(three)])
-                mark = qf[unit_at[m], :]
-                wide_pair = jnp.concatenate([pair, jnp.concatenate([mark, mark], axis=0)], axis=1)
-                scores = lax.dot_general(wide_keys, wide_pair, NT, preferred_element_type=f32)
-                chances = jnp.exp(scores - lse[chunk(RING[i]), pl.ds(step * LONG + m, 1), :])
-                flow = lax.dot_general(values, grads, NT, preferred_element_type=f32)
-                inner = jnp.sum(chances * flow, axis=0, keepdims=True)
-                slopes = (chances * (flow - inner)).astype(low)
-                v_sum = v_sum + jnp.dot(chances.astype(low), grads, preferred_element_type=f32)
-                k_sum = k_sum + jnp.dot(slopes, pair, preferred_element_type=f32)
-                flipped = lax.dot_general(keys, slopes, TN, preferred_element_type=f32)
+                two = slice(m * 2 * UNIT, (m + 1) * 2 * UNIT)
                 at = pl.ds(pl.multiple_of(slot * LONG * UNIT + m * UNIT, UNIT), UNIT)
-                y[at, lanes(0)] = (from_two(flipped) * scale).astype(low)
+                y[at, lanes(0)] = (from_two(flipped[:, two]) * scale).astype(low)
             at = pl.ds(pl.multiple_of(slot * LONG * UNIT, UNIT), LONG * UNIT)
             y[at, lanes(cut)] = k_sum.astype(low)
             y[at, lanes(2 * cut)] = v_sum.astype(low)
             return c
 
-        lax.fori_loop(0, pairs * 3, attend_body, 0)
-        clock.work(9.0)
+        lax.fori_loop(0, pairs * 3, attend_body, 0, unroll=2)
+        clock.work(10.5)
         if i + 1 < parts:
             at_x = load_x(i + 1)
         for u in range(FIRST_OWN, LAST_OWN + 1):
@@ -1294,46 +1356,50 @@
         clock.work(2.0)
         if i + 1 < parts:
             at_wi = load_wi(i + 1)
-        grad_qkv_chunk(i)
-
-    def last_body(i, total):
-        at = pl.ds(pl.multiple_of(i * 16, 16), 16)
+
+    def last_body(begin, count, total):
+        at = pl.ds(begin, count)
         value = acc[at, :]
         arena[at, :] = value.astype(low)
-        return total + value
-
-    total = jnp.sum(lax.fori_loop(0, rows // 16, last_body, zero_row), axis=0, keepdims=True)
+        return total + fold(value)
+
+    total = jnp.sum(by_rows(rows, last_body, zero_row), axis=0, keepdims=True)
     store = fetch(4, arena.at[pl.ds(0, rows), :], input_grad)
     small[0:1, :] = total * small_in[15:16, :]
     small[1:2, :] = total
     clock.work(2.0)
-    small_copies = []
-
-    def small_step(n):
-        copy = pltpu.make_async_remote_copy(
-            small, small_in_far.at[n], small_send.at[n], small_recv.at[n],
-            device_id=[partner, (d ^ 2, z), (d ^ 4, z), (d, z ^ 1), (d, z ^ 2)][n], device_id_type=MESH,
-        )
-        copy.start()
+    stages = [[partner], [(d ^ 2, z), (d ^ 4, z), (d ^ 6, z)], [(d, z ^ k) for k in (1, 2, 3)]]
+
+    def small_stage(n, first_slot):
+        sent = []
+        for slot, device in enumerate(stages[n], first_slot):
+            copy = pltpu.make_async_remote_copy(
+                small, small_in_far.at[slot], small_send.at[slot], small_recv.at[slot],
+                device_id=device, device_id_type=MESH,
+            )
+            copy.start()
+            sent.append(copy)
 
         def take():
-            copy.wait()
-            small[...] += small_in_far[n]
-            if n < 4:
-                small_step(n + 1)
-
-        clock.send("c", 0.4e6, take)
-
-    small_step(0)
+            for copy in sent:
+                copy.wait()
+            for slot in range(first_slot, first_slot + len(sent)):
+                small[...] += small_in_far[slot]
+            if n + 1 < len(stages):
+                small_stage(n + 1, first_slot + len(sent))
+
+        clock.send("c", 0.6e6, take)
+
+    small_stage(0, 0)
+    grad_qkv_chunk(parts - 1)
     clock.drain()
-    for g in groups:
-        finish(g)
+    assert sum(finished.values()) == 4 * parts
     small_out[...] = small[...]
     store.wait()
     for (g, i, kind), copy in hops.items():
         if kind or i >= 2:
             copy.wait_send()
-    for copy in exchanges[parts:]:
+    for copy in exchanges[parts + 1 :]:
         copy.wait_send()
     for sender, receiver, copy in halos:
         @pl.when(z == sender)
@@ -1374,10 +1440,9 @@
             pltpu.VMEM((parts, 2 * rows, D), low),
             pltpu.VMEM((D, 3 * cut), low),
             pltpu.VMEM((2 * rows, 512), low),
-            pltpu.VMEM((rows, 512), low),
             pltpu.VMEM((window, D), low),
             pltpu.VMEM((16, D), f32),
-            pltpu.VMEM((5, 16, D), f32),
+            pltpu.VMEM((7, 16, D), f32),
         ]
         + buffers
         + [
@@ -1388,11 +1453,11 @@
             dma((2 * parts + 1,)),
             dma((2,)),
             dma((2,)),
-            dma((5,)),
-            dma((5,)),
+            dma((7,)),
+            dma((7,)),
         ],
         compiler_params=pltpu.CompilerParams(
-            collective_id=1, has_side_effects=True, vmem_limit_bytes=60 * 2**20
+            collective_id=1, has_side_effects=True, vmem_limit_bytes=60 * 2**20 + 2**19
         ),
     )(perm, back, *vmem_in, *hbm_in)
 

time: 399 us -> 362 us (0.907)
  Pallas kernels: 377 us -> 340 us
    pallas_call x1, Pallas kernels: 192 us -> 170 us  [fore_call(): pl.pallas_call(functools.partial(fore_kernel, rows, window, parts), out_s...]
    pallas_call x1, Pallas kernels: 185 us -> 171 us  [back_call(): pl.pallas_call(functools.partial(back_kernel, rows, window, parts), out_s...]
where the time goes in v4:
time: 362 us; the launch traced here: 359 us
  Pallas kernels  340 us (94%)
  local copies, waits for them, and re-layouts  12.6 us (3%)
  other arithmetic  4.43 us (1%)
    pallas_call x1, Pallas kernels, back_call(): pl.pallas_call(functools.partial(back_kernel, rows, window, parts), out_s...  171 us
    pallas_call x1, Pallas kernels, fore_call(): pl.pallas_call(functools.partial(fore_kernel, rows, window, parts), out_s...  170 us

profile of v4, /device:TPU:0, one launch (start us, length us, event | category | flops | bytes accessed | tf_op | source)
XLA Modules:
  0.0 359.0 jit_solution(11086992647033434230)
XLA Ops:
  0.7 0.7 copy.28
  1.5 0.1 reduce
  1.6 0.1 convert_reduce_fusion
  1.7 0.1 slice.24
  1.8 0.2 convert_reduce_fusion.2
  2.0 0.2 convert_reduce_fusion.1.back
  2.2 0.0 copy-start.9
  2.2 0.6 select_reduce_fusion.perm
  2.8 1.7 copy.29
  4.5 0.0 copy-done.9
  4.5 0.0 copy-start.7
  4.5 0.0 copy-start.8
  4.6 0.0 copy-start.5
  4.6 1.6 copy.30.w_qkv
  6.2 0.0 copy-done.7
  6.2 0.0 copy-done.8
  6.2 0.1 pad.5.clone
  6.3 0.7 maximum_maximum_fusion.1.biases
  7.6 0.0 copy-done.5
  7.7 0.6 fusion.1
  8.3 0.1 pad.2.clone
  8.3 0.7 maximum_maximum_fusion.vectors
  9.0 1.1 select_convert_fusion
  10.2 169.6 %shard_map.178 = (bf16[4,1024,768]{2,1,0:T(8,128)(2,1)}, bf16[4,256,1024]{2,1,0:T(8,128)(2,1)}, bf16[4,1024,1024]{2,1,0:T(8,128)(2,1)}, bf16[4,1024,1024]{2,1,0:...) custom-call(s32[12]{0:T(128)} %select_reduce_fusion.perm, ...), custom_call_target="tpu_custom_call" | custom-call | tf_op jit(solution)/shard_map/pallas_call | solution.py:858
  179.8 170.6 %shard_map.179 = (bf16[592,1024]{1,0:T(8,128)(2,1)}, f32[128,768]{1,0:T(8,128)}, f32[256,128]{1,0:T(8,128)}, f32[128,1024]{1,0:T(8,128)}, f32[1024,128]{1,0:T(8,128)}, /*index=5*/f32[16,1024]{1,0:T(8,128)}) custom-call(s32[12]{0:T(128)} %select_reduce_fusion.perm, s32[12]{0:T(128)} %copy-done.9, bf16[592,1024]{1,0:T(8,128)(2,1)} %get-tuple-element.34.sec_low, ...), custom_call_target="tpu_custom_call" | custom-call | tf_op jit(solution)/shard_map/pallas_call | solution.py:1427
  350.5 0.0 copy-start.6
  350.5 0.0 copy-start
  350.5 1.3 copy.31
  351.7 0.0 copy-start.1
  351.7 0.9 copy.32
  352.7 0.0 copy-done.6
  352.7 0.6 constant_dynamic-slice_fusion
  353.3 0.6 dynamic_slice.7
  353.9 0.6 slice.31
  354.5 0.0 copy-done
  354.5 1.0 copy.42
  355.5 0.0 copy-done.1
  355.5 0.0 copy-start.4
  355.5 0.0 copy-start.3
  355.5 0.0 copy-start.2
  355.5 1.0 copy.43
  356.5 0.0 copy-done.4
  356.5 0.7 copy.44
  357.2 0.0 copy-done.3
  357.2 0.8 copy.45
  358.0 0.0 copy-done.2
  358.0 0.8 copy.46
  (13 shorter events, 0.1 us)
Async XLA Ops:
  2.2 2.4 copy-start.9
  4.5 1.6 copy-start.7
  4.5 1.6 copy-start.8
  4.6 3.1 copy-start.5
  350.5 2.2 copy-start.6
  350.5 4.0 %copy-start = (bf16[592,1024]{1,0:T(8,128)(2,1)S(1)}, bf16[592,1024]{1,0:T(8,128)(2,1)}, u32[]{:S(2)}) copy-start(bf16[592,1024]{1,0:T(8,128)(2,1)} %get-tuple-element.101) | copy-start | bytes 3637252
  351.7 3.8 %copy-start.1 = (bf16[592,1024]{1,0:T(8,128)(2,1)S(1)}, bf16[592,1024]{1,0:T(8,128)(2,1)}, u32[]{:S(2)}) copy-start(bf16[592,1024]{1,0:T(8,128)(2,1)} %get-tuple-element.102) | copy-start | bytes 3637252
  355.5 1.0 copy-start.4
  355.5 1.7 copy-start.3
  355.5 2.5 copy-start.2

commit v5 on v4

--- a/solution.py
+++ b/solution.py
@@ -343,16 +343,16 @@
 
 
 class Clock:
-    def __init__(self):
+    def __init__(self, rate):
+        self.rate = {"c": 400e3, "x": rate, "y": rate, "z": rate}
         self.now = 0.0
         self.free = {}
         self.queue = []
         self.count = 0
 
     def send(self, link, size, action, share=1.0):
-        rate = {"c": 400e3, "x": 44e3, "y": 44e3, "z": 44e3}[link]
         begin = max(self.now, self.free.get(link, 0.0))
-        end = begin + share * size / rate
+        end = begin + share * size / self.rate[link]
         self.free[link] = end
         self.count += 1
         heapq.heappush(self.queue, (end + 1.5, self.count, action))
@@ -380,7 +380,7 @@
 
 
 RING = (2, 3, 1, 0)
-HALO_TIME = 34.0
+HALO_TIME = 25.0
 
 
 def fore_kernel(
@@ -408,7 +408,7 @@
     for peer in peers:
         pl.semaphore_signal(barrier, inc=1, device_id=peer, device_id_type=MESH)
     pl.semaphore_wait(barrier, len(peers))
-    clock = Clock()
+    clock = Clock(44e3)
 
     order = [sorted((o for o in range(parts) if o != j), key=lambda o: (abs(o - j), o)) for j in range(parts)]
     source = [pick([order[j][n] for j in range(parts)], z) for n in range(parts - 1)]
@@ -476,8 +476,8 @@
             there = here + 1 if owner < here else here - 1
             if 0 <= there < parts:
                 along(owner, part(fulls[g], owner, d, sizes[g]), here, there, send.at[i, 0], g)
-        if n == 0 and g < 2:
-            send_own(g + 2)
+        if g == 2 and n == 0:
+            send_own(3)
         pass_on(i, 1, d, (d ^ 2, z))
         pass_on(i, 2, d, (d ^ 4, z))
         pass_on(i, 5, d, partner)
@@ -515,9 +515,6 @@
             clock.step()
         for kind in range(5, 10):
             copies[i, kind].wait_recv()
-
-    send_own(0)
-    send_own(1)
 
     halos = []
     for j in range(parts - 1):
@@ -536,6 +533,8 @@
         def _(copy=copy):
             copy.start()
     clock.send("z", max(offsets) * D * 2, lambda: None)
+    send_own(0)
+    send_own(1)
     bias_copies = []
     for k in (1, 2, 3):
         copy = pltpu.make_async_remote_copy(
@@ -615,6 +614,7 @@
         @pl.when(z == receiver)
         def _(copy=copy):
             copy.wait_recv()
+    send_own(2)
     for j in range(parts):
         @pl.when(z == j)
         def _(j=j):
@@ -637,9 +637,6 @@
         if k == 0:
             wq_ref, wo_ref = w_qkv, w_out
         else:
-            arrive(index_of[0, k - 1])
-            arrive(index_of[1, k - 1])
-            load_q, load_o = fetch(1, f_qkv.at[at_z], wq), fetch(2, f_out.at[at_z], wo)
             wq_ref, wo_ref = wq, wo
             load_q.wait()
         slot_i = i % 2
@@ -660,7 +657,10 @@
 
         lax.fori_loop(0, window // 512, project, 0)
         stores[i] = fetch(3 + slot_i, xq.at[slot_i], qkv.at[at_z])
-        clock.work(4.0)
+        clock.work(3.5)
+        if i + 1 < parts:
+            arrive(index_of[0, i])
+            load_q = fetch(1, f_qkv.at[source[i]], wq)
 
         def attend(step, c):
             p, slot = step // 3, lax.rem(step, 3)
@@ -707,7 +707,10 @@
             return c
 
         lax.fori_loop(0, D // 256, out_body, 0)
-        clock.work(1.0)
+        clock.work(1.5)
+        if i + 1 < parts:
+            arrive(index_of[1, i])
+            load_o = fetch(2, f_out.at[source[i]], wo)
 
     def norm_one(begin, count, c):
         at = pl.ds(begin, count)
@@ -736,10 +739,6 @@
         if k == 0:
             up_ref, down_ref = w_up, w_down
         else:
-            arrive(index_of[2, k - 1])
-            load_u = fetch(1, f_up.at[at_z], wu)
-            arrive(index_of[3, k - 1])
-            load_d = fetch(2, f_down.at[at_z], wd)
             up_ref, down_ref = wu, wd
             load_u.wait()
         if i >= 2:
@@ -765,6 +764,9 @@
             fetch(10 + slot_i, slope.at[slot_i], slopes.at[:, hidden]),
         )
         clock.work(4.0)
+        if i + 1 < parts:
+            arrive(index_of[2, i])
+            load_u = fetch(1, f_up.at[source[i]], wu)
         if k:
             load_d.wait()
 
@@ -779,6 +781,9 @@
 
         lax.fori_loop(0, D // 256, down_body, 0)
         clock.work(2.0)
+        if i + 1 < parts:
+            arrive(index_of[3, i])
+            load_d = fetch(2, f_down.at[source[i]], wd)
         if i == 0:
             first_copy.wait_recv()
             turned_out.wait()
@@ -941,7 +946,7 @@
     for peer in peers:
         pl.semaphore_signal(barrier, inc=1, device_id=peer, device_id_type=MESH)
     pl.semaphore_wait(barrier, len(peers))
-    clock = Clock()
+    clock = Clock(48e3)
     tail = []
 
     wide = 2 * rows

time: 362 us -> 337 us (0.931)
  Pallas kernels: 340 us -> 315 us
    pallas_call x1, Pallas kernels: 170 us -> 153 us  [fore_call(): pl.pallas_call(functools.partial(fore_kernel, rows, window, parts), out_s...]
    pallas_call x1, Pallas kernels: 171 us -> 162 us  [back_call(): pl.pallas_call(functools.partial(back_kernel, rows, window, parts), out_s...]
where the time goes in v5:
time: 337 us; the launch traced here: 333 us
  Pallas kernels  315 us (93%)
  local copies, waits for them, and re-layouts  12.6 us (4%)
  other arithmetic  4.43 us (1%)
    pallas_call x1, Pallas kernels, back_call(): pl.pallas_call(functools.partial(back_kernel, rows, window, parts), out_s...  162 us
    pallas_call x1, Pallas kernels, fore_call(): pl.pallas_call(functools.partial(fore_kernel, rows, window, parts), out_s...  153 us
    unnamed x29, local copies, waits for them, and re-layouts  6.98 us

profile of v5, /device:TPU:0, one launch (start us, length us, event | category | flops | bytes accessed | tf_op | source)
XLA Modules:
  0.0 333.5 jit_solution(9641093730833989943)
XLA Ops:
  0.7 0.7 copy.28
  1.5 0.1 reduce
  1.6 0.1 convert_reduce_fusion
  1.7 0.1 slice.24
  1.8 0.2 convert_reduce_fusion.2
  2.0 0.2 convert_reduce_fusion.1.back
  2.2 0.0 copy-start.9
  2.2 0.6 select_reduce_fusion.perm
  2.8 1.7 copy.29
  4.5 0.0 copy-done.9
  4.5 0.0 copy-start.7
  4.5 0.0 copy-start.8
  4.6 0.0 copy-start.5
  4.6 1.6 copy.30.w_qkv
  6.2 0.0 copy-done.7
  6.2 0.0 copy-done.8
  6.2 0.1 pad.5.clone
  6.3 0.7 maximum_maximum_fusion.1.biases
  7.6 0.0 copy-done.5
  7.7 0.6 fusion.1
  8.3 0.1 pad.2.clone
  8.3 0.7 maximum_maximum_fusion.vectors
  9.0 1.1 select_convert_fusion
  10.2 153.0 %shard_map.178 = (bf16[4,1024,768]{2,1,0:T(8,128)(2,1)}, bf16[4,256,1024]{2,1,0:T(8,128)(2,1)}, bf16[4,1024,1024]{2,1,0:T(8,128)(2,1)}, bf16[4,1024,1024]{2,1,0:...) custom-call(s32[12]{0:T(128)} %select_reduce_fusion.perm, ...), custom_call_target="tpu_custom_call" | custom-call | tf_op jit(solution)/shard_map/pallas_call | solution.py:863
  163.2 161.7 %shard_map.179 = (bf16[592,1024]{1,0:T(8,128)(2,1)}, f32[128,768]{1,0:T(8,128)}, f32[256,128]{1,0:T(8,128)}, f32[128,1024]{1,0:T(8,128)}, f32[1024,128]{1,0:T(8,128)}, /*index=5*/f32[16,1024]{1,0:T(8,128)}) custom-call(s32[12]{0:T(128)} %select_reduce_fusion.perm, s32[12]{0:T(128)} %copy-done.9, bf16[592,1024]{1,0:T(8,128)(2,1)} %get-tuple-element.34.sec_low, ...), custom_call_target="tpu_custom_call" | custom-call | tf_op jit(solution)/shard_map/pallas_call | solution.py:1432
  324.9 0.0 copy-start.6
  324.9 0.0 copy-start
  324.9 1.3 copy.31
  326.2 0.0 copy-start.1
  326.2 0.9 copy.32
  327.1 0.0 copy-done.6
  327.1 0.6 constant_dynamic-slice_fusion
  327.7 0.6 dynamic_slice.7
  328.3 0.6 slice.31
  328.9 0.0 copy-done
  328.9 1.0 copy.42
  330.0 0.0 copy-done.1
  330.0 0.0 copy-start.4
  330.0 0.0 copy-start.3
  330.0 0.0 copy-start.2
  330.0 1.0 copy.43
  331.0 0.0 copy-done.4
  331.0 0.7 copy.44
  331.7 0.0 copy-done.3
  331.7 0.8 copy.45
  332.4 0.0 copy-done.2
  332.5 0.8 copy.46
  (13 shorter events, 0.1 us)
Async XLA Ops:
  2.2 2.4 copy-start.9
  4.5 1.6 copy-start.7
  4.5 1.6 copy-start.8
  4.6 3.1 copy-start.5
  324.9 2.2 copy-start.6
  324.9 4.0 %copy-start = (bf16[592,1024]{1,0:T(8,128)(2,1)S(1)}, bf16[592,1024]{1,0:T(8,128)(2,1)}, u32[]{:S(2)}) copy-start(bf16[592,1024]{1,0:T(8,128)(2,1)} %get-tuple-element.101) | copy-start | bytes 3637252
  326.2 3.8 %copy-start.1 = (bf16[592,1024]{1,0:T(8,128)(2,1)S(1)}, bf16[592,1024]{1,0:T(8,128)(2,1)}, u32[]{:S(2)}) copy-start(bf16[592,1024]{1,0:T(8,128)(2,1)} %get-tuple-element.102) | copy-start | bytes 3637252
  330.0 1.0 copy-start.4
  330.0 1.7 copy-start.3
  330.0 2.5 copy-start.2
